TPU v7x, 32 devices: a whole 2x2x4 slice. The times are simulated.
32 devices in a mesh: elem: 8 (over z, x), band: 4 (over y, core).
Axes of the slice: x: 2, y: 2, z: 4, core: 2. Of those that a mesh axis runs over, the one named last changes fastest.
Arguments:
- basis_sizes: int32 [128], P('elem'), may hold values from 96 to 160, as said below
- coupling_pattern: int32 [128], P('elem'), may hold values 0 or 1
- h_diag: bfloat16 [128, 160, 160], P('elem'), may hold values from -0.6708204 to 0.6708204, as said below
- h_couple: bfloat16 [128, 160, 160], P('elem'), may hold values from -0.25 to 0.25
- bands: bfloat16 [1024, 20480], P('band', 'elem'), may hold values from -1500 to 1500
Outputs:
- filtered: bfloat16 [1024, 20480], P('band', 'elem')
Inputs may be any that keep to these rules, and one draw needn't show every extreme that they name: `basis_sizes`: every element has between 96 and 160 basis functions; some element has exactly 160 and some exactly 96. `h_diag`: each block is symmetric.
All inputs are finite; a program needn't handle non-finite values. No bound on the sum of `coupling_pattern` on one device may be relied on, other than what follows from the above.
Results may differ from a plain program's by a relative error of at most 0.0085.
Values may be sent and summed in bfloat16 or wider, within the bound.
No kernel may reach another device: no remote copies, remote signals or barrier semaphores. Data moves between devices by JAX's collectives and lax.ppermute only.
A program may use at most 64 MiB of HBM per device.

v0:
```python
import math

import jax
import jax.numpy as jnp
from jax import lax
from jax.sharding import PartitionSpec as P

DEGREE = 6


center_shift = 0.4
half_width = 2.8
epsilon_norm = 1e-06


def from_behind(value, axis, steps):
    count = lax.axis_size(axis)
    pairs = [(source, (source + steps) % count) for source in range(count)]
    return lax.ppermute(value, axis, pairs)


def identity_block(shape, offset):
    row_ids = lax.broadcasted_iota(jnp.int32, shape, 0) + offset
    col_ids = lax.broadcasted_iota(jnp.int32, shape, 1)
    return (row_ids == col_ids).astype(jnp.float32)


def rotation_columns(gram_strip, scales, offset, total_rows):
    own_scales = lax.dynamic_slice_in_dim(scales, offset, gram_strip.shape[0], 0)
    identity = identity_block(gram_strip.shape, offset)
    normed = own_scales[:, None] * gram_strip * scales[None, :]
    return (math.sqrt(total_rows) * scales[None, :] * (1.5 * identity - 0.5 * normed)).astype(
        jnp.bfloat16
    )


def shards(basis_sizes, coupling_pattern, h_diag, h_couple, bands):
    elem_local = h_diag.shape[0]
    basis_width = h_diag.shape[1]
    band_local = bands.shape[0]
    total_rows = elem_local * lax.axis_size("elem") * basis_width
    columns = lax.broadcasted_iota(jnp.int32, (elem_local, basis_width), 1)
    valid_rows = (columns < basis_sizes[:, None]).astype(jnp.float32)
    coupling = h_couple * coupling_pattern.astype(jnp.bfloat16)[:, None, None]
    current = (
        bands.reshape(band_local, elem_local, basis_width) * valid_rows.astype(jnp.bfloat16)[None]
    )
    previous = current
    for degree in range(DEGREE):
        current_float = current.astype(jnp.float32)
        local_term = jnp.einsum("eij,bej->bei", h_diag, current, preferred_element_type=jnp.float32)
        following = from_behind(current[:, 0], "elem", -1)
        ahead_rows = jnp.concatenate([current[:, 1:], following[:, None]], axis=1)
        upper_term = jnp.einsum(
            "eij,bej->bei", coupling, ahead_rows, preferred_element_type=jnp.float32
        )
        carried = jnp.einsum("eji,bej->bei", coupling, current, preferred_element_type=jnp.float32)
        arrived = from_behind(carried[:, -1], "elem", 1)
        lower_term = jnp.concatenate([arrived[:, None], carried[:, :-1]], axis=1)
        applied = (local_term + upper_term + lower_term) * valid_rows[None]
        shifted = applied - center_shift * current_float
        if degree == 0:
            next_iterate = shifted / half_width
        else:
            next_iterate = 2.0 * shifted / half_width - previous.astype(jnp.float32)
        previous, current = (current, next_iterate.astype(jnp.bfloat16))
    filtered = current.reshape(band_local, elem_local * basis_width)
    every_band = lax.all_gather(filtered, "band", axis=0, tiled=True)
    strip = lax.dot_general(
        filtered, every_band, (((1,), (1,)), ((), ())), preferred_element_type=jnp.float32
    )
    squares = jnp.sum(jnp.square(every_band.astype(jnp.float32)), axis=1)
    strip, squares = lax.psum((strip, squares), "elem")
    scales = lax.rsqrt(squares + epsilon_norm)
    offset = lax.axis_index("band") * band_local
    weights = rotation_columns(strip, scales, offset, total_rows)
    return jnp.dot(weights, every_band, preferred_element_type=jnp.float32).astype(jnp.bfloat16)


def solution(mesh):
    in_specs = (
        P("elem"),
        P("elem"),
        P("elem", None, None),
        P("elem", None, None),
        P("band", "elem"),
    )
    out_specs = P("band", "elem")
    return jax.shard_map(shards, mesh=mesh, in_specs=in_specs, out_specs=out_specs, check_vma=False)
```

profile of v0, /device:TPU:0, one launch (start us, length us, event | category | flops | bytes accessed | tf_op | source)
XLA Modules:
  0.0 215.4 jit_solution(1154020046193810225)
XLA Ops:
  6.5 1.7 copy.6
  10.5 3.0 %collective-permute-start.1 = (f32[256,160]{0,1:T(8,128)S(1)}, f32[256,160]{0,1:T(8,128)S(1)}, u32[]{:S(2)}, u32[]{:S(2)}) collective-permute-start(f32[256,160]{0,1:T(8,128)S(1)} %slice_bitcast_fusion.5), channel_id=1, source_target_pairs={{0,4},{4,8},{8,12},{12,16},{16,20},{20,24},{24,28},{28,0},{1,5},{5... | collective-permute-start | bytes 491528 | tf_op jit(solution)/shard_map/ppermute | solution.py:19
  13.5 3.1 %collective-permute-start = (bf16[256,160]{0,1:T(8,128)(2,1)S(1)}, bf16[256,160]{0,1:T(8,128)(2,1)S(1)}, u32[]{:S(2)}, u32[]{:S(2)}) collective-permute-start(bf16[256,160]{0,1:T(8,128)(2,1)S(1)} %slice_bitcast_fusion.11), channel_id=1, source_target_pairs={{0,28},{4,0},{8,4},{12,8},{16,12},{20,16},{24,20},{28,24},{1,29},{... | collective-permute-start | bytes 245768 | tf_op jit(solution)/shard_map/ppermute | solution.py:19
  17.2 4.2 %collective-permute-done = bf16[256,160]{0,1:T(8,128)(2,1)S(1)} collective-permute-done((bf16[256,160]{0,1:T(8,128)(2,1)S(1)}, bf16[256,160]{0,1:T(8,128)(2,1)S(1)}, u32[]{:S(2)}, u32[]{:S(2)}) %collective-permute-start) | collective-permute-done | bytes 81952 | tf_op jit(solution)/shard_map/ppermute | solution.py:19
  23.8 4.7 %collective-permute-start.2 = (bf16[256,160]{0,1:T(8,128)(2,1)S(1)}, bf16[256,160]{0,1:T(8,128)(2,1)S(1)}, u32[]{:S(2)}, u32[]{:S(2)}) collective-permute-start(bf16[256,160]{0,1:T(8,128)(2,1)S(1)} %slice_bitcast_fusion.10), channel_id=1, source_target_pairs={{0,28},{4,0},{8,4},{12,8},{16,12},{20,16},{24,20},{28,24},{1,29},{... | collective-permute-start | bytes 245768 | tf_op jit(solution)/shard_map/ppermute | solution.py:19
  29.1 1.4 collective-permute-done.2
  31.9 1.5 fusion.3
  34.4 4.7 %collective-permute-start.4 = (bf16[256,160]{0,1:T(8,128)(2,1)S(1)}, bf16[256,160]{0,1:T(8,128)(2,1)S(1)}, u32[]{:S(2)}, u32[]{:S(2)}) collective-permute-start(bf16[256,160]{0,1:T(8,128)(2,1)S(1)} %slice_bitcast_fusion.9), channel_id=1, source_target_pairs={{0,28},{4,0},{8,4},{12,8},{16,12},{20,16},{24,20},{28,24},{1,29},{... | collective-permute-start | bytes 245768 | tf_op jit(solution)/shard_map/ppermute | solution.py:19
  42.4 1.5 fusion.6
  45.0 4.5 %collective-permute-start.6 = (bf16[256,160]{0,1:T(8,128)(2,1)S(1)}, bf16[256,160]{0,1:T(8,128)(2,1)S(1)}, u32[]{:S(2)}, u32[]{:S(2)}) collective-permute-start(bf16[256,160]{0,1:T(8,128)(2,1)S(1)} %slice_bitcast_fusion.8), channel_id=1, source_target_pairs={{0,28},{4,0},{8,4},{12,8},{16,12},{20,16},{24,20},{28,24},{1,29},{... | collective-permute-start | bytes 245768 | tf_op jit(solution)/shard_map/ppermute | solution.py:19
  50.2 3.4 %collective-permute-done.6 = bf16[256,160]{0,1:T(8,128)(2,1)S(1)} collective-permute-done((bf16[256,160]{0,1:T(8,128)(2,1)S(1)}, bf16[256,160]{0,1:T(8,128)(2,1)S(1)}, u32[]{:S(2)}, u32[]{:S(2)}) %collective-permute-start.6) | collective-permute-done | bytes 81952 | tf_op jit(solution)/shard_map/ppermute | solution.py:19
  53.6 1.5 fusion.9
  56.3 4.5 %collective-permute-start.8 = (bf16[256,160]{0,1:T(8,128)(2,1)S(1)}, bf16[256,160]{0,1:T(8,128)(2,1)S(1)}, u32[]{:S(2)}, u32[]{:S(2)}) collective-permute-start(bf16[256,160]{0,1:T(8,128)(2,1)S(1)} %slice_bitcast_fusion.7), channel_id=1, source_target_pairs={{0,28},{4,0},{8,4},{12,8},{16,12},{20,16},{24,20},{28,24},{1,29},{... | collective-permute-start | bytes 245768 | tf_op jit(solution)/shard_map/ppermute | solution.py:19
  61.5 1.4 collective-permute-done.8
  62.9 2.0 collective-permute-done.9
  64.9 1.5 fusion.12
  67.4 4.7 %collective-permute-start.10 = (bf16[256,160]{0,1:T(8,128)(2,1)S(1)}, bf16[256,160]{0,1:T(8,128)(2,1)S(1)}, u32[]{:S(2)}, u32[]{:S(2)}) collective-permute-start(bf16[256,160]{0,1:T(8,128)(2,1)S(1)} %slice_bitcast_fusion.6), channel_id=1, source_target_pairs={{0,28},{4,0},{8,4},{12,8},{16,12},{20,16},{24,20},{28,24},{1,29},{... | collective-permute-start | bytes 245768 | tf_op jit(solution)/shard_map/ppermute | solution.py:19
  75.4 2.3 %fusion.15 = bf16[256,16,160]{0,2,1:T(8,128)(2,1)} fusion(bf16[256,16,160]{0,2,1:T(8,128)(2,1)S(1)} %fusion.9, f32[256,15,160]{0,2,1:T(8,128)S(1)} %slice-done.5, f32[256,1,160]{0,2,1:T(8,128)S(1)} %bitcast.86, bf16[256,16,160]{0,2,1:T(8,128)(2,1)S(1)} %fusion.12, f32[16,256,160]{1,2,0:T(8,128)S(1)} %fusion.81, bf16[256,1,160]{0,2,1:T(8,128)(2,1)S(1)} %bitcast.92, ...), kind=kOutput, calls=%fused_computation.27 | convolution fusion | flops 221184000 | bytes 11315232 | tf_op jit(solution)/shard_map/eij,bej->bei/dot_general | solution.py:54
  77.8 41.7 %all-gather.2.cloned.1.call-done = bf16[1024,2560]{0,1:T(8,128)(2,1)} async-done(((bf16[256,2560]{0,1:T(8,128)(2,1)}), bf16[1024,2560]{0,1:T(8,128)(2,1)}) %all-gather.2.cloned.1.call-update) | async-done | bytes 5242896 | tf_op jit(solution)/shard_map/all_gather | solution.py:68
  119.5 5.0 %fusion.75 = f32[256,1024]{1,0:T(8,128)} fusion(bf16[256,2560]{0,1:T(8,128)(2,1)S(1)} %bitcast.84, bf16[1024,2560]{0,1:T(8,128)(2,1)} %all-gather.2.cloned.1.call-done), kind=kOutput, calls=%fused_computation.109 | convolution fusion | flops 1342177280 | bytes 7602176 | tf_op jit(solution)/shard_map/dot_general | solution.py:69
  124.6 3.6 %multiply_reduce_fusion = f32[1024]{0:T(1024)S(1)} fusion(bf16[1024,2560]{0,1:T(8,128)(2,1)} %all-gather.2.cloned.1.call-done), kind=kLoop, calls=%fused_computation | loop fusion | flops 7863296 | bytes 5246976 | tf_op jit(solution)/shard_map/reduce_sum | solution.py:72
  128.2 21.6 %psum.14 = f32[1024]{0:T(1024)S(1)} all-reduce(f32[1024]{0:T(1024)S(1)} %multiply_reduce_fusion), channel_id=1, replica_groups=mesh['elem'=8,'band'=4] {'elem'}, use_global_device_ids=true, to_apply=%region_1.0 | all-reduce | flops 1024 | bytes 8192 | tf_op jit(solution)/shard_map/psum | solution.py:73
  149.8 53.1 %all-reduce.2.cloned.1.call-done = f32[256,1024]{1,0:T(8,128)} async-done(((f32[256,1024]{1,0:T(8,128)}), f32[256,1024]{1,0:T(8,128)}) %all-reduce.2.cloned.1.call-update) | async-done | bytes 1048592 | tf_op jit(solution)/shard_map/psum | solution.py:73
  203.0 5.6 %convolution_convert_fusion = bf16[256,2560]{1,0:T(8,128)(2,1)} fusion(bf16[1024,2560]{0,1:T(8,128)(2,1)} %all-gather.2.cloned.1.call-done, f32[256,1024]{1,0:T(8,128)} %all-reduce.2.cloned.1.call-done, f32[1024]{0:T(1024)S(1)} %get-tuple-element.6, f32[256]{0:T(256)S(1)} %dynamic_slice.3, s32[256]{0:T(256)S(1)} %iota_add_fusion, f32[1024]{0:T(1024)S(1)} %get-tuple-element.5), kind=kOutput, calls=%fused_computation.1 | convolution fusion | flops 1344929792 | bytes 7612416 | tf_op jit(solution)/shard_map/dot_general | solution.py:77
  (87 shorter events, 18.9 us)
Async XLA Ops:
  6.5 10.1 %copy-start = (bf16[16,160,160]{2,1,0:T(8,128)(2,1)S(1)}, bf16[16,160,160]{2,1,0:T(8,128)(2,1)}, u32[]{:S(2)}) copy-start(bf16[16,160,160]{2,1,0:T(8,128)(2,1)} %param.7) | copy-start | bytes 2457604
  6.5 113.0 %all-gather.2.cloned.1.call-start = ((), (), s32[]{:S(2)}) async-start(), calls=%async_computation | async-start | bytes 6553600 | tf_op jit(solution)/shard_map/all_gather | solution.py:68
  10.5 6.7 %copy-start.3 = (f32[256,16,160]{0,2,1:T(8,128)}, f32[256,16,160]{0,2,1:T(8,128)S(1)}, u32[]{:S(2)}) copy-start(f32[256,16,160]{0,2,1:T(8,128)S(1)} %convolution_bitcast_fusion.5) | copy-start | bytes 7864324
  10.5 10.9 %collective-permute-start.1 = (f32[256,160]{0,1:T(8,128)S(1)}, f32[256,160]{0,1:T(8,128)S(1)}, u32[]{:S(2)}, u32[]{:S(2)}) collective-permute-start(f32[256,160]{0,1:T(8,128)S(1)} %slice_bitcast_fusion.5), channel_id=1, source_target_pairs={{0,4},{4,8},{8,12},{12,16},{16,20},{20,24},{24,28},{28,0},{1,5},{5... | collective-permute-start | bytes 491528 | tf_op jit(solution)/shard_map/ppermute | solution.py:19
  13.5 8.0 %collective-permute-start = (bf16[256,160]{0,1:T(8,128)(2,1)S(1)}, bf16[256,160]{0,1:T(8,128)(2,1)S(1)}, u32[]{:S(2)}, u32[]{:S(2)}) collective-permute-start(bf16[256,160]{0,1:T(8,128)(2,1)S(1)} %slice_bitcast_fusion.11), channel_id=1, source_target_pairs={{0,28},{4,0},{8,4},{12,8},{16,12},{20,16},{24,20},{28,24},{1,29},{... | collective-permute-start | bytes 245768 | tf_op jit(solution)/shard_map/ppermute | solution.py:19
  17.1 4.3 %slice-start = ((f32[256,16,160]{0,2,1:T(8,128)}), f32[256,15,160]{0,2,1:T(8,128)S(1)}, s32[]{:S(2)}) async-start(f32[256,16,160]{0,2,1:T(8,128)} %copy-done.3), calls=%async_computation.2 | async-start | bytes 4915200 | tf_op jit(solution)/shard_map/slice | solution.py:59
  23.7 5.3 %copy-start.4 = (f32[256,16,160]{0,2,1:T(8,128)}, f32[256,16,160]{0,2,1:T(8,128)S(1)}, u32[]{:S(2)}) copy-start(f32[256,16,160]{0,2,1:T(8,128)S(1)} %convolution_bitcast_fusion.4) | copy-start | bytes 7864324
  23.7 8.2 %collective-permute-start.3 = (f32[256,160]{0,1:T(8,128)S(1)}, f32[256,160]{0,1:T(8,128)S(1)}, u32[]{:S(2)}, u32[]{:S(2)}) collective-permute-start(f32[256,160]{0,1:T(8,128)S(1)} %slice_bitcast_fusion.4), channel_id=1, source_target_pairs={{0,4},{4,8},{8,12},{12,16},{16,20},{20,24},{24,28},{28,0},{1,5},{5... | collective-permute-start | bytes 491528 | tf_op jit(solution)/shard_map/ppermute | solution.py:19
  23.8 6.8 %collective-permute-start.2 = (bf16[256,160]{0,1:T(8,128)(2,1)S(1)}, bf16[256,160]{0,1:T(8,128)(2,1)S(1)}, u32[]{:S(2)}, u32[]{:S(2)}) collective-permute-start(bf16[256,160]{0,1:T(8,128)(2,1)S(1)} %slice_bitcast_fusion.10), channel_id=1, source_target_pairs={{0,28},{4,0},{8,4},{12,8},{16,12},{20,16},{24,20},{28,24},{1,29},{... | collective-permute-start | bytes 245768 | tf_op jit(solution)/shard_map/ppermute | solution.py:19
  34.3 5.3 %copy-start.5 = (f32[256,16,160]{0,2,1:T(8,128)}, f32[256,16,160]{0,2,1:T(8,128)S(1)}, u32[]{:S(2)}) copy-start(f32[256,16,160]{0,2,1:T(8,128)S(1)} %convolution_bitcast_fusion.3) | copy-start | bytes 7864324
  34.3 8.1 %collective-permute-start.5 = (f32[256,160]{0,1:T(8,128)S(1)}, f32[256,160]{0,1:T(8,128)S(1)}, u32[]{:S(2)}, u32[]{:S(2)}) collective-permute-start(f32[256,160]{0,1:T(8,128)S(1)} %slice_bitcast_fusion.3), channel_id=1, source_target_pairs={{0,4},{4,8},{8,12},{12,16},{16,20},{20,24},{24,28},{28,0},{1,5},{5... | collective-permute-start | bytes 491528 | tf_op jit(solution)/shard_map/ppermute | solution.py:19
  34.4 6.8 %collective-permute-start.4 = (bf16[256,160]{0,1:T(8,128)(2,1)S(1)}, bf16[256,160]{0,1:T(8,128)(2,1)S(1)}, u32[]{:S(2)}, u32[]{:S(2)}) collective-permute-start(bf16[256,160]{0,1:T(8,128)(2,1)S(1)} %slice_bitcast_fusion.9), channel_id=1, source_target_pairs={{0,28},{4,0},{8,4},{12,8},{16,12},{20,16},{24,20},{28,24},{1,29},{... | collective-permute-start | bytes 245768 | tf_op jit(solution)/shard_map/ppermute | solution.py:19
  44.8 5.3 %copy-start.6 = (f32[256,16,160]{0,2,1:T(8,128)}, f32[256,16,160]{0,2,1:T(8,128)S(1)}, u32[]{:S(2)}) copy-start(f32[256,16,160]{0,2,1:T(8,128)S(1)} %convolution_bitcast_fusion.2) | copy-start | bytes 7864324
  44.8 8.8 %collective-permute-start.7 = (f32[256,160]{0,1:T(8,128)S(1)}, f32[256,160]{0,1:T(8,128)S(1)}, u32[]{:S(2)}, u32[]{:S(2)}) collective-permute-start(f32[256,160]{0,1:T(8,128)S(1)} %slice_bitcast_fusion.2), channel_id=1, source_target_pairs={{0,4},{4,8},{8,12},{12,16},{16,20},{20,24},{24,28},{28,0},{1,5},{5... | collective-permute-start | bytes 491528 | tf_op jit(solution)/shard_map/ppermute | solution.py:19
  45.0 8.6 %collective-permute-start.6 = (bf16[256,160]{0,1:T(8,128)(2,1)S(1)}, bf16[256,160]{0,1:T(8,128)(2,1)S(1)}, u32[]{:S(2)}, u32[]{:S(2)}) collective-permute-start(bf16[256,160]{0,1:T(8,128)(2,1)S(1)} %slice_bitcast_fusion.8), channel_id=1, source_target_pairs={{0,28},{4,0},{8,4},{12,8},{16,12},{20,16},{24,20},{28,24},{1,29},{... | collective-permute-start | bytes 245768 | tf_op jit(solution)/shard_map/ppermute | solution.py:19
  56.0 5.3 %copy-start.7 = (f32[256,16,160]{0,2,1:T(8,128)}, f32[256,16,160]{0,2,1:T(8,128)S(1)}, u32[]{:S(2)}) copy-start(f32[256,16,160]{0,2,1:T(8,128)S(1)} %convolution_bitcast_fusion.1) | copy-start | bytes 7864324
  56.1 8.9 %collective-permute-start.9 = (f32[256,160]{0,1:T(8,128)S(1)}, f32[256,160]{0,1:T(8,128)S(1)}, u32[]{:S(2)}, u32[]{:S(2)}) collective-permute-start(f32[256,160]{0,1:T(8,128)S(1)} %slice_bitcast_fusion.1), channel_id=1, source_target_pairs={{0,4},{4,8},{8,12},{12,16},{16,20},{20,24},{24,28},{28,0},{1,5},{5... | collective-permute-start | bytes 491528 | tf_op jit(solution)/shard_map/ppermute | solution.py:19
  56.3 6.6 %collective-permute-start.8 = (bf16[256,160]{0,1:T(8,128)(2,1)S(1)}, bf16[256,160]{0,1:T(8,128)(2,1)S(1)}, u32[]{:S(2)}, u32[]{:S(2)}) collective-permute-start(bf16[256,160]{0,1:T(8,128)(2,1)S(1)} %slice_bitcast_fusion.7), channel_id=1, source_target_pairs={{0,28},{4,0},{8,4},{12,8},{16,12},{20,16},{24,20},{28,24},{1,29},{... | collective-permute-start | bytes 245768 | tf_op jit(solution)/shard_map/ppermute | solution.py:19
  61.4 3.6 %slice-start.4 = ((f32[256,16,160]{0,2,1:T(8,128)}), f32[256,15,160]{0,2,1:T(8,128)S(1)}, s32[]{:S(2)}) async-start(f32[256,16,160]{0,2,1:T(8,128)} %copy-done.7), calls=%async_computation.6 | async-start | bytes 4915200 | tf_op jit(solution)/shard_map/slice | solution.py:59
  67.3 5.3 %copy-start.8 = (f32[256,16,160]{0,2,1:T(8,128)}, f32[256,16,160]{0,2,1:T(8,128)S(1)}, u32[]{:S(2)}) copy-start(f32[256,16,160]{0,2,1:T(8,128)S(1)} %convolution_bitcast_fusion) | copy-start | bytes 7864324
  67.4 8.1 %collective-permute-start.11 = (f32[256,160]{0,1:T(8,128)S(1)}, f32[256,160]{0,1:T(8,128)S(1)}, u32[]{:S(2)}, u32[]{:S(2)}) collective-permute-start(f32[256,160]{0,1:T(8,128)S(1)} %slice_bitcast_fusion), channel_id=1, source_target_pairs={{0,4},{4,8},{8,12},{12,16},{16,20},{20,24},{24,28},{28,0},{1,5},{5... | collective-permute-start | bytes 491528 | tf_op jit(solution)/shard_map/ppermute | solution.py:19
  67.4 6.8 %collective-permute-start.10 = (bf16[256,160]{0,1:T(8,128)(2,1)S(1)}, bf16[256,160]{0,1:T(8,128)(2,1)S(1)}, u32[]{:S(2)}, u32[]{:S(2)}) collective-permute-start(bf16[256,160]{0,1:T(8,128)(2,1)S(1)} %slice_bitcast_fusion.6), channel_id=1, source_target_pairs={{0,28},{4,0},{8,4},{12,8},{16,12},{20,16},{24,20},{28,24},{1,29},{... | collective-permute-start | bytes 245768 | tf_op jit(solution)/shard_map/ppermute | solution.py:19
  77.8 41.8 %copy-start.2 = (bf16[256,16,160]{0,2,1:T(8,128)(2,1)S(1)}, bf16[256,16,160]{0,2,1:T(8,128)(2,1)}, u32[]{:S(2)}) copy-start(bf16[256,16,160]{0,2,1:T(8,128)(2,1)} %fusion.15) | copy-start | bytes 3932164
  77.8 125.2 %all-reduce.2.cloned.1.call-start = ((), (), s32[]{:S(2)}) async-start(), calls=%async_computation.1 | async-start | bytes 2097152 | tf_op jit(solution)/shard_map/psum | solution.py:73
  (7 other events, 16.8 us)
Sparse Core Ops, SparseCore 0:
  77.9 41.5 all-gather.1
  124.7 78.2 all-reduce.1
where the time goes:
time: 216 us; the launch traced here: 215 us
  waiting for transfers between devices  114 us (53%)
  starting transfers between devices  30 us (14%)
  matrix products  28.4 us (13%)
  blocking collectives  21.6 us (10%)
  between operations  13.9 us (6%)
  other arithmetic  4.1 us (2%)
  local copies, waits for them, and re-layouts  3.35 us (2%)
    psum x1, waiting for transfers between devices, shards(): strip, squares = lax.psum((strip, squares), 'elem')  53.1 us
    all_gather x1, waiting for transfers between devices, shards(): every_band = lax.all_gather(filtered, 'band', axis=0, tiled=True)  41.7 us
    ppermute x12, starting transfers between devices, from_behind(): return lax.ppermute(value, axis, pairs)  30 us
    psum x1, blocking collectives, shards(): strip, squares = lax.psum((strip, squares), 'elem')  21.6 us
    ppermute x12, waiting for transfers between devices, from_behind(): return lax.ppermute(value, axis, pairs)  19.2 us
    dot_general x6, matrix products, shards(): jnp.einsum('eij,bej->bei', coupling, ahead_rows, preferred_element_type=j...  9.89 us
    dot_general x1, matrix products, shards(): jnp.dot(weights, every_band, preferred_element_type=jnp.float32)  5.56 us
    dot_general x1, matrix products, shards(): lax.dot_general(filtered, every_band, (((1,), (1,)), ((), ())), preferred...  5 us
  transfers between devices with their start and end apart: 14, of which 12 were waited for; matrix products, arithmetic and copies ran while one was open for 3% of the time, Pallas kernels for 0%

commit v1 on v0

--- a/solution.py
+++ b/solution.py
@@ -1,22 +1,364 @@
+import functools
 import math
 
 import jax
 import jax.numpy as jnp
 from jax import lax
+from jax.experimental import pallas as pl
+from jax.experimental.pallas import tpu as pltpu
 from jax.sharding import PartitionSpec as P
 
 DEGREE = 6
-
+STRIPS = (3, 3)
 
 center_shift = 0.4
 half_width = 2.8
 epsilon_norm = 1e-06
+
+LANES = 128
+VMEM = pl.BlockSpec(memory_space=pltpu.VMEM)
+SMEM = pl.BlockSpec(memory_space=pltpu.SMEM)
+BF16 = jnp.bfloat16
+F32 = jnp.float32
 
 
 def from_behind(value, axis, steps):
     count = lax.axis_size(axis)
     pairs = [(source, (source + steps) % count) for source in range(count)]
     return lax.ppermute(value, axis, pairs)
+
+
+def swap(value, axis, bit):
+    count = lax.axis_size(axis)
+    return lax.ppermute(value, axis, [(source, source ^ bit) for source in range(count)])
+
+
+def params():
+    return pltpu.CompilerParams(vmem_limit_bytes=52 * 1024 * 1024)
+
+
+def advance(row, window, center, before, first):
+    total = jnp.dot(row, window, preferred_element_type=F32)
+    shifted = total - center_shift * center.astype(F32)
+    if first:
+        return (shifted * (1.0 / half_width)).astype(BF16)
+    return (shifted * (2.0 / half_width) - before.astype(F32)).astype(BF16)
+
+
+def add_squares(total, values):
+    values = values.astype(F32)
+    return total + jnp.sum(values * values, axis=0, keepdims=True)
+
+
+def interior_kernel(width, count, y_ref, rows_ref, out_ref, left_ref, right_ref, squares_ref, odd_ref, even_ref):
+    n = width
+    buffers = (even_ref, odd_ref)
+    for step in range(DEGREE):
+        source = y_ref if step == 0 else buffers[step % 2]
+        target = buffers[(step + 1) % 2]
+        older = y_ref if step == 1 else target
+        left_ref[step] = source[step * n : (step + 2) * n, :]
+        right_ref[step] = source[(count - step - 2) * n : (count - step) * n, :]
+
+        def body(e, carry):
+            at = pl.multiple_of(e * n, 16)
+            window = source[pl.ds(pl.multiple_of((e - 1) * n, 16), 3 * n), :]
+            center = source[pl.ds(at, n), :]
+            before = older[pl.ds(at, n), :]
+            target[pl.ds(at, n), :] = advance(rows_ref[e, :, : 3 * n], window, center, before, step == 0)
+            return carry
+
+        lax.fori_loop(step + 1, count - 1 - step, body, 0, unroll=2)
+    result = buffers[DEGREE % 2][DEGREE * n : (count - DEGREE) * n, :]
+    out_ref[...] = result
+    squares_ref[...] = add_squares(jnp.zeros(squares_ref.shape, F32), result)
+
+
+def strip_kernel(
+    width,
+    count,
+    strip,
+    offset,
+    last,
+    me_ref,
+    left_y_ref,
+    right_y_ref,
+    left_edge_ref,
+    right_edge_ref,
+    rows_ref,
+    left_rows_ref,
+    right_rows_ref,
+    squares_in_ref,
+    out_ref,
+    left_out_ref,
+    right_out_ref,
+    squares_ref,
+    left_scr,
+    right_scr,
+    halo_left,
+    halo_right,
+):
+    n = width
+    depth = DEGREE - 1
+    me = me_ref[0]
+    pieces = left_rows_ref.shape[0]
+    lanes = left_rows_ref.shape[2]
+    for piece in range(pieces):
+        owner = me ^ piece
+        halo_left[:, :, piece * lanes : (piece + 1) * lanes] = left_rows_ref[owner].reshape(depth, n, lanes)
+        halo_right[:, :, piece * lanes : (piece + 1) * lanes] = right_rows_ref[owner].reshape(depth, n, lanes)
+
+    def left_row(e):
+        if e < 0:
+            return halo_left[depth + e, :, : 3 * n]
+        if e > 0:
+            return rows_ref[e, :, : 3 * n]
+        turned = jnp.transpose(halo_left[depth - 1, :, 2 * n : 3 * n].astype(F32))
+        keep = rows_ref[0, :, 3 * n : 3 * n + 1].astype(F32)
+        return jnp.concatenate([(turned * keep).astype(BF16), rows_ref[0, :, n : 3 * n]], axis=1)
+
+    def right_row(e):
+        if e < count:
+            return rows_ref[e, :, : 3 * n]
+        if e > count:
+            return halo_right[e - count, :, : 3 * n]
+        turned = jnp.transpose(rows_ref[count - 1, :, 2 * n : 3 * n].astype(F32))
+        keep = halo_right[0, :, 3 * n : 3 * n + 1].astype(F32)
+        return jnp.concatenate([(turned * keep).astype(BF16), halo_right[0, :, n : 3 * n]], axis=1)
+
+    left_scr[0, : strip * n, :] = left_y_ref[...]
+    right_scr[0, 2 * n :, :] = right_y_ref[...]
+    for step in range(DEGREE):
+        left_scr[step, strip * n :, :] = left_edge_ref[step]
+        right_scr[step, : 2 * n, :] = right_edge_ref[step]
+        for j in range(strip):
+            e = offset + step + 1 + j
+            left_scr[step + 1, j * n : (j + 1) * n, :] = advance(
+                left_row(e),
+                left_scr[step, j * n : (j + 3) * n, :],
+                left_scr[step, (j + 1) * n : (j + 2) * n, :],
+                left_scr[max(step - 1, 0), (j + 2) * n : (j + 3) * n, :],
+                step == 0,
+            )
+            e = count - 1 - (offset + strip + step) + j
+            right_scr[step + 1, (j + 2) * n : (j + 3) * n, :] = advance(
+                right_row(e),
+                right_scr[step, j * n : (j + 3) * n, :],
+                right_scr[step, (j + 1) * n : (j + 2) * n, :],
+                right_scr[max(step - 1, 0), j * n : (j + 1) * n, :],
+                step == 0,
+            )
+        if not last:
+            left_out_ref[step] = left_scr[step, : 2 * n, :]
+            right_out_ref[step] = right_scr[step, strip * n : (strip + 2) * n, :]
+    result_left = left_scr[DEGREE, : strip * n, :]
+    result_right = right_scr[DEGREE, 2 * n :, :]
+    out_ref[: strip * n, :] = result_left
+    out_ref[strip * n : 2 * strip * n, :] = result_right
+    squares = add_squares(add_squares(squares_in_ref[...], result_left), result_right)
+    squares_ref[...] = squares
+    if last:
+        high = squares.astype(BF16).astype(F32)
+        low = squares - high
+        place = lax.broadcasted_iota(jnp.int32, (16, squares.shape[1]), 0)
+        both = jnp.where(place == 0, high, jnp.where(place == 1, low, 0.0))
+        out_ref[2 * strip * n :, :] = both.astype(BF16)
+
+
+def gram_kernel(chunks, blocks, shares, *refs):
+    out_ref = refs[-1]
+    grid = [refs[c * blocks : (c + 1) * blocks] for c in range(chunks)]
+    local = grid[0][0].shape[1]
+    rows = local // shares
+    full = [grid[c][0].shape[0] - (16 if c == chunks - 1 else 0) for c in range(chunks)]
+    totals = [None] * blocks
+    for c in range(chunks):
+        turned = jnp.transpose(grid[c][0][: full[c], :])
+        for r in range(blocks):
+            term = jnp.dot(turned, grid[c][r][: full[c], :], preferred_element_type=F32)
+            totals[r] = term if totals[r] is None else totals[r] + term
+    for r in range(blocks):
+        out_ref[:, :, r * local : (r + 1) * local] = totals[r].astype(BF16).reshape(shares, rows, local)
+    tail = jnp.zeros((rows, LANES), BF16)
+    place = lax.broadcasted_iota(jnp.int32, (rows, LANES), 0)
+    parts = local // LANES
+    extra = jnp.zeros((rows, LANES), F32)
+    for r in range(blocks):
+        both = grid[chunks - 1][r][full[-1] :, :].astype(F32)
+        for p in range(parts):
+            for half in range(2):
+                line = both[half : half + 1, p * LANES : (p + 1) * LANES]
+                extra = jnp.where(place == half * blocks * parts + r * parts + p, line, extra)
+    for share in range(shares):
+        out_ref[share, :, blocks * local :] = extra.astype(BF16)
+
+
+def weights_kernel(total_columns, blocks, me_ref, got_ref, out_ref):
+    shares, rows, wide = got_ref.shape
+    bands = wide - LANES
+    local = bands // blocks
+    parts = bands // LANES
+    total = got_ref[0].astype(F32)
+    for share in range(1, shares):
+        total = total + got_ref[share].astype(F32)
+    tail = total[:, bands:]
+    squares = tail[:parts, :] + tail[parts : 2 * parts, :]
+    scales = lax.rsqrt(squares + epsilon_norm)
+    me = me_ref[0]
+    first = me * rows
+    row_ids = lax.broadcasted_iota(jnp.int32, (rows, LANES), 0) + first
+    lane_ids = lax.broadcasted_iota(jnp.int32, (rows, LANES), 1)
+    own = jnp.zeros((rows, 1), F32)
+    for p in range(local // LANES):
+        hit = row_ids == lane_ids + p * LANES
+        own = own + jnp.sum(jnp.where(hit, scales[p : p + 1, :], 0.0), axis=1, keepdims=True)
+    for p in range(parts):
+        part = total[:, p * LANES : (p + 1) * LANES]
+        across = scales[p : p + 1, :]
+        diagonal = 0.0
+        if p < local // LANES:
+            hit = row_ids == lane_ids + p * LANES
+            part = jnp.where(hit, squares[p : p + 1, :], part)
+            diagonal = jnp.where(hit, 1.5, 0.0)
+        weights = math.sqrt(total_columns) * across * (diagonal - 0.5 * (own * part * across))
+        weights = weights.astype(BF16)
+        for share in range(shares):
+            out_ref[share, :, p * LANES : (p + 1) * LANES] = weights
+
+
+def rotate_kernel(chunks, blocks, spans, weights_ref, *refs):
+    out_ref = refs[-1]
+    grid = [refs[c * blocks : (c + 1) * blocks] for c in range(chunks)]
+    local = grid[0][0].shape[1]
+    for c in range(chunks):
+        for begin, size, column in spans[c]:
+            total = None
+            for r in range(blocks):
+                term = lax.dot_general(
+                    weights_ref[:, r * local : (r + 1) * local],
+                    grid[c][r][begin : begin + size, :],
+                    (((1,), (1,)), ((), ())),
+                    preferred_element_type=F32,
+                )
+                total = term if total is None else total + term
+            out_ref[:, column : column + size] = total.astype(BF16)
+
+
+def gather_blocks(own):
+    held = [own]
+    bit = lax.axis_size("band") // 2
+    found = {0: own}
+    while bit:
+        for index in list(found):
+            found[index ^ bit] = swap(found[index], "band", bit)
+        bit //= 2
+    del held
+    return [found[index] for index in range(lax.axis_size("band"))]
+
+
+def fast_shards(basis_sizes, coupling_pattern, h_diag, h_couple, bands):
+    count, n = h_diag.shape[:2]
+    local = bands.shape[0]
+    elem_size, band_size = lax.axis_size("elem"), lax.axis_size("band")
+    total_columns = elem_size * count * n
+    depth = DEGREE - 1
+    wide = -(-(3 * n + 1) // LANES) * LANES
+    lanes = wide // band_size
+    elem_me = lax.axis_index("elem").astype(jnp.int32).reshape(1)
+    band_me = lax.axis_index("band").astype(jnp.int32).reshape(1)
+
+    valid = (lax.broadcasted_iota(jnp.int32, (count, n), 1) < basis_sizes[:, None]).astype(BF16)
+    start = jnp.transpose(bands) * valid.reshape(count * n, 1)
+
+    with jax.named_scope("halo_vectors"):
+        left_y, right_y = [], []
+        near = 0
+        for strip in STRIPS:
+            far = near + strip
+            left_y.append(from_behind(start[(count - far) * n : (count - near) * n], "elem", 1))
+            right_y.append(from_behind(start[near * n : far * n], "elem", -1))
+            near = far
+
+    with jax.named_scope("rows"):
+        coupling = h_couple * coupling_pattern.astype(BF16)[:, None, None]
+        turned = jnp.swapaxes(coupling, 1, 2)
+        behind = jnp.concatenate([jnp.zeros_like(turned[:1]), turned[:-1]], axis=0)
+        spare = jnp.broadcast_to(valid[:, :, None], (count, n, wide - 3 * n))
+        rows = jnp.concatenate([behind, h_diag, coupling, spare], axis=2) * valid[:, :, None]
+
+    with jax.named_scope("halo_rows"):
+
+        def piece(block):
+            return lax.dynamic_slice_in_dim(block.reshape(depth * n, wide), band_me[0] * lanes, lanes, 1)
+
+        left_rows = from_behind(piece(rows[count - depth :]), "elem", 1)
+        right_rows = from_behind(piece(rows[:depth]), "elem", -1)
+        both = gather_blocks(jnp.stack([left_rows, right_rows]))
+        left_rows = jnp.stack([block[0] for block in both])
+        right_rows = jnp.stack([block[1] for block in both])
+
+    inner = (count - 2 * DEGREE) * n
+    edges = jax.ShapeDtypeStruct((DEGREE, 2 * n, local), BF16)
+    squares_shape = jax.ShapeDtypeStruct((1, local), F32)
+    chunk, left_edge, right_edge, squares = pl.pallas_call(
+        functools.partial(interior_kernel, n, count),
+        out_shape=[jax.ShapeDtypeStruct((inner, local), BF16), edges, edges, squares_shape],
+        in_specs=[VMEM] * 2,
+        out_specs=[VMEM] * 4,
+        scratch_shapes=[pltpu.VMEM((count * n, local), BF16)] * 2,
+        compiler_params=params(),
+        name="interior",
+    )(start, rows)
+    chunks = [gather_blocks(chunk)]
+    spans = [[(0, inner, DEGREE * n)]]
+    offset = 0
+    for index, strip in enumerate(STRIPS):
+        last = index == len(STRIPS) - 1
+        offset -= strip
+        size = 2 * strip * n + (16 if last else 0)
+        chunk, left_edge, right_edge, squares = pl.pallas_call(
+            functools.partial(strip_kernel, n, count, strip, offset, last),
+            out_shape=[jax.ShapeDtypeStruct((size, local), BF16), edges, edges, squares_shape],
+            in_specs=[SMEM] + [VMEM] * 8,
+            out_specs=[VMEM] * 4,
+            scratch_shapes=[pltpu.VMEM((DEGREE + 1, (strip + 2) * n, local), BF16)] * 2
+            + [pltpu.VMEM((depth, n, wide), BF16)] * 2,
+            compiler_params=params(),
+            name="strip",
+        )(band_me, left_y[index], right_y[index], left_edge, right_edge, rows, left_rows, right_rows, squares)
+        chunks.append(gather_blocks(chunk))
+        first = offset + DEGREE
+        spans.append([(0, strip * n, first * n), (strip * n, strip * n, (count - first - strip) * n)])
+
+    flat = [block for blocks in chunks for block in blocks]
+    slice_rows = local // elem_size
+    all_bands = local * band_size
+    partial = pl.pallas_call(
+        functools.partial(gram_kernel, len(chunks), band_size, elem_size),
+        out_shape=jax.ShapeDtypeStruct((elem_size, slice_rows, all_bands + LANES), BF16),
+        in_specs=[VMEM] * len(flat),
+        out_specs=VMEM,
+        compiler_params=params(),
+        name="gram",
+    )(*flat)
+    got = lax.all_to_all(partial, "elem", 0, 0, tiled=True)
+    mine = pl.pallas_call(
+        functools.partial(weights_kernel, total_columns, band_size),
+        out_shape=jax.ShapeDtypeStruct((elem_size, slice_rows, all_bands), BF16),
+        in_specs=[SMEM, VMEM],
+        out_specs=VMEM,
+        compiler_params=params(),
+        name="weights",
+    )(elem_me, got)
+    weights = lax.all_to_all(mine, "elem", 0, 0, tiled=True).reshape(local, all_bands)
+    return pl.pallas_call(
+        functools.partial(rotate_kernel, len(chunks), band_size, spans),
+        out_shape=jax.ShapeDtypeStruct((local, count * n), BF16),
+        in_specs=[VMEM] * (1 + len(flat)),
+        out_specs=VMEM,
+        compiler_params=params(),
+        name="rotate",
+    )(weights, *flat)
 
 
 def identity_block(shape, offset):
@@ -34,7 +376,7 @@
     )
 
 
-def shards(basis_sizes, coupling_pattern, h_diag, h_couple, bands):
+def general_shards(basis_sizes, coupling_pattern, h_diag, h_couple, bands):
     elem_local = h_diag.shape[0]
     basis_width = h_diag.shape[1]
     band_local = bands.shape[0]
@@ -77,6 +419,26 @@
     return jnp.dot(weights, every_band, preferred_element_type=jnp.float32).astype(jnp.bfloat16)
 
 
+def shards(basis_sizes, coupling_pattern, h_diag, h_couple, bands):
+    count, n = h_diag.shape[:2]
+    local = bands.shape[0]
+    elem_size, band_size = lax.axis_size("elem"), lax.axis_size("band")
+    rows = local // elem_size
+    wide = -(-(3 * n + 1) // LANES) * LANES
+    fits = (
+        band_size & (band_size - 1) == 0
+        and wide % (band_size * LANES) == 0
+        and local % LANES == 0
+        and local % elem_size == 0
+        and rows % 16 == 0
+        and rows * LANES >= 2 * local * band_size
+        and count > 2 * DEGREE
+        and n % 16 == 0
+    )
+    form = fast_shards if fits else general_shards
+    return form(basis_sizes, coupling_pattern, h_diag, h_couple, bands)
+
+
 def solution(mesh):
     in_specs = (
         P("elem"),

time: 216 us -> 148 us (0.69)
  waiting for transfers between devices: 114 us -> 54.1 us
  Pallas kernels: 0 us -> 31.3 us
  matrix products: 28.4 us -> 0 us
  between operations: 13.9 us -> 0.26 us
  local copies, waits for them, and re-layouts: 3.35 us -> 9.29 us
  other arithmetic: 4.1 us -> 8.34 us
  starting transfers between devices: 30 us -> 25.9 us
  blocking collectives: 21.6 us -> 18.2 us
    psum x1 -> x0, waiting for transfers between devices: 53.1 us -> none  [shards(): strip, squares = lax.psum((strip, squares), 'elem')]
    all_gather x1 -> x0, waiting for transfers between devices: 41.7 us -> none  [shards(): every_band = lax.all_gather(filtered, 'band', axis=0, tiled=True)]
    pallas_call x0 -> x6, Pallas kernels: none -> 31.3 us  [the longest x2 11.4 us: fast_shards(): pl.pallas_call(functools.partial(strip_kernel, n, count, strip, offset, l...]
    ppermute x0 -> x12, waiting for transfers between devices: none -> 30.5 us  [swap(): lax.ppermute(value, axis, [(source, source ^ bit) for source in range(cou...]
    dot_general x20 -> x0, matrix products: 28.4 us -> none  [the longest x6 9.89 us: shards(): jnp.einsum('eij,bej->bei', coupling, ahead_rows, preferred_element_type=j...]
    psum x1 -> x0, blocking collectives: 21.6 us -> none  [shards(): strip, squares = lax.psum((strip, squares), 'elem')]
    all_to_all x0 -> x1, blocking collectives: none -> 18.2 us  [fast_shards(): lax.all_to_all(mine, 'elem', 0, 0, tiled=True).reshape(local, all_bands)]
    all_to_all x0 -> x1, waiting for transfers between devices: none -> 16.2 us  [fast_shards(): got = lax.all_to_all(partial, 'elem', 0, 0, tiled=True)]
  transfers between devices with their start and end apart: 14 -> 19, of which waited for: 12 -> 6; matrix products, arithmetic and copies ran while one was open for 3% -> 2% of each run, Pallas kernels for 0% -> 11%
where the time goes in v1:
time: 148 us; the launch traced here: 147 us
  waiting for transfers between devices  54.1 us (37%)
  Pallas kernels  31.3 us (21%)
  starting transfers between devices  25.9 us (18%)
  blocking collectives  18.2 us (12%)
  local copies, waits for them, and re-layouts  9.29 us (6%)
  other arithmetic  8.34 us (6%)
    ppermute x12, waiting for transfers between devices, swap(): lax.ppermute(value, axis, [(source, source ^ bit) for source in range(cou...  30.5 us
    all_to_all x1, blocking collectives, fast_shards(): lax.all_to_all(mine, 'elem', 0, 0, tiled=True).reshape(local, all_bands)  18.2 us
    all_to_all x1, waiting for transfers between devices, fast_shards(): got = lax.all_to_all(partial, 'elem', 0, 0, tiled=True)  16.2 us
    ppermute x6, starting transfers between devices, from_behind(): return lax.ppermute(value, axis, pairs)  15.8 us
    pallas_call x2, Pallas kernels, fast_shards(): pl.pallas_call(functools.partial(strip_kernel, n, count, strip, offset, l...  11.4 us
    pallas_call x1, Pallas kernels, fast_shards(): pl.pallas_call(functools.partial(interior_kernel, n, count), out_shape=[j...  10.4 us
    ppermute x6, waiting for transfers between devices, from_behind(): return lax.ppermute(value, axis, pairs)  7.37 us
    unnamed x28, local copies, waits for them, and re-layouts  6.68 us
  transfers between devices with their start and end apart: 19, of which 6 were waited for; matrix products, arithmetic and copies ran while one was open for 2% of the time, Pallas kernels for 11%

profile of v1, /device:TPU:0, one launch (start us, length us, event | category | flops | bytes accessed | tf_op | source)
XLA Modules:
  0.0 147.4 jit_solution(13524180381635253229)
XLA Ops:
  0.7 1.6 %fusion.11 = bf16[16,160,160]{1,2,0:T(8,128)(2,1)S(1)} fusion(bf16[16,160,160]{2,1,0:T(8,128)(2,1)} %param.8, bf16[16]{0:T(256)(128)(2,1)S(1)} %convert_element_type.21), kind=kLoop, calls=%fused_computation.20 | loop fusion | flops 409600 | bytes 1638432 | tf_op jit(solution)/shard_map/rows/transpose | solution.py:284
  3.1 1.1 slice.52
  4.2 2.1 %copy.8 = bf16[15,160,160]{2,1,0:T(8,128)(2,1)S(1)} copy(bf16[15,160,160]{1,2,0:T(8,128)(2,1)} %slice.52) | data formatting | bytes 1536000
  6.7 4.3 %fusion.4.rows_ref = bf16[16,160,512]{2,1,0:T(8,128)(2,1)S(1)} fusion(bf16[15,160,160]{2,1,0:T(8,128)(2,1)S(1)} %copy.8, bf16[16,160,32]{2,1,0:T(8,128)(2,1)S(1)} %broadcast_in_dim.2, bf16[16,160,160]{2,1,0:T(8,128)(2,1)S(1)} %broadcast_multiply_fusion, bf16[16,160,160]{2,1,0:T(8,128)(2,1)} %param.7, bf16[16,160]{1,0:T(8,128)(2,1)S(1)} %fusion.5), kind=kLoop, calls=%fused_computation.5 | loop fusion | flops 15728640 | bytes 5196800 | tf_op jit(solution)/shard_map/rows/mul | solution.py:287
  11.1 1.5 copy-done.2
  12.7 3.0 %collective-permute-start.5 = (bf16[800,128]{1,0:T(8,128)(2,1)S(1)}, bf16[800,128]{1,0:T(8,128)(2,1)S(1)}, u32[]{:S(2)}, u32[]{:S(2)}) collective-permute-start(bf16[800,128]{1,0:T(8,128)(2,1)S(1)} %constant_dynamic-slice_fusion.1), channel_id=1, source_target_pairs={{0,4},{4,8},{8,12},{12,16},{16,20},{20,24},{24,28},{28,0},{1,5},{5... | collective-permute-start | bytes 614408 | tf_op jit(solution)/shard_map/halo_rows/ppermute | solution.py:28
  16.4 3.1 %collective-permute-start.6 = (bf16[800,128]{1,0:T(8,128)(2,1)}, bf16[800,128]{1,0:T(8,128)(2,1)S(1)}, u32[]{:S(2)}, u32[]{:S(2)}) collective-permute-start(bf16[800,128]{1,0:T(8,128)(2,1)} %constant_dynamic-slice_fusion), channel_id=1, source_target_pairs={{0,28},{4,0},{8,4},{12,8},{16,12},{20,16},{24,20},{28,24},{1,29},{... | collective-permute-start | bytes 614408 | tf_op jit(solution)/shard_map/halo_rows/ppermute | solution.py:28
  20.2 4.2 %collective-permute-done.5 = bf16[800,128]{1,0:T(8,128)(2,1)S(1)} collective-permute-done((bf16[800,128]{1,0:T(8,128)(2,1)S(1)}, bf16[800,128]{1,0:T(8,128)(2,1)S(1)}, u32[]{:S(2)}, u32[]{:S(2)}) %collective-permute-start.5) | collective-permute-done | bytes 204832 | tf_op jit(solution)/shard_map/halo_rows/ppermute | solution.py:28
  24.4 3.1 %collective-permute-done.6 = bf16[800,128]{1,0:T(8,128)(2,1)S(1)} collective-permute-done((bf16[800,128]{1,0:T(8,128)(2,1)}, bf16[800,128]{1,0:T(8,128)(2,1)S(1)}, u32[]{:S(2)}, u32[]{:S(2)}) %collective-permute-start.6) | collective-permute-done | bytes 204832 | tf_op jit(solution)/shard_map/halo_rows/ppermute | solution.py:28
  27.6 1.6 %collective-permute-start.8 = (bf16[2,800,128]{2,1,0:T(8,128)(2,1)S(1)}, bf16[2,800,128]{2,1,0:T(8,128)(2,1)S(1)}, u32[]{:S(2)}, u32[]{:S(2)}) collective-permute-start(bf16[2,800,128]{2,1,0:T(8,128)(2,1)S(1)} %pad_maximum_fusion.2), channel_id=1, source_target_pairs={{0,2},{1,3},{2,0},{3,1},{4,6},{5,7},{6,4},{7,5},{8,10},{9,11},{10,... | collective-permute-start | bytes 1228808 | tf_op jit(solution)/shard_map/halo_rows/ppermute | solution.py:33
  29.8 4.7 %collective-permute-start.4 = (bf16[480,256]{1,0:T(8,128)(2,1)S(1)}, bf16[480,256]{1,0:T(8,128)(2,1)S(1)}, u32[]{:S(2)}, u32[]{:S(2)}) collective-permute-start(bf16[480,256]{1,0:T(8,128)(2,1)S(1)} %get-tuple-element.27), channel_id=1, source_target_pairs={{0,28},{4,0},{8,4},{12,8},{16,12},{20,16},{24,20},{28,24},{1,29},{... | collective-permute-start | bytes 737288 | tf_op jit(solution)/shard_map/halo_vectors/ppermute | solution.py:28
  34.5 10.4 %interior.1 = (bf16[640,256]{1,0:T(8,128)(2,1)S(1)}, bf16[6,320,256]{2,1,0:T(8,128)(2,1)S(1)}, bf16[6,320,256]{2,1,0:T(8,128)(2,1)}, f32[1,256]{1,0:T(1,128)S(1)}) custom-call(bf16[2560,256]{1,0:T(8,128)(2,1)} %copy-done.3, bf16[16,160,512]{2,1,0:T(8,128)(2,1)} %copy-done.2), custom_call_target="tpu_custom_call" | custom-call | tf_op jit(solution)/shard_map/interior/pallas_call | solution.py:303
  45.0 5.0 %collective-permute-start.14 = (bf16[480,256]{1,0:T(8,128)(2,1)S(1)}, bf16[480,256]{1,0:T(8,128)(2,1)S(1)}, u32[]{:S(2)}, u32[]{:S(2)}) collective-permute-start(bf16[480,256]{1,0:T(8,128)(2,1)S(1)} %get-tuple-element.25), channel_id=1, source_target_pairs={{0,28},{4,0},{8,4},{12,8},{16,12},{20,16},{24,20},{28,24},{1,29},{... | collective-permute-start | bytes 737288 | tf_op jit(solution)/shard_map/halo_vectors/ppermute | solution.py:28
  51.2 5.8 %strip.2 = (bf16[960,256]{1,0:T(8,128)(2,1)S(1)}, bf16[6,320,256]{2,1,0:T(8,128)(2,1)}, bf16[6,320,256]{2,1,0:T(8,128)(2,1)}, f32[1,256]{1,0:T(1,128)S(1)}) custom-call(s32[1]{0:T(128)} %bitcast.3.me_ref, bf16[480,256]{1,0:T(8,128)(2,1)S(1)} %collective-permute-done.3.left_y_ref, bf16[480,256]{1,0:T(8,128)(2,1)S(1)} %collective-permute-done.4.right_y_ref, ...), custom_call_target="tpu_custom_call" | custom-call | tf_op jit(solution)/shard_map/strip/pallas_call | solution.py:319
  56.9 5.6 %strip.3 = (bf16[976,256]{1,0:T(8,128)(2,1)S(1)}, bf16[6,320,256]{2,1,0:T(8,128)(2,1)}, bf16[6,320,256]{2,1,0:T(8,128)(2,1)}, f32[1,256]{1,0:T(1,128)}) custom-call(s32[1]{0:T(128)} %bitcast.3.me_ref, bf16[480,256]{1,0:T(8,128)(2,1)S(1)} %collective-permute-done.13.left_y_ref, bf16[480,256]{1,0:T(8,128)(2,1)S(1)} %collective-permute-done.14.right_y_ref, ...), custom_call_target="tpu_custom_call" | custom-call | tf_op jit(solution)/shard_map/strip/pallas_call | solution.py:319
  63.0 1.5 %collective-permute-start.11 = (bf16[960,256]{1,0:T(8,128)(2,1)S(1)}, bf16[960,256]{1,0:T(8,128)(2,1)S(1)}, u32[]{:S(2)}, u32[]{:S(2)}) collective-permute-start(bf16[960,256]{1,0:T(8,128)(2,1)S(1)} %get-tuple-element.18.refs_4_), channel_id=1, source_target_pairs={{0,2},{1,3},{2,0},{3,1},{4,6},{5,7},{6,4},{7,5},{8,10},{9,11},{10,... | collective-permute-start | bytes 1474568 | tf_op jit(solution)/shard_map/ppermute | solution.py:33
  65.6 11.2 %collective-permute-done.16.refs_10_ = bf16[976,256]{1,0:T(8,128)(2,1)S(1)} collective-permute-done((bf16[976,256]{1,0:T(8,128)(2,1)S(1)}, bf16[976,256]{1,0:T(8,128)(2,1)S(1)}, u32[]{:S(2)}, u32[]{:S(2)}) %collective-permute-start.16) | collective-permute-done | bytes 499744 | tf_op jit(solution)/shard_map/ppermute | solution.py:33
  76.8 16.8 %collective-permute-done.1.refs_2_ = bf16[640,256]{1,0:T(8,128)(2,1)S(1)} collective-permute-done((bf16[640,256]{1,0:T(8,128)(2,1)S(1)}, bf16[640,256]{1,0:T(8,128)(2,1)S(1)}, u32[]{:S(2)}, u32[]{:S(2)}) %collective-permute-start.1) | collective-permute-done | bytes 327712 | tf_op jit(solution)/shard_map/ppermute | solution.py:33
  94.2 2.4 %collective-permute-done.2.refs_3_ = bf16[640,256]{1,0:T(8,128)(2,1)S(1)} collective-permute-done((bf16[640,256]{1,0:T(8,128)(2,1)S(1)}, bf16[640,256]{1,0:T(8,128)(2,1)S(1)}, u32[]{:S(2)}, u32[]{:S(2)}) %collective-permute-start.2) | collective-permute-done | bytes 327712 | tf_op jit(solution)/shard_map/ppermute | solution.py:33
  98.6 4.4 %gram.1 = bf16[8,32,1152]{2,1,0:T(8,128)(2,1)} custom-call(bf16[640,256]{1,0:T(8,128)(2,1)S(1)} %get-tuple-element.14.refs_0_, bf16[640,256]{1,0:T(8,128)(2,1)S(1)} %collective-permute-done.refs_1_, bf16[640,256]{1,0:T(8,128)(2,1)S(1)} %collective-permute-done.1.refs_2_, bf16[640,256]{1,0:T(8,128)(2,1)S(1)} %collective-permute-done.2.refs_3_, ...), custom_call_target="tpu_custom_call" | custom-call | tf_op jit(solution)/shard_map/gram/pallas_call | solution.py:336
  103.0 4.9 %all-to-all-start = ((bf16[8,32,1152]{2,1,0:T(8,128)(2,1)}), bf16[8,32,1152]{2,1,0:T(8,128)(2,1)S(1)}, u32[]{:S(2)}, u32[]{:S(2)}) async-start(bf16[8,32,1152]{2,1,0:T(8,128)(2,1)} %gram.1), calls=%async_computation | async-start | bytes 1179648 | tf_op jit(solution)/shard_map/all_to_all | solution.py:344
  107.9 16.2 %all-to-all-done.got_ref = bf16[8,32,1152]{2,1,0:T(8,128)(2,1)S(1)} async-done(((bf16[8,32,1152]{2,1,0:T(8,128)(2,1)}), bf16[8,32,1152]{2,1,0:T(8,128)(2,1)S(1)}, u32[]{:S(2)}, u32[]{:S(2)}) %all-to-all-start) | async-done | bytes 589856 | tf_op jit(solution)/shard_map/all_to_all | solution.py:344
  124.3 18.2 %all_to_all.10 = bf16[8,32,1024]{2,1,0:T(8,128)(2,1)} all-to-all(bf16[8,32,1024]{2,1,0:T(8,128)(2,1)S(1)} %weights.1), channel_id=1, replica_groups=mesh['elem'=8,'band'=4] {'elem'}, dimensions={0} | all-to-all | bytes 1048576 | tf_op jit(solution)/shard_map/all_to_all | solution.py:353
  142.5 4.9 %rotate.1 = bf16[256,2560]{1,0:T(8,128)(2,1)} custom-call(bf16[256,1024]{1,0:T(8,128)(2,1)} %bitcast.11, bf16[640,256]{1,0:T(8,128)(2,1)S(1)} %get-tuple-element.14.refs_0_, bf16[640,256]{1,0:T(8,128)(2,1)S(1)} %collective-permute-done.refs_1_, bf16[640,256]{1,0:T(8,128)(2,1)S(1)} %collective-permute-done.1.refs_2_, ...), custom_call_target="tpu_custom_call" | custom-call | tf_op jit(solution)/shard_map/rotate/pallas_call | solution.py:354
  (67 shorter events, 9.5 us)
Async XLA Ops:
  12.6 7.0 %copy-start.11 = (bf16[256,2560]{1,0:T(8,128)(2,1)S(1)}, bf16[256,2560]{1,0:T(8,128)(2,1)}, u32[]{:S(2)}) copy-start(bf16[256,2560]{1,0:T(8,128)(2,1)} %param.9) | copy-start | bytes 3932164
  12.7 11.7 %collective-permute-start.5 = (bf16[800,128]{1,0:T(8,128)(2,1)S(1)}, bf16[800,128]{1,0:T(8,128)(2,1)S(1)}, u32[]{:S(2)}, u32[]{:S(2)}) collective-permute-start(bf16[800,128]{1,0:T(8,128)(2,1)S(1)} %constant_dynamic-slice_fusion.1), channel_id=1, source_target_pairs={{0,4},{4,8},{8,12},{12,16},{16,20},{20,24},{24,28},{28,0},{1,5},{5... | collective-permute-start | bytes 614408 | tf_op jit(solution)/shard_map/halo_rows/ppermute | solution.py:28
  16.4 11.1 %collective-permute-start.6 = (bf16[800,128]{1,0:T(8,128)(2,1)}, bf16[800,128]{1,0:T(8,128)(2,1)S(1)}, u32[]{:S(2)}, u32[]{:S(2)}) collective-permute-start(bf16[800,128]{1,0:T(8,128)(2,1)} %constant_dynamic-slice_fusion), channel_id=1, source_target_pairs={{0,28},{4,0},{8,4},{12,8},{16,12},{20,16},{24,20},{28,24},{1,29},{... | collective-permute-start | bytes 614408 | tf_op jit(solution)/shard_map/halo_rows/ppermute | solution.py:28
  27.6 17.4 %collective-permute-start.8 = (bf16[2,800,128]{2,1,0:T(8,128)(2,1)S(1)}, bf16[2,800,128]{2,1,0:T(8,128)(2,1)S(1)}, u32[]{:S(2)}, u32[]{:S(2)}) collective-permute-start(bf16[2,800,128]{2,1,0:T(8,128)(2,1)S(1)} %pad_maximum_fusion.2), channel_id=1, source_target_pairs={{0,2},{1,3},{2,0},{3,1},{4,6},{5,7},{6,4},{7,5},{8,10},{9,11},{10,... | collective-permute-start | bytes 1228808 | tf_op jit(solution)/shard_map/halo_rows/ppermute | solution.py:33
  29.6 4.9 %copy-start.3 = (bf16[2560,256]{1,0:T(8,128)(2,1)}, bf16[2560,256]{1,0:T(8,128)(2,1)S(1)}, u32[]{:S(2)}) copy-start(bf16[2560,256]{1,0:T(8,128)(2,1)S(1)} %multiply_bitcast_fusion.y_ref) | copy-start | bytes 3932164
  29.6 15.4 %collective-permute-start.7 = (bf16[2,800,128]{2,1,0:T(8,128)(2,1)S(1)}, bf16[2,800,128]{2,1,0:T(8,128)(2,1)S(1)}, u32[]{:S(2)}, u32[]{:S(2)}) collective-permute-start(bf16[2,800,128]{2,1,0:T(8,128)(2,1)S(1)} %pad_maximum_fusion.2), channel_id=1, source_target_pairs={{0,1},{1,0},{2,3},{3,2},{4,5},{5,4},{6,7},{7,6},{8,9},{9,8},{10,11... | collective-permute-start | bytes 1228808 | tf_op jit(solution)/shard_map/halo_rows/ppermute | solution.py:33
  29.8 21.4 %collective-permute-start.3 = (bf16[480,256]{1,0:T(8,128)(2,1)S(1)}, bf16[480,256]{1,0:T(8,128)(2,1)S(1)}, u32[]{:S(2)}, u32[]{:S(2)}) collective-permute-start(bf16[480,256]{1,0:T(8,128)(2,1)S(1)} %get-tuple-element.28), channel_id=1, source_target_pairs={{0,4},{4,8},{8,12},{12,16},{16,20},{20,24},{24,28},{28,0},{1,5},{5... | collective-permute-start | bytes 737288 | tf_op jit(solution)/shard_map/halo_vectors/ppermute | solution.py:28
  29.8 21.3 %collective-permute-start.4 = (bf16[480,256]{1,0:T(8,128)(2,1)S(1)}, bf16[480,256]{1,0:T(8,128)(2,1)S(1)}, u32[]{:S(2)}, u32[]{:S(2)}) collective-permute-start(bf16[480,256]{1,0:T(8,128)(2,1)S(1)} %get-tuple-element.27), channel_id=1, source_target_pairs={{0,28},{4,0},{8,4},{12,8},{16,12},{20,16},{24,20},{28,24},{1,29},{... | collective-permute-start | bytes 737288 | tf_op jit(solution)/shard_map/halo_vectors/ppermute | solution.py:28
  34.5 22.4 %collective-permute-start.13 = (bf16[480,256]{1,0:T(8,128)(2,1)S(1)}, bf16[480,256]{1,0:T(8,128)(2,1)S(1)}, u32[]{:S(2)}, u32[]{:S(2)}) collective-permute-start(bf16[480,256]{1,0:T(8,128)(2,1)S(1)} %get-tuple-element.26), channel_id=1, source_target_pairs={{0,4},{4,8},{8,12},{12,16},{16,20},{20,24},{24,28},{28,0},{1,5},{5... | collective-permute-start | bytes 737288 | tf_op jit(solution)/shard_map/halo_vectors/ppermute | solution.py:28
  45.0 6.2 %copy-start.1 = (bf16[6,320,256]{2,1,0:T(8,128)(2,1)}, bf16[6,320,256]{2,1,0:T(8,128)(2,1)S(1)}, u32[]{:S(2)}) copy-start(bf16[6,320,256]{2,1,0:T(8,128)(2,1)S(1)} %get-tuple-element.15.left_edge_ref) | copy-start | bytes 2949124
  45.0 5.0 %collective-permute-start.9 = (bf16[2,800,128]{2,1,0:T(8,128)(2,1)S(1)}, bf16[2,800,128]{2,1,0:T(8,128)(2,1)S(1)}, u32[]{:S(2)}, u32[]{:S(2)}) collective-permute-start(bf16[2,800,128]{2,1,0:T(8,128)(2,1)S(1)} %collective-permute-done.8), channel_id=1, source_target_pairs={{0,1},{1,0},{2,3},{3,2},{4,5},{5,4},{6,7},{7,6},{8,9},{9,8},{10,11... | collective-permute-start | bytes 1228808 | tf_op jit(solution)/shard_map/halo_rows/ppermute | solution.py:33
  45.0 11.9 %collective-permute-start.14 = (bf16[480,256]{1,0:T(8,128)(2,1)S(1)}, bf16[480,256]{1,0:T(8,128)(2,1)S(1)}, u32[]{:S(2)}, u32[]{:S(2)}) collective-permute-start(bf16[480,256]{1,0:T(8,128)(2,1)S(1)} %get-tuple-element.25), channel_id=1, source_target_pairs={{0,28},{4,0},{8,4},{12,8},{16,12},{20,16},{24,20},{28,24},{1,29},{... | collective-permute-start | bytes 737288 | tf_op jit(solution)/shard_map/halo_vectors/ppermute | solution.py:28
  62.5 34.2 %copy-start = (bf16[976,256]{1,0:T(8,128)(2,1)}, bf16[976,256]{1,0:T(8,128)(2,1)S(1)}, u32[]{:S(2)}) copy-start(bf16[976,256]{1,0:T(8,128)(2,1)S(1)} %get-tuple-element.22.refs_8_) | copy-start | bytes 1499140
  62.5 14.2 %collective-permute-start.16 = (bf16[976,256]{1,0:T(8,128)(2,1)S(1)}, bf16[976,256]{1,0:T(8,128)(2,1)S(1)}, u32[]{:S(2)}, u32[]{:S(2)}) collective-permute-start(bf16[976,256]{1,0:T(8,128)(2,1)S(1)} %get-tuple-element.22.refs_8_), channel_id=1, source_target_pairs={{0,2},{1,3},{2,0},{3,1},{4,6},{5,7},{6,4},{7,5},{8,10},{9,11},{10,... | collective-permute-start | bytes 1499144 | tf_op jit(solution)/shard_map/ppermute | solution.py:33
  63.0 30.6 %collective-permute-start.11 = (bf16[960,256]{1,0:T(8,128)(2,1)S(1)}, bf16[960,256]{1,0:T(8,128)(2,1)S(1)}, u32[]{:S(2)}, u32[]{:S(2)}) collective-permute-start(bf16[960,256]{1,0:T(8,128)(2,1)S(1)} %get-tuple-element.18.refs_4_), channel_id=1, source_target_pairs={{0,2},{1,3},{2,0},{3,1},{4,6},{5,7},{6,4},{7,5},{8,10},{9,11},{10,... | collective-permute-start | bytes 1474568 | tf_op jit(solution)/shard_map/ppermute | solution.py:33
  64.6 29.0 %collective-permute-start.1 = (bf16[640,256]{1,0:T(8,128)(2,1)S(1)}, bf16[640,256]{1,0:T(8,128)(2,1)S(1)}, u32[]{:S(2)}, u32[]{:S(2)}) collective-permute-start(bf16[640,256]{1,0:T(8,128)(2,1)S(1)} %get-tuple-element.14.refs_0_), channel_id=1, source_target_pairs={{0,2},{1,3},{2,0},{3,1},{4,6},{5,7},{6,4},{7,5},{8,10},{9,11},{10,... | collective-permute-start | bytes 983048 | tf_op jit(solution)/shard_map/ppermute | solution.py:33
  65.1 29.1 %collective-permute-start = (bf16[640,256]{1,0:T(8,128)(2,1)S(1)}, bf16[640,256]{1,0:T(8,128)(2,1)S(1)}, u32[]{:S(2)}, u32[]{:S(2)}) collective-permute-start(bf16[640,256]{1,0:T(8,128)(2,1)S(1)} %get-tuple-element.14.refs_0_), channel_id=1, source_target_pairs={{0,1},{1,0},{2,3},{3,2},{4,5},{5,4},{6,7},{7,6},{8,9},{9,8},{10,11... | collective-permute-start | bytes 983048 | tf_op jit(solution)/shard_map/ppermute | solution.py:33
  65.1 31.6 %collective-permute-start.15 = (bf16[976,256]{1,0:T(8,128)(2,1)S(1)}, bf16[976,256]{1,0:T(8,128)(2,1)S(1)}, u32[]{:S(2)}, u32[]{:S(2)}) collective-permute-start(bf16[976,256]{1,0:T(8,128)(2,1)S(1)} %get-tuple-element.22.refs_8_), channel_id=1, source_target_pairs={{0,1},{1,0},{2,3},{3,2},{4,5},{5,4},{6,7},{7,6},{8,9},{9,8},{10,11... | collective-permute-start | bytes 1499144 | tf_op jit(solution)/shard_map/ppermute | solution.py:33
  76.8 19.9 %copy-start.5 = (bf16[976,256]{1,0:T(8,128)(2,1)}, bf16[976,256]{1,0:T(8,128)(2,1)S(1)}, u32[]{:S(2)}) copy-start(bf16[976,256]{1,0:T(8,128)(2,1)S(1)} %collective-permute-done.16.refs_10_) | copy-start | bytes 1499140
  76.8 19.9 %collective-permute-start.17 = (bf16[976,256]{1,0:T(8,128)(2,1)S(1)}, bf16[976,256]{1,0:T(8,128)(2,1)S(1)}, u32[]{:S(2)}, u32[]{:S(2)}) collective-permute-start(bf16[976,256]{1,0:T(8,128)(2,1)S(1)} %collective-permute-done.16.refs_10_), channel_id=1, source_target_pairs={{0,1},{1,0},{2,3},{3,2},{4,5},{5,4},{6,7},{7,6},{8,9},{9,8},{10,11... | collective-permute-start | bytes 1499144 | tf_op jit(solution)/shard_map/ppermute | solution.py:33
  93.6 3.0 %collective-permute-start.10 = (bf16[960,256]{1,0:T(8,128)(2,1)S(1)}, bf16[960,256]{1,0:T(8,128)(2,1)S(1)}, u32[]{:S(2)}, u32[]{:S(2)}) collective-permute-start(bf16[960,256]{1,0:T(8,128)(2,1)S(1)} %get-tuple-element.18.refs_4_), channel_id=1, source_target_pairs={{0,1},{1,0},{2,3},{3,2},{4,5},{5,4},{6,7},{7,6},{8,9},{9,8},{10,11... | collective-permute-start | bytes 1474568 | tf_op jit(solution)/shard_map/ppermute | solution.py:33
  93.6 3.0 %collective-permute-start.12 = (bf16[960,256]{1,0:T(8,128)(2,1)S(1)}, bf16[960,256]{1,0:T(8,128)(2,1)S(1)}, u32[]{:S(2)}, u32[]{:S(2)}) collective-permute-start(bf16[960,256]{1,0:T(8,128)(2,1)S(1)} %collective-permute-done.11.refs_6_), channel_id=1, source_target_pairs={{0,1},{1,0},{2,3},{3,2},{4,5},{5,4},{6,7},{7,6},{8,9},{9,8},{10,11... | collective-permute-start | bytes 1474568 | tf_op jit(solution)/shard_map/ppermute | solution.py:33
  94.1 2.5 %collective-permute-start.2 = (bf16[640,256]{1,0:T(8,128)(2,1)S(1)}, bf16[640,256]{1,0:T(8,128)(2,1)S(1)}, u32[]{:S(2)}, u32[]{:S(2)}) collective-permute-start(bf16[640,256]{1,0:T(8,128)(2,1)S(1)} %collective-permute-done.1.refs_2_), channel_id=1, source_target_pairs={{0,1},{1,0},{2,3},{3,2},{4,5},{5,4},{6,7},{7,6},{8,9},{9,8},{10,11... | collective-permute-start | bytes 983048 | tf_op jit(solution)/shard_map/ppermute | solution.py:33
  103.0 21.1 %all-to-all-start = ((bf16[8,32,1152]{2,1,0:T(8,128)(2,1)}), bf16[8,32,1152]{2,1,0:T(8,128)(2,1)S(1)}, u32[]{:S(2)}, u32[]{:S(2)}) async-start(bf16[8,32,1152]{2,1,0:T(8,128)(2,1)} %gram.1), calls=%async_computation | async-start | bytes 1179648 | tf_op jit(solution)/shard_map/all_to_all | solution.py:344
  (8 other events, 10.6 us)

commit v2 on v1

--- a/solution.py
+++ b/solution.py
@@ -10,6 +10,7 @@
 
 DEGREE = 6
 STRIPS = (3, 3)
+SPLIT = 2
 
 center_shift = 0.4
 half_width = 2.8
@@ -33,8 +34,52 @@
     return lax.ppermute(value, axis, [(source, source ^ bit) for source in range(count)])
 
 
-def params():
-    return pltpu.CompilerParams(vmem_limit_bytes=52 * 1024 * 1024)
+def after(value, *others):
+    return lax.optimization_barrier((value, *others))[0]
+
+
+def params(mib):
+    return pltpu.CompilerParams(vmem_limit_bytes=mib * 1024 * 1024)
+
+
+def about(microseconds):
+    return pl.CostEstimate(flops=int(microseconds * 1.15e9), bytes_accessed=1, transcendentals=0)
+
+
+def rows_kernel(width, lanes, me_ref, sizes_ref, pattern_ref, diag_ref, couple_ref, rows_ref, first_ref, last_ref):
+    n = width
+    count = rows_ref.shape[0]
+    depth = DEGREE - 1
+    wide = rows_ref.shape[2]
+    place = lax.broadcasted_iota(jnp.int32, (n, wide), 0)
+    behind = jnp.zeros((n, n), F32)
+    ones = jnp.ones((n, wide - 3 * n), F32)
+    for e in range(count):
+        couple = couple_ref[e].astype(F32) * pattern_ref[e].astype(F32)
+        whole = jnp.concatenate([behind, diag_ref[e].astype(F32), couple, ones], axis=1)
+        rows_ref[e] = jnp.where(place < sizes_ref[e], whole, 0.0).astype(BF16)
+        behind = jnp.transpose(couple)
+    at = pl.ds(pl.multiple_of(me_ref[0] * lanes, lanes), lanes)
+    for e in range(depth):
+        first_ref[e * n : (e + 1) * n, :] = rows_ref[e, :, at]
+        last_ref[e * n : (e + 1) * n, :] = rows_ref[count - depth + e, :, at]
+
+
+def vectors_kernel(width, count, group, sizes_ref, bands_ref, out_ref, *edge_refs):
+    n = width
+    local = bands_ref.shape[0]
+    place = lax.broadcasted_iota(jnp.int32, (n, local), 0)
+    for begin in range(0, count, group):
+        turned = jnp.transpose(bands_ref[:, begin * n : (begin + group) * n])
+        for e in range(begin, begin + group):
+            part = turned[(e - begin) * n : (e - begin + 1) * n, :].astype(F32)
+            out_ref[e * n : (e + 1) * n, :] = jnp.where(place < sizes_ref[e], part, 0.0).astype(BF16)
+    near = 0
+    for index, strip in enumerate(STRIPS):
+        far = near + strip
+        edge_refs[2 * index][...] = out_ref[near * n : far * n, :]
+        edge_refs[2 * index + 1][...] = out_ref[(count - far) * n : (count - near) * n, :]
+        near = far
 
 
 def advance(row, window, center, before, first):
@@ -50,15 +95,30 @@
     return total + jnp.sum(values * values, axis=0, keepdims=True)
 
 
-def interior_kernel(width, count, y_ref, rows_ref, out_ref, left_ref, right_ref, squares_ref, odd_ref, even_ref):
+def interior_kernel(width, count, begin, end, rows_ref, *refs):
     n = width
+    if begin == 0:
+        first_ref, refs = refs[0], refs[1:]
+    else:
+        older_ref, newer_ref, refs = refs[0], refs[1], refs[2:]
+    if end < DEGREE:
+        left_ref, right_ref, even_ref, odd_ref = refs
+    else:
+        left_ref, right_ref, out_ref, squares_ref, even_ref, odd_ref = refs
     buffers = (even_ref, odd_ref)
-    for step in range(DEGREE):
-        source = y_ref if step == 0 else buffers[step % 2]
-        target = buffers[(step + 1) % 2]
-        older = y_ref if step == 1 else target
-        left_ref[step] = source[step * n : (step + 2) * n, :]
-        right_ref[step] = source[(count - step - 2) * n : (count - step) * n, :]
+    for step in range(begin, end):
+        source = buffers[step % 2]
+        older = target = buffers[(step + 1) % 2]
+        if step == begin:
+            source = first_ref if begin == 0 else newer_ref
+        if step == 1 and begin == 0:
+            older = first_ref
+        elif step == begin and begin > 0:
+            older = older_ref
+        elif step == begin + 1 and begin > 0:
+            older = newer_ref
+        left_ref[step - begin] = source[step * n : (step + 2) * n, :]
+        right_ref[step - begin] = source[(count - step - 2) * n : (count - step) * n, :]
 
         def body(e, carry):
             at = pl.multiple_of(e * n, 16)
@@ -69,9 +129,10 @@
             return carry
 
         lax.fori_loop(step + 1, count - 1 - step, body, 0, unroll=2)
-    result = buffers[DEGREE % 2][DEGREE * n : (count - DEGREE) * n, :]
-    out_ref[...] = result
-    squares_ref[...] = add_squares(jnp.zeros(squares_ref.shape, F32), result)
+    if end == DEGREE:
+        result = buffers[DEGREE % 2][DEGREE * n : (count - DEGREE) * n, :]
+        out_ref[...] = result
+        squares_ref[...] = add_squares(jnp.zeros(squares_ref.shape, F32), result)
 
 
 def strip_kernel(
@@ -80,33 +141,32 @@
     strip,
     offset,
     last,
+    edge_sizes,
+    pieces,
     me_ref,
     left_y_ref,
     right_y_ref,
-    left_edge_ref,
-    right_edge_ref,
     rows_ref,
-    left_rows_ref,
-    right_rows_ref,
     squares_in_ref,
-    out_ref,
-    left_out_ref,
-    right_out_ref,
-    squares_ref,
-    left_scr,
-    right_scr,
-    halo_left,
-    halo_right,
+    *refs,
 ):
     n = width
     depth = DEGREE - 1
     me = me_ref[0]
-    pieces = left_rows_ref.shape[0]
-    lanes = left_rows_ref.shape[2]
-    for piece in range(pieces):
-        owner = me ^ piece
-        halo_left[:, :, piece * lanes : (piece + 1) * lanes] = left_rows_ref[owner].reshape(depth, n, lanes)
-        halo_right[:, :, piece * lanes : (piece + 1) * lanes] = right_rows_ref[owner].reshape(depth, n, lanes)
+    refs, outs = refs[:-8], refs[-8:]
+    all_ref = outs[1]
+    half = len(edge_sizes)
+    left_edge = [ref.at[k] for ref, size in zip(refs[:half], edge_sizes) for k in range(size)]
+    right_edge = [ref.at[k] for ref, size in zip(refs[half : 2 * half], edge_sizes) for k in range(size)]
+    refs = refs[2 * half :]
+    before = refs[4 * pieces :]
+    out_ref, left_out_ref, right_out_ref, squares_ref, left_scr, right_scr, halo_left, halo_right = outs
+    lanes = refs[0].shape[1]
+    for index in range(pieces):
+        for side in range(2):
+            at = pl.ds(pl.multiple_of((me ^ (side * pieces + index)) * lanes, lanes), lanes)
+            halo_left[:, :, at] = refs[2 * side * pieces + index][...].reshape(depth, n, lanes)
+            halo_right[:, :, at] = refs[(2 * side + 1) * pieces + index][...].reshape(depth, n, lanes)
 
     def left_row(e):
         if e < 0:
@@ -129,8 +189,8 @@
     left_scr[0, : strip * n, :] = left_y_ref[...]
     right_scr[0, 2 * n :, :] = right_y_ref[...]
     for step in range(DEGREE):
-        left_scr[step, strip * n :, :] = left_edge_ref[step]
-        right_scr[step, : 2 * n, :] = right_edge_ref[step]
+        left_scr[step, strip * n :, :] = left_edge[step][...]
+        right_scr[step, : 2 * n, :] = right_edge[step][...]
         for j in range(strip):
             e = offset + step + 1 + j
             left_scr[step + 1, j * n : (j + 1) * n, :] = advance(
@@ -163,32 +223,55 @@
         place = lax.broadcasted_iota(jnp.int32, (16, squares.shape[1]), 0)
         both = jnp.where(place == 0, high, jnp.where(place == 1, low, 0.0))
         out_ref[2 * strip * n :, :] = both.astype(BF16)
-
-
-def gram_kernel(chunks, blocks, shares, *refs):
-    out_ref = refs[-1]
-    grid = [refs[c * blocks : (c + 1) * blocks] for c in range(chunks)]
-    local = grid[0][0].shape[1]
-    rows = local // shares
-    full = [grid[c][0].shape[0] - (16 if c == chunks - 1 else 0) for c in range(chunks)]
-    totals = [None] * blocks
-    for c in range(chunks):
-        turned = jnp.transpose(grid[c][0][: full[c], :])
-        for r in range(blocks):
-            term = jnp.dot(turned, grid[c][r][: full[c], :], preferred_element_type=F32)
-            totals[r] = term if totals[r] is None else totals[r] + term
-    for r in range(blocks):
-        out_ref[:, :, r * local : (r + 1) * local] = totals[r].astype(BF16).reshape(shares, rows, local)
-    tail = jnp.zeros((rows, LANES), BF16)
+        begin = 0
+        for ref in (*before, out_ref):
+            all_ref[begin : begin + ref.shape[0], :] = ref[...]
+            begin += ref.shape[0]
+
+
+def gram_kernel(chunks, blocks, shares, early, *refs):
+    outs = refs[-2:] if early else refs[-1:]
+    out_ref = outs[0]
+    half = blocks // 2
+    rows = out_ref.shape[1]
+    lower = refs[:half]
+    local = lower[0].shape[1]
+    length = lower[0].shape[0] - 16
+    totals = [None] * half
+    if early:
+        turned_ref = outs[1]
+        turned_ref[...] = jnp.transpose(lower[0][:length, :])
+        for r in range(half):
+            totals[r] = jnp.dot(turned_ref[...], lower[r][:length, :], preferred_element_type=F32)
+    else:
+        turned_ref = refs[half]
+        begin = 0
+        upper = [refs[half + 1 + c * half : half + 1 + (c + 1) * half] for c in range(chunks)]
+        for c in range(chunks):
+            size = upper[c][0].shape[0] - (16 if c == chunks - 1 else 0)
+            for r in range(half):
+                term = jnp.dot(
+                    turned_ref[:, begin : begin + size], upper[c][r][:size, :], preferred_element_type=F32
+                )
+                totals[r] = term if c == 0 else totals[r] + term
+            begin += size
+    base = 0 if early else half
+    for r in range(half):
+        at = (base + r) * local
+        out_ref[:, :, at : at + local] = totals[r].astype(BF16).reshape(shares, rows, local)
+    if early:
+        return
+    out_ref[:, :, : half * local] = refs[-2][...]
     place = lax.broadcasted_iota(jnp.int32, (rows, LANES), 0)
     parts = local // LANES
     extra = jnp.zeros((rows, LANES), F32)
     for r in range(blocks):
-        both = grid[chunks - 1][r][full[-1] :, :].astype(F32)
+        ref = lower[r] if r < half else upper[-1][r - half]
+        both = ref[ref.shape[0] - 16 :, :].astype(F32)
         for p in range(parts):
-            for half in range(2):
-                line = both[half : half + 1, p * LANES : (p + 1) * LANES]
-                extra = jnp.where(place == half * blocks * parts + r * parts + p, line, extra)
+            for part in range(2):
+                line = both[part : part + 1, p * LANES : (p + 1) * LANES]
+                extra = jnp.where(place == part * blocks * parts + r * parts + p, line, extra)
     for share in range(shares):
         out_ref[share, :, blocks * local :] = extra.astype(BF16)
 
@@ -228,32 +311,38 @@
 
 def rotate_kernel(chunks, blocks, spans, weights_ref, *refs):
     out_ref = refs[-1]
-    grid = [refs[c * blocks : (c + 1) * blocks] for c in range(chunks)]
-    local = grid[0][0].shape[1]
+    half = blocks // 2
+    lower = refs[:half]
+    upper = [refs[half + c * half : half + (c + 1) * half] for c in range(chunks)]
+    local = lower[0].shape[1]
+    start = 0
     for c in range(chunks):
         for begin, size, column in spans[c]:
             total = None
             for r in range(blocks):
+                if r < half:
+                    part = lower[r][start + begin : start + begin + size, :]
+                else:
+                    part = upper[c][r - half][begin : begin + size, :]
                 term = lax.dot_general(
                     weights_ref[:, r * local : (r + 1) * local],
-                    grid[c][r][begin : begin + size, :],
+                    part,
                     (((1,), (1,)), ((), ())),
                     preferred_element_type=F32,
                 )
                 total = term if total is None else total + term
             out_ref[:, column : column + size] = total.astype(BF16)
-
-
-def gather_blocks(own):
-    held = [own]
-    bit = lax.axis_size("band") // 2
+        start += sum(size for _, size, _ in spans[c])
+
+
+def lower_blocks(own):
+    bit = lax.axis_size("band") // 4
     found = {0: own}
     while bit:
         for index in list(found):
             found[index ^ bit] = swap(found[index], "band", bit)
         bit //= 2
-    del held
-    return [found[index] for index in range(lax.axis_size("band"))]
+    return [found[index] for index in sorted(found)]
 
 
 def fast_shards(basis_sizes, coupling_pattern, h_diag, h_couple, bands):
@@ -264,90 +353,133 @@
     depth = DEGREE - 1
     wide = -(-(3 * n + 1) // LANES) * LANES
     lanes = wide // band_size
+    half = band_size // 2
     elem_me = lax.axis_index("elem").astype(jnp.int32).reshape(1)
     band_me = lax.axis_index("band").astype(jnp.int32).reshape(1)
 
-    valid = (lax.broadcasted_iota(jnp.int32, (count, n), 1) < basis_sizes[:, None]).astype(BF16)
-    start = jnp.transpose(bands) * valid.reshape(count * n, 1)
-
-    with jax.named_scope("halo_vectors"):
-        left_y, right_y = [], []
-        near = 0
-        for strip in STRIPS:
-            far = near + strip
-            left_y.append(from_behind(start[(count - far) * n : (count - near) * n], "elem", 1))
-            right_y.append(from_behind(start[near * n : far * n], "elem", -1))
-            near = far
-
-    with jax.named_scope("rows"):
-        coupling = h_couple * coupling_pattern.astype(BF16)[:, None, None]
-        turned = jnp.swapaxes(coupling, 1, 2)
-        behind = jnp.concatenate([jnp.zeros_like(turned[:1]), turned[:-1]], axis=0)
-        spare = jnp.broadcast_to(valid[:, :, None], (count, n, wide - 3 * n))
-        rows = jnp.concatenate([behind, h_diag, coupling, spare], axis=2) * valid[:, :, None]
-
-    with jax.named_scope("halo_rows"):
-
-        def piece(block):
-            return lax.dynamic_slice_in_dim(block.reshape(depth * n, wide), band_me[0] * lanes, lanes, 1)
-
-        left_rows = from_behind(piece(rows[count - depth :]), "elem", 1)
-        right_rows = from_behind(piece(rows[:depth]), "elem", -1)
-        both = gather_blocks(jnp.stack([left_rows, right_rows]))
-        left_rows = jnp.stack([block[0] for block in both])
-        right_rows = jnp.stack([block[1] for block in both])
+    rows, first_rows, last_rows = pl.pallas_call(
+        functools.partial(rows_kernel, n, lanes),
+        out_shape=[jax.ShapeDtypeStruct((count, n, wide), BF16)]
+        + [jax.ShapeDtypeStruct((depth * n, lanes), BF16)] * 2,
+        in_specs=[SMEM] * 3 + [VMEM] * 2,
+        out_specs=[VMEM] * 3,
+        compiler_params=params(16),
+        cost_estimate=about(0.01),
+        name="rows",
+    )(band_me, basis_sizes, coupling_pattern, h_diag, h_couple)
+    left_rows = from_behind(last_rows, "elem", 1)
+    right_rows = from_behind(first_rows, "elem", -1)
+
+    start, *ends = pl.pallas_call(
+        functools.partial(vectors_kernel, n, count, math.lcm(n, LANES) // n),
+        out_shape=[jax.ShapeDtypeStruct((count * n, local), BF16)]
+        + [jax.ShapeDtypeStruct((strip * n, local), BF16) for strip in STRIPS for _ in range(2)],
+        in_specs=[SMEM, VMEM],
+        out_specs=[VMEM] * (1 + 2 * len(STRIPS)),
+        compiler_params=params(16),
+        cost_estimate=about(0.01),
+        name="vectors",
+    )(basis_sizes, bands)
+    left_y = [from_behind(ends[2 * index + 1], "elem", 1) for index in range(len(STRIPS))]
+    right_y = [from_behind(ends[2 * index], "elem", -1) for index in range(len(STRIPS))]
 
     inner = (count - 2 * DEGREE) * n
-    edges = jax.ShapeDtypeStruct((DEGREE, 2 * n, local), BF16)
+    whole = jax.ShapeDtypeStruct((count * n, local), BF16)
     squares_shape = jax.ShapeDtypeStruct((1, local), F32)
-    chunk, left_edge, right_edge, squares = pl.pallas_call(
-        functools.partial(interior_kernel, n, count),
-        out_shape=[jax.ShapeDtypeStruct((inner, local), BF16), edges, edges, squares_shape],
+
+    def edges(steps):
+        return [jax.ShapeDtypeStruct((steps, 2 * n, local), BF16)] * 2
+
+    left_edge, right_edge, even, odd = pl.pallas_call(
+        functools.partial(interior_kernel, n, count, 0, SPLIT),
+        out_shape=edges(SPLIT) + [whole] * 2,
         in_specs=[VMEM] * 2,
         out_specs=[VMEM] * 4,
+        compiler_params=params(20),
+        cost_estimate=about(0.01),
+        name="interior_first",
+    )(rows, start)
+    own_rows = [after(side, even) for side in (left_rows, right_rows)]
+    across_rows = [swap(side, "band", half) for side in own_rows]
+    older, newer = (odd, even) if SPLIT % 2 == 0 else (even, odd)
+    left_more, right_more, chunk, squares = pl.pallas_call(
+        functools.partial(interior_kernel, n, count, SPLIT, DEGREE),
+        out_shape=edges(DEGREE - SPLIT) + [jax.ShapeDtypeStruct((inner, local), BF16), squares_shape],
+        in_specs=[VMEM] * 3,
+        out_specs=[VMEM] * 4,
         scratch_shapes=[pltpu.VMEM((count * n, local), BF16)] * 2,
-        compiler_params=params(),
-        name="interior",
-    )(start, rows)
-    chunks = [gather_blocks(chunk)]
+        compiler_params=params(20),
+        cost_estimate=about(0.01),
+        name="interior_rest",
+    )(rows, older, newer)
+    left_edge = [left_edge, left_more]
+    right_edge = [right_edge, right_more]
+    across_rows = [after(side, chunk, left_y[0], right_y[0]) for side in across_rows]
+    both = [block for side in (*own_rows, *across_rows) for block in lower_blocks(side)]
+    chunks, across = [chunk], [swap(chunk, "band", half)]
     spans = [[(0, inner, DEGREE * n)]]
     offset = 0
     for index, strip in enumerate(STRIPS):
         last = index == len(STRIPS) - 1
         offset -= strip
+        if index:
+            left_edge = [after(left_edge[0], across[index - 1])]
         size = 2 * strip * n + (16 if last else 0)
-        chunk, left_edge, right_edge, squares = pl.pallas_call(
-            functools.partial(strip_kernel, n, count, strip, offset, last),
-            out_shape=[jax.ShapeDtypeStruct((size, local), BF16), edges, edges, squares_shape],
-            in_specs=[SMEM] + [VMEM] * 8,
+        sizes = [edge.shape[0] for edge in left_edge]
+        shape = jax.ShapeDtypeStruct((size, local), BF16)
+        full = jax.ShapeDtypeStruct((count * n + 16, local), BF16)
+        before = chunks if last else []
+        chunk, *others, squares = pl.pallas_call(
+            functools.partial(strip_kernel, n, count, strip, offset, last, sizes, half),
+            out_shape=[shape, *([full, jax.ShapeDtypeStruct((8, LANES), F32)] if last else edges(DEGREE)), squares_shape],
+            in_specs=[SMEM] + [VMEM] * (4 + 2 * len(sizes) + 4 * half + len(before)),
             out_specs=[VMEM] * 4,
             scratch_shapes=[pltpu.VMEM((DEGREE + 1, (strip + 2) * n, local), BF16)] * 2
             + [pltpu.VMEM((depth, n, wide), BF16)] * 2,
-            compiler_params=params(),
+            compiler_params=params(32),
+            cost_estimate=about(3),
             name="strip",
-        )(band_me, left_y[index], right_y[index], left_edge, right_edge, rows, left_rows, right_rows, squares)
-        chunks.append(gather_blocks(chunk))
+        )(band_me, left_y[index], right_y[index], rows, squares, *left_edge, *right_edge, *both, *before)
+        left_edge, right_edge = [others[0]], [others[1]]
+        if last:
+            own = others[0]
+            chunk = after(chunk, across[index])
+        chunks.append(chunk)
+        across.append(swap(chunk, "band", half))
         first = offset + DEGREE
         spans.append([(0, strip * n, first * n), (strip * n, strip * n, (count - first - strip) * n)])
 
-    flat = [block for blocks in chunks for block in blocks]
     slice_rows = local // elem_size
     all_bands = local * band_size
-    partial = pl.pallas_call(
-        functools.partial(gram_kernel, len(chunks), band_size, elem_size),
-        out_shape=jax.ShapeDtypeStruct((elem_size, slice_rows, all_bands + LANES), BF16),
-        in_specs=[VMEM] * len(flat),
-        out_specs=VMEM,
-        compiler_params=params(),
-        name="gram",
-    )(*flat)
+
+    def gram(early, blocks):
+        wide = all_bands // 2 if early else all_bands + LANES
+        shapes = [jax.ShapeDtypeStruct((elem_size, slice_rows, wide), BF16)]
+        if early:
+            shapes.append(jax.ShapeDtypeStruct((local, count * n), BF16))
+        return pl.pallas_call(
+            functools.partial(gram_kernel, len(chunks), band_size, elem_size, early),
+            out_shape=shapes,
+            in_specs=[VMEM] * len(blocks),
+            out_specs=[VMEM] * len(shapes),
+            compiler_params=params(20),
+            cost_estimate=about(0.01),
+            name="gram_early" if early else "gram_late",
+        )(*blocks)
+
+    lower = lower_blocks(after(own, across[-2]))
+    early, turned = gram(True, lower)
+    upper = [block for chunk in across for block in lower_blocks(chunk)]
+    (partial,) = gram(False, [*lower, turned, *upper, early])
     got = lax.all_to_all(partial, "elem", 0, 0, tiled=True)
+    flat = [*lower, *upper]
     mine = pl.pallas_call(
         functools.partial(weights_kernel, total_columns, band_size),
         out_shape=jax.ShapeDtypeStruct((elem_size, slice_rows, all_bands), BF16),
         in_specs=[SMEM, VMEM],
         out_specs=VMEM,
-        compiler_params=params(),
+        compiler_params=params(8),
+        cost_estimate=about(0.01),
         name="weights",
     )(elem_me, got)
     weights = lax.all_to_all(mine, "elem", 0, 0, tiled=True).reshape(local, all_bands)
@@ -356,7 +488,8 @@
         out_shape=jax.ShapeDtypeStruct((local, count * n), BF16),
         in_specs=[VMEM] * (1 + len(flat)),
         out_specs=VMEM,
-        compiler_params=params(),
+        compiler_params=params(24),
+        cost_estimate=about(0.01),
         name="rotate",
     )(weights, *flat)
 

time: 148 us -> 120 us (0.81)
  waiting for transfers between devices: 54.1 us -> 42.8 us
  Pallas kernels: 31.3 us -> 22.1 us
  other arithmetic: 8.34 us -> 0 us
  starting transfers between devices: 25.9 us -> 28.9 us
  local copies, waits for them, and re-layouts: 9.29 us -> 7.24 us
    ppermute x12 -> x13, waiting for transfers between devices: 30.5 us -> 17.5 us  [swap(): lax.ppermute(value, axis, [(source, source ^ bit) for source in range(cou...]
    pallas_call x2, Pallas kernels: 11.4 us -> 5.85 us  [fast_shards(): pl.pallas_call(functools.partial(strip_kernel, n, count, strip, offset, l...]
    mul x3 -> x0, other arithmetic: 4.9 us -> none  [the longest x1 4.34 us: fast_shards(): jnp.concatenate([behind, h_diag, coupling, spare], axis=2)]
    pallas_call x1, Pallas kernels: 4.89 us -> 2.82 us  [fast_shards(): pl.pallas_call(functools.partial(rotate_kernel, len(chunks), band_size, s...]
    ppermute x12 -> x13, starting transfers between devices: 5.27 us -> 7.29 us  [swap(): lax.ppermute(value, axis, [(source, source ^ bit) for source in range(cou...]
    ppermute x6, waiting for transfers between devices: 7.37 us -> 9.04 us  [from_behind(): return lax.ppermute(value, axis, pairs)]
    pallas_call x2 -> x6, Pallas kernels: 14.8 us -> 13.2 us  [the longest x1 3.99 us: fast_shards(): pl.pallas_call(functools.partial(interior_kernel, n, count, SPLIT, DEGREE...]
    transpose x1 -> x0, other arithmetic: 1.57 us -> none  [fast_shards(): turned = jnp.swapaxes(coupling, 1, 2)]
  transfers between devices with their start and end apart: 19 -> 20, of which waited for: 6 -> 9; matrix products, arithmetic and copies ran while one was open for 2% -> 0% of each run, Pallas kernels for 11% -> 13%
where the time goes in v2:
time: 120 us; the launch traced here: 119 us
  waiting for transfers between devices  42.8 us (36%)
  starting transfers between devices  28.9 us (24%)
  Pallas kernels  22.1 us (18%)
  blocking collectives  18.2 us (15%)
  local copies, waits for them, and re-layouts  7.24 us (6%)
    all_to_all x1, blocking collectives, fast_shards(): lax.all_to_all(mine, 'elem', 0, 0, tiled=True).reshape(local, all_bands)  18.2 us
    ppermute x13, waiting for transfers between devices, swap(): lax.ppermute(value, axis, [(source, source ^ bit) for source in range(cou...  17.5 us
    all_to_all x1, waiting for transfers between devices, fast_shards(): got = lax.all_to_all(partial, 'elem', 0, 0, tiled=True)  16.2 us
    ppermute x6, starting transfers between devices, from_behind(): return lax.ppermute(value, axis, pairs)  16 us
    ppermute x6, waiting for transfers between devices, from_behind(): return lax.ppermute(value, axis, pairs)  9.04 us
    ppermute x13, starting transfers between devices, swap(): lax.ppermute(value, axis, [(source, source ^ bit) for source in range(cou...  7.29 us
    unnamed x30, local copies, waits for them, and re-layouts  7.24 us
    pallas_call x2, Pallas kernels, fast_shards(): pl.pallas_call(functools.partial(strip_kernel, n, count, strip, offset, l...  5.85 us
  transfers between devices with their start and end apart: 20, of which 9 were waited for; matrix products, arithmetic and copies ran while one was open for 0% of the time, Pallas kernels for 13%

profile of v2, /device:TPU:0, one launch (start us, length us, event | category | flops | bytes accessed | tf_op | source)
XLA Modules:
  0.0 119.3 jit_solution(2965186452734645464)
XLA Ops:
  0.0 1.3 %copy-done.11 = bf16[16,160,160]{2,1,0:T(8,128)(2,1)S(1)} copy-done((bf16[16,160,160]{2,1,0:T(8,128)(2,1)S(1)}, bf16[16,160,160]{2,1,0:T(8,128)(2,1)}, u32[]{:S(2)}) %copy-start.11) | copy-done | bytes 819224
  1.3 1.3 %copy-done.12 = bf16[16,160,160]{2,1,0:T(8,128)(2,1)S(1)} copy-done((bf16[16,160,160]{2,1,0:T(8,128)(2,1)S(1)}, bf16[16,160,160]{2,1,0:T(8,128)(2,1)}, u32[]{:S(2)}) %copy-start.12) | copy-done | bytes 819224
  3.9 2.1 %rows.1 = (bf16[16,160,512]{2,1,0:T(8,128)(2,1)S(1)}, bf16[800,128]{1,0:T(8,128)(2,1)S(1)}, bf16[800,128]{1,0:T(8,128)(2,1)S(1)}) custom-call(s32[1]{0:T(128)} %bitcast.1.me_ref, s32[16]{0:T(128)S(1)} %copy-done.13, s32[16]{0:T(128)S(1)} %copy-done.14, bf16[16,160,160]{2,1,0:T(8,128)(2,1)S(1)} %copy-done.11, bf16[16,160,160]{2,1,0:T(8,128)(2,1)S(1)} %copy-done.12), custom_call_target="tpu_custom_call" | custom-call | flops 11500000 | bytes 1 | tf_op jit(solution)/shard_map/rows/pallas_call | solution.py:360
  6.1 6.0 %collective-permute-start.6 = (bf16[800,128]{1,0:T(8,128)(2,1)S(1)}, bf16[800,128]{1,0:T(8,128)(2,1)S(1)}, u32[]{:S(2)}, u32[]{:S(2)}) collective-permute-start(bf16[800,128]{1,0:T(8,128)(2,1)S(1)} %get-tuple-element.51), channel_id=1, source_target_pairs={{0,28},{4,0},{8,4},{12,8},{16,12},{20,16},{24,20},{28,24},{1,29},{... | collective-permute-start | bytes 614408 | tf_op jit(solution)/shard_map/ppermute | solution.py:29
  13.2 4.8 %collective-permute-start.3 = (bf16[480,256]{1,0:T(8,128)(2,1)S(1)}, bf16[480,256]{1,0:T(8,128)(2,1)S(1)}, u32[]{:S(2)}, u32[]{:S(2)}) collective-permute-start(bf16[480,256]{1,0:T(8,128)(2,1)S(1)} %get-tuple-element.40), channel_id=1, source_target_pairs={{0,28},{4,0},{8,4},{12,8},{16,12},{20,16},{24,20},{28,24},{1,29},{... | collective-permute-start | bytes 737288 | tf_op jit(solution)/shard_map/ppermute | solution.py:29
  18.0 3.4 %interior_first.1 = (bf16[2,320,256]{2,1,0:T(8,128)(2,1)S(1)}, bf16[2,320,256]{2,1,0:T(8,128)(2,1)S(1)}, bf16[2560,256]{1,0:T(8,128)(2,1)S(1)}, bf16[2560,256]{1,0:T(8,128)(2,1)S(1)}) custom-call(bf16[16,160,512]{2,1,0:T(8,128)(2,1)S(1)} %get-tuple-element.38.rows_ref, bf16[2560,256]{1,0:T(8,128)(2,1)S(1)} %get-tuple-element.41.refs_0_), custom_call_target="tpu_custom_call" | custom-call | flops 11500000 | bytes 1 | tf_op jit(solution)/shard_map/interior_first/pallas_call | solution.py:393
  21.4 1.6 %collective-permute-start.10 = (bf16[800,128]{1,0:T(8,128)(2,1)S(1)}, bf16[800,128]{1,0:T(8,128)(2,1)S(1)}, u32[]{:S(2)}, u32[]{:S(2)}) collective-permute-start(bf16[800,128]{1,0:T(8,128)(2,1)S(1)} %collective-permute-done.6.refs_6_.refs_4_), channel_id=1, source_target_pairs={{0,2},{1,3},{2,0},{3,1},{4,6},{5,7},{6,4},{7,5},{8,10},{9,11},{10,... | collective-permute-start | bytes 614408 | tf_op jit(solution)/shard_map/ppermute | solution.py:34
  24.1 1.5 %collective-permute-start.8 = (bf16[800,128]{1,0:T(8,128)(2,1)S(1)}, bf16[800,128]{1,0:T(8,128)(2,1)S(1)}, u32[]{:S(2)}, u32[]{:S(2)}) collective-permute-start(bf16[800,128]{1,0:T(8,128)(2,1)S(1)} %collective-permute-done.4.refs_4_.refs_2_), channel_id=1, source_target_pairs={{0,2},{1,3},{2,0},{3,1},{4,6},{5,7},{6,4},{7,5},{8,10},{9,11},{10,... | collective-permute-start | bytes 614408 | tf_op jit(solution)/shard_map/ppermute | solution.py:34
  25.6 4.0 %interior_rest.1 = (bf16[4,320,256]{2,1,0:T(8,128)(2,1)S(1)}, bf16[4,320,256]{2,1,0:T(8,128)(2,1)S(1)}, bf16[640,256]{1,0:T(8,128)(2,1)S(1)}, f32[1,256]{1,0:T(1,128)S(1)}) custom-call(bf16[16,160,512]{2,1,0:T(8,128)(2,1)S(1)} %get-tuple-element.38.rows_ref, bf16[2560,256]{1,0:T(8,128)(2,1)S(1)} %get-tuple-element.42.refs_0_, ...), custom_call_target="tpu_custom_call" | custom-call | flops 11500000 | bytes 1 | tf_op jit(solution)/shard_map/interior_rest/pallas_call | solution.py:405
  30.3 1.5 %collective-permute-done.8.refs_8_.refs_6_ = bf16[800,128]{1,0:T(8,128)(2,1)S(1)} collective-permute-done((bf16[800,128]{1,0:T(8,128)(2,1)S(1)}, bf16[800,128]{1,0:T(8,128)(2,1)S(1)}, u32[]{:S(2)}, u32[]{:S(2)}) %collective-permute-start.8) | collective-permute-done | bytes 204832 | tf_op jit(solution)/shard_map/ppermute | solution.py:34
  32.4 1.5 %collective-permute-start.12 = (bf16[640,256]{1,0:T(8,128)(2,1)S(1)}, bf16[640,256]{1,0:T(8,128)(2,1)S(1)}, u32[]{:S(2)}, u32[]{:S(2)}) collective-permute-start(bf16[640,256]{1,0:T(8,128)(2,1)S(1)} %get-tuple-element.53.refs_10_), channel_id=1, source_target_pairs={{0,2},{1,3},{2,0},{3,1},{4,6},{5,7},{6,4},{7,5},{8,10},{9,11},{10,... | collective-permute-start | bytes 983048 | tf_op jit(solution)/shard_map/ppermute | solution.py:34
  33.9 1.6 %collective-permute-start = (bf16[480,256]{1,0:T(8,128)(2,1)S(1)}, bf16[480,256]{1,0:T(8,128)(2,1)S(1)}, u32[]{:S(2)}, u32[]{:S(2)}) collective-permute-start(bf16[480,256]{1,0:T(8,128)(2,1)S(1)} %get-tuple-element.36), channel_id=1, source_target_pairs={{0,4},{4,8},{8,12},{12,16},{16,20},{20,24},{24,28},{28,0},{1,5},{5... | collective-permute-start | bytes 737288 | tf_op jit(solution)/shard_map/ppermute | solution.py:29
  35.5 3.6 %collective-permute-start.1 = (bf16[480,256]{1,0:T(8,128)(2,1)S(1)}, bf16[480,256]{1,0:T(8,128)(2,1)S(1)}, u32[]{:S(2)}, u32[]{:S(2)}) collective-permute-start(bf16[480,256]{1,0:T(8,128)(2,1)S(1)} %get-tuple-element.37), channel_id=1, source_target_pairs={{0,28},{4,0},{8,4},{12,8},{16,12},{20,16},{24,20},{28,24},{1,29},{... | collective-permute-start | bytes 737288 | tf_op jit(solution)/shard_map/ppermute | solution.py:29
  39.1 2.7 %strip.2 = (bf16[960,256]{1,0:T(8,128)(2,1)S(1)}, bf16[6,320,256]{2,1,0:T(8,128)(2,1)S(1)}, bf16[6,320,256]{2,1,0:T(8,128)(2,1)S(1)}, f32[1,256]{1,0:T(1,128)S(1)}) custom-call(s32[1]{0:T(128)} %bitcast.1.me_ref, bf16[480,256]{1,0:T(8,128)(2,1)S(1)} %collective-permute-done.2.left_y_ref, bf16[480,256]{1,0:T(8,128)(2,1)S(1)} %collective-permute-done.3.right_y_ref, ...), custom_call_target="tpu_custom_call" | custom-call | flops 3449999872 | bytes 1 | tf_op jit(solution)/shard_map/strip/pallas_call | solution.py:432
  42.3 3.6 %collective-permute-done.left_y_ref = bf16[480,256]{1,0:T(8,128)(2,1)S(1)} collective-permute-done((bf16[480,256]{1,0:T(8,128)(2,1)S(1)}, bf16[480,256]{1,0:T(8,128)(2,1)S(1)}, u32[]{:S(2)}, u32[]{:S(2)}) %collective-permute-start) | collective-permute-done | bytes 245792 | tf_op jit(solution)/shard_map/ppermute | solution.py:29
  45.9 4.2 %collective-permute-done.1.right_y_ref = bf16[480,256]{1,0:T(8,128)(2,1)S(1)} collective-permute-done((bf16[480,256]{1,0:T(8,128)(2,1)S(1)}, bf16[480,256]{1,0:T(8,128)(2,1)S(1)}, u32[]{:S(2)}, u32[]{:S(2)}) %collective-permute-start.1) | collective-permute-done | bytes 245792 | tf_op jit(solution)/shard_map/ppermute | solution.py:29
  50.1 3.2 %strip.3 = (bf16[976,256]{1,0:T(8,128)(2,1)S(1)}, bf16[2576,256]{1,0:T(8,128)(2,1)S(1)}, f32[8,128]{1,0:T(8,128)}, f32[1,256]{1,0:T(1,128)}) custom-call(s32[1]{0:T(128)} %bitcast.1.me_ref, bf16[480,256]{1,0:T(8,128)(2,1)S(1)} %collective-permute-done.left_y_ref, bf16[480,256]{1,0:T(8,128)(2,1)S(1)} %collective-permute-done.1.right_y_ref, ...), custom_call_target="tpu_custom_call" | custom-call | flops 3449999872 | bytes 1 | tf_op jit(solution)/shard_map/strip/pallas_call | solution.py:432
  54.9 13.3 %collective-permute-done.17.refs_7_.refs_6_ = bf16[976,256]{1,0:T(8,128)(2,1)S(1)} collective-permute-done((bf16[976,256]{1,0:T(8,128)(2,1)S(1)}, bf16[976,256]{1,0:T(8,128)(2,1)S(1)}, u32[]{:S(2)}, u32[]{:S(2)}) %collective-permute-start.17) | collective-permute-done | bytes 499744 | tf_op jit(solution)/shard_map/ppermute | solution.py:34
  69.6 1.6 %collective-permute-done.15.refs_4_.refs_3_ = bf16[640,256]{1,0:T(8,128)(2,1)S(1)} collective-permute-done((bf16[640,256]{1,0:T(8,128)(2,1)S(1)}, bf16[640,256]{1,0:T(8,128)(2,1)S(1)}, u32[]{:S(2)}, u32[]{:S(2)}) %collective-permute-start.15) | collective-permute-done | bytes 327712 | tf_op jit(solution)/shard_map/ppermute | solution.py:34
  71.3 1.7 %gram_late.1 = bf16[8,32,1152]{2,1,0:T(8,128)(2,1)} custom-call(bf16[2576,256]{1,0:T(8,128)(2,1)S(1)} %get-tuple-element.62.refs_0_, bf16[2576,256]{1,0:T(8,128)(2,1)S(1)} %collective-permute-done.14.refs_1_, bf16[256,2560]{1,0:T(8,128)(2,1)S(1)} %get-tuple-element.63.refs_2_, bf16[640,256]{1,0:T(8,128)(2,1)S(1)} %collective-permute-done.12.refs_3_.refs_2_, ...), custom_call_target="tpu_custom_call" | custom-call | flops 11500000 | bytes 1 | tf_op jit(solution)/shard_map/gram_late/pallas_call | solution.py:460
  75.3 5.6 %all-to-all-start = ((bf16[8,32,1152]{2,1,0:T(8,128)(2,1)}), bf16[8,32,1152]{2,1,0:T(8,128)(2,1)S(1)}, u32[]{:S(2)}, u32[]{:S(2)}) async-start(bf16[8,32,1152]{2,1,0:T(8,128)(2,1)} %gram_late.1), calls=%async_computation | async-start | bytes 1179648 | tf_op jit(solution)/shard_map/all_to_all | solution.py:474
  80.9 16.2 %all-to-all-done.got_ref = bf16[8,32,1152]{2,1,0:T(8,128)(2,1)S(1)} async-done(((bf16[8,32,1152]{2,1,0:T(8,128)(2,1)}), bf16[8,32,1152]{2,1,0:T(8,128)(2,1)S(1)}, u32[]{:S(2)}, u32[]{:S(2)}) %all-to-all-start) | async-done | bytes 589856 | tf_op jit(solution)/shard_map/all_to_all | solution.py:474
  97.3 18.2 %all_to_all.10 = bf16[8,32,1024]{2,1,0:T(8,128)(2,1)S(1)} all-to-all(bf16[8,32,1024]{2,1,0:T(8,128)(2,1)S(1)} %weights.1), channel_id=1, replica_groups=mesh['elem'=8,'band'=4] {'elem'}, dimensions={0} | all-to-all | bytes 1048576 | tf_op jit(solution)/shard_map/all_to_all | solution.py:485
  116.5 2.8 %rotate.1 = bf16[256,2560]{1,0:T(8,128)(2,1)} custom-call(bf16[256,1024]{1,0:T(8,128)(2,1)S(1)} %bitcast.3, bf16[2576,256]{1,0:T(8,128)(2,1)S(1)} %get-tuple-element.62.refs_0_, bf16[2576,256]{1,0:T(8,128)(2,1)S(1)} %collective-permute-done.14.refs_1_, bf16[640,256]{1,0:T(8,128)(2,1)S(1)} %collective-permute-done.12.refs_3_.refs_2_, ...), custom_call_target="tpu_custom_call" | custom-call | flops 11500000 | bytes 1 | tf_op jit(solution)/shard_map/rotate/pallas_call | solution.py:486
  (57 shorter events, 11.8 us)
Async XLA Ops:
  6.1 15.3 %collective-permute-start.6 = (bf16[800,128]{1,0:T(8,128)(2,1)S(1)}, bf16[800,128]{1,0:T(8,128)(2,1)S(1)}, u32[]{:S(2)}, u32[]{:S(2)}) collective-permute-start(bf16[800,128]{1,0:T(8,128)(2,1)S(1)} %get-tuple-element.51), channel_id=1, source_target_pairs={{0,28},{4,0},{8,4},{12,8},{16,12},{20,16},{24,20},{28,24},{1,29},{... | collective-permute-start | bytes 614408 | tf_op jit(solution)/shard_map/ppermute | solution.py:29
  12.1 11.9 %collective-permute-start.4 = (bf16[800,128]{1,0:T(8,128)(2,1)S(1)}, bf16[800,128]{1,0:T(8,128)(2,1)S(1)}, u32[]{:S(2)}, u32[]{:S(2)}) collective-permute-start(bf16[800,128]{1,0:T(8,128)(2,1)S(1)} %get-tuple-element.49), channel_id=1, source_target_pairs={{0,4},{4,8},{8,12},{12,16},{16,20},{20,24},{24,28},{28,0},{1,5},{5... | collective-permute-start | bytes 614408 | tf_op jit(solution)/shard_map/ppermute | solution.py:29
  13.2 16.5 %collective-permute-start.2 = (bf16[480,256]{1,0:T(8,128)(2,1)S(1)}, bf16[480,256]{1,0:T(8,128)(2,1)S(1)}, u32[]{:S(2)}, u32[]{:S(2)}) collective-permute-start(bf16[480,256]{1,0:T(8,128)(2,1)S(1)} %get-tuple-element.39), channel_id=1, source_target_pairs={{0,4},{4,8},{8,12},{12,16},{16,20},{20,24},{24,28},{28,0},{1,5},{5... | collective-permute-start | bytes 737288 | tf_op jit(solution)/shard_map/ppermute | solution.py:29
  13.2 17.1 %collective-permute-start.3 = (bf16[480,256]{1,0:T(8,128)(2,1)S(1)}, bf16[480,256]{1,0:T(8,128)(2,1)S(1)}, u32[]{:S(2)}, u32[]{:S(2)}) collective-permute-start(bf16[480,256]{1,0:T(8,128)(2,1)S(1)} %get-tuple-element.40), channel_id=1, source_target_pairs={{0,28},{4,0},{8,4},{12,8},{16,12},{20,16},{24,20},{28,24},{1,29},{... | collective-permute-start | bytes 737288 | tf_op jit(solution)/shard_map/ppermute | solution.py:29
  21.4 8.9 %collective-permute-start.10 = (bf16[800,128]{1,0:T(8,128)(2,1)S(1)}, bf16[800,128]{1,0:T(8,128)(2,1)S(1)}, u32[]{:S(2)}, u32[]{:S(2)}) collective-permute-start(bf16[800,128]{1,0:T(8,128)(2,1)S(1)} %collective-permute-done.6.refs_6_.refs_4_), channel_id=1, source_target_pairs={{0,2},{1,3},{2,0},{3,1},{4,6},{5,7},{6,4},{7,5},{8,10},{9,11},{10,... | collective-permute-start | bytes 614408 | tf_op jit(solution)/shard_map/ppermute | solution.py:34
  24.1 7.8 %collective-permute-start.8 = (bf16[800,128]{1,0:T(8,128)(2,1)S(1)}, bf16[800,128]{1,0:T(8,128)(2,1)S(1)}, u32[]{:S(2)}, u32[]{:S(2)}) collective-permute-start(bf16[800,128]{1,0:T(8,128)(2,1)S(1)} %collective-permute-done.4.refs_4_.refs_2_), channel_id=1, source_target_pairs={{0,2},{1,3},{2,0},{3,1},{4,6},{5,7},{6,4},{7,5},{8,10},{9,11},{10,... | collective-permute-start | bytes 614408 | tf_op jit(solution)/shard_map/ppermute | solution.py:34
  29.6 4.3 %collective-permute-start.5 = (bf16[800,128]{1,0:T(8,128)(2,1)S(1)}, bf16[800,128]{1,0:T(8,128)(2,1)S(1)}, u32[]{:S(2)}, u32[]{:S(2)}) collective-permute-start(bf16[800,128]{1,0:T(8,128)(2,1)S(1)} %collective-permute-done.4.refs_4_.refs_2_), channel_id=1, source_target_pairs={{0,1},{1,0},{2,3},{3,2},{4,5},{5,4},{6,7},{7,6},{8,9},{9,8},{10,11... | collective-permute-start | bytes 614408 | tf_op jit(solution)/shard_map/ppermute | solution.py:34
  29.7 5.8 %collective-permute-start.7 = (bf16[800,128]{1,0:T(8,128)(2,1)S(1)}, bf16[800,128]{1,0:T(8,128)(2,1)S(1)}, u32[]{:S(2)}, u32[]{:S(2)}) collective-permute-start(bf16[800,128]{1,0:T(8,128)(2,1)S(1)} %collective-permute-done.6.refs_6_.refs_4_), channel_id=1, source_target_pairs={{0,1},{1,0},{2,3},{3,2},{4,5},{5,4},{6,7},{7,6},{8,9},{9,8},{10,11... | collective-permute-start | bytes 614408 | tf_op jit(solution)/shard_map/ppermute | solution.py:34
  31.9 7.2 %collective-permute-start.9 = (bf16[800,128]{1,0:T(8,128)(2,1)S(1)}, bf16[800,128]{1,0:T(8,128)(2,1)S(1)}, u32[]{:S(2)}, u32[]{:S(2)}) collective-permute-start(bf16[800,128]{1,0:T(8,128)(2,1)S(1)} %collective-permute-done.8.refs_8_.refs_6_), channel_id=1, source_target_pairs={{0,1},{1,0},{2,3},{3,2},{4,5},{5,4},{6,7},{7,6},{8,9},{9,8},{10,11... | collective-permute-start | bytes 614408 | tf_op jit(solution)/shard_map/ppermute | solution.py:34
  31.9 7.2 %collective-permute-start.11 = (bf16[800,128]{1,0:T(8,128)(2,1)S(1)}, bf16[800,128]{1,0:T(8,128)(2,1)S(1)}, u32[]{:S(2)}, u32[]{:S(2)}) collective-permute-start(bf16[800,128]{1,0:T(8,128)(2,1)S(1)} %collective-permute-done.10.refs_10_.refs_8_), channel_id=1, source_target_pairs={{0,1},{1,0},{2,3},{3,2},{4,5},{5,4},{6,7},{7,6},{8,9},{9,8},{10,11... | collective-permute-start | bytes 614408 | tf_op jit(solution)/shard_map/ppermute | solution.py:34
  32.4 9.9 %collective-permute-start.12 = (bf16[640,256]{1,0:T(8,128)(2,1)S(1)}, bf16[640,256]{1,0:T(8,128)(2,1)S(1)}, u32[]{:S(2)}, u32[]{:S(2)}) collective-permute-start(bf16[640,256]{1,0:T(8,128)(2,1)S(1)} %get-tuple-element.53.refs_10_), channel_id=1, source_target_pairs={{0,2},{1,3},{2,0},{3,1},{4,6},{5,7},{6,4},{7,5},{8,10},{9,11},{10,... | collective-permute-start | bytes 983048 | tf_op jit(solution)/shard_map/ppermute | solution.py:34
  33.9 12.0 %collective-permute-start = (bf16[480,256]{1,0:T(8,128)(2,1)S(1)}, bf16[480,256]{1,0:T(8,128)(2,1)S(1)}, u32[]{:S(2)}, u32[]{:S(2)}) collective-permute-start(bf16[480,256]{1,0:T(8,128)(2,1)S(1)} %get-tuple-element.36), channel_id=1, source_target_pairs={{0,4},{4,8},{8,12},{12,16},{16,20},{20,24},{24,28},{28,0},{1,5},{5... | collective-permute-start | bytes 737288 | tf_op jit(solution)/shard_map/ppermute | solution.py:29
  35.5 14.6 %collective-permute-start.1 = (bf16[480,256]{1,0:T(8,128)(2,1)S(1)}, bf16[480,256]{1,0:T(8,128)(2,1)S(1)}, u32[]{:S(2)}, u32[]{:S(2)}) collective-permute-start(bf16[480,256]{1,0:T(8,128)(2,1)S(1)} %get-tuple-element.37), channel_id=1, source_target_pairs={{0,28},{4,0},{8,4},{12,8},{16,12},{20,16},{24,20},{28,24},{1,29},{... | collective-permute-start | bytes 737288 | tf_op jit(solution)/shard_map/ppermute | solution.py:29
  41.7 12.6 %collective-permute-start.13 = (bf16[960,256]{1,0:T(8,128)(2,1)S(1)}, bf16[960,256]{1,0:T(8,128)(2,1)S(1)}, u32[]{:S(2)}, u32[]{:S(2)}) collective-permute-start(bf16[960,256]{1,0:T(8,128)(2,1)S(1)} %get-tuple-element.60.refs_11_), channel_id=1, source_target_pairs={{0,2},{1,3},{2,0},{3,1},{4,6},{5,7},{6,4},{7,5},{8,10},{9,11},{10,... | collective-permute-start | bytes 1474568 | tf_op jit(solution)/shard_map/ppermute | solution.py:34
  54.4 14.3 %collective-permute-start.14 = (bf16[2576,256]{1,0:T(8,128)(2,1)S(1)}, bf16[2576,256]{1,0:T(8,128)(2,1)S(1)}, u32[]{:S(2)}, u32[]{:S(2)}) collective-permute-start(bf16[2576,256]{1,0:T(8,128)(2,1)S(1)} %get-tuple-element.62.refs_0_), channel_id=1, source_target_pairs={{0,1},{1,0},{2,3},{3,2},{4,5},{5,4},{6,7},{7,6},{8,9},{9,8},{10,11... | collective-permute-start | bytes 3956744 | tf_op jit(solution)/shard_map/ppermute | solution.py:34
  54.4 13.8 %collective-permute-start.17 = (bf16[976,256]{1,0:T(8,128)(2,1)S(1)}, bf16[976,256]{1,0:T(8,128)(2,1)S(1)}, u32[]{:S(2)}, u32[]{:S(2)}) collective-permute-start(bf16[976,256]{1,0:T(8,128)(2,1)S(1)} %get-tuple-element.65), channel_id=1, source_target_pairs={{0,2},{1,3},{2,0},{3,1},{4,6},{5,7},{6,4},{7,5},{8,10},{9,11},{10,... | collective-permute-start | bytes 1499144 | tf_op jit(solution)/shard_map/ppermute | solution.py:34
  68.2 3.1 %collective-permute-start.18 = (bf16[976,256]{1,0:T(8,128)(2,1)S(1)}, bf16[976,256]{1,0:T(8,128)(2,1)S(1)}, u32[]{:S(2)}, u32[]{:S(2)}) collective-permute-start(bf16[976,256]{1,0:T(8,128)(2,1)S(1)} %collective-permute-done.17.refs_7_.refs_6_), channel_id=1, source_target_pairs={{0,1},{1,0},{2,3},{3,2},{4,5},{5,4},{6,7},{7,6},{8,9},{9,8},{10,11... | collective-permute-start | bytes 1499144 | tf_op jit(solution)/shard_map/ppermute | solution.py:34
  68.2 3.0 %collective-permute-start.16 = (bf16[960,256]{1,0:T(8,128)(2,1)S(1)}, bf16[960,256]{1,0:T(8,128)(2,1)S(1)}, u32[]{:S(2)}, u32[]{:S(2)}) collective-permute-start(bf16[960,256]{1,0:T(8,128)(2,1)S(1)} %collective-permute-done.13.refs_5_.refs_4_), channel_id=1, source_target_pairs={{0,1},{1,0},{2,3},{3,2},{4,5},{5,4},{6,7},{7,6},{8,9},{9,8},{10,11... | collective-permute-start | bytes 1474568 | tf_op jit(solution)/shard_map/ppermute | solution.py:34
  68.7 2.5 %collective-permute-start.15 = (bf16[640,256]{1,0:T(8,128)(2,1)S(1)}, bf16[640,256]{1,0:T(8,128)(2,1)S(1)}, u32[]{:S(2)}, u32[]{:S(2)}) collective-permute-start(bf16[640,256]{1,0:T(8,128)(2,1)S(1)} %collective-permute-done.12.refs_3_.refs_2_), channel_id=1, source_target_pairs={{0,1},{1,0},{2,3},{3,2},{4,5},{5,4},{6,7},{7,6},{8,9},{9,8},{10,11... | collective-permute-start | bytes 983048 | tf_op jit(solution)/shard_map/ppermute | solution.py:34
  75.3 21.8 %all-to-all-start = ((bf16[8,32,1152]{2,1,0:T(8,128)(2,1)}), bf16[8,32,1152]{2,1,0:T(8,128)(2,1)S(1)}, u32[]{:S(2)}, u32[]{:S(2)}) async-start(bf16[8,32,1152]{2,1,0:T(8,128)(2,1)} %gram_late.1), calls=%async_computation | async-start | bytes 1179648 | tf_op jit(solution)/shard_map/all_to_all | solution.py:474
  97.1 18.5 %copy-start.1 = (bf16[976,256]{1,0:T(8,128)(2,1)S(1)}, bf16[976,256]{1,0:T(8,128)(2,1)}, u32[]{:S(2)}) copy-start(bf16[976,256]{1,0:T(8,128)(2,1)} %copy-done) | copy-start | bytes 1499140
  97.1 18.5 %copy-start.3 = (bf16[976,256]{1,0:T(8,128)(2,1)S(1)}, bf16[976,256]{1,0:T(8,128)(2,1)}, u32[]{:S(2)}) copy-start(bf16[976,256]{1,0:T(8,128)(2,1)} %copy-done.2) | copy-start | bytes 1499140
  97.1 18.5 %copy-start.5 = (bf16[960,256]{1,0:T(8,128)(2,1)S(1)}, bf16[960,256]{1,0:T(8,128)(2,1)}, u32[]{:S(2)}) copy-start(bf16[960,256]{1,0:T(8,128)(2,1)} %copy-done.4) | copy-start | bytes 1474564
  97.1 18.5 %copy-start.7 = (bf16[960,256]{1,0:T(8,128)(2,1)S(1)}, bf16[960,256]{1,0:T(8,128)(2,1)}, u32[]{:S(2)}) copy-start(bf16[960,256]{1,0:T(8,128)(2,1)} %copy-done.6) | copy-start | bytes 1474564
  (11 other events, 35.3 us)

commit v3 on v2

--- a/solution.py
+++ b/solution.py
@@ -18,6 +18,7 @@
 
 LANES = 128
 VMEM = pl.BlockSpec(memory_space=pltpu.VMEM)
+HBM = pl.BlockSpec(memory_space=pltpu.HBM)
 SMEM = pl.BlockSpec(memory_space=pltpu.SMEM)
 BF16 = jnp.bfloat16
 F32 = jnp.float32
@@ -46,7 +47,25 @@
     return pl.CostEstimate(flops=int(microseconds * 1.15e9), bytes_accessed=1, transcendentals=0)
 
 
-def rows_kernel(width, lanes, me_ref, sizes_ref, pattern_ref, diag_ref, couple_ref, rows_ref, first_ref, last_ref):
+def rows_kernel(
+    width, lanes, me_ref, sizes_in, pattern_in, diag_in, couple_in, rows_ref, first_ref, last_ref, *scratch
+):
+    sizes_ref, pattern_ref, diag_ref, couple_ref, scalar_sems, diag_sems, couple_sems = scratch
+    parts = diag_sems.shape[0]
+    each = diag_in.shape[0] // parts
+    scalars = [
+        pltpu.make_async_copy(sizes_in, sizes_ref, scalar_sems.at[0]),
+        pltpu.make_async_copy(pattern_in, pattern_ref, scalar_sems.at[1]),
+    ]
+    blocks = []
+    for part in range(parts):
+        at = pl.ds(part * each, each)
+        blocks.append(pltpu.make_async_copy(couple_in.at[at], couple_ref.at[at], couple_sems.at[part]))
+        blocks.append(pltpu.make_async_copy(diag_in.at[at], diag_ref.at[at], diag_sems.at[part]))
+    for copy in scalars + blocks:
+        copy.start()
+    for copy in scalars:
+        copy.wait()
     n = width
     count = rows_ref.shape[0]
     depth = DEGREE - 1
@@ -55,6 +74,9 @@
     behind = jnp.zeros((n, n), F32)
     ones = jnp.ones((n, wide - 3 * n), F32)
     for e in range(count):
+        if e % each == 0:
+            blocks[2 * (e // each)].wait()
+            blocks[2 * (e // each) + 1].wait()
         couple = couple_ref[e].astype(F32) * pattern_ref[e].astype(F32)
         whole = jnp.concatenate([behind, diag_ref[e].astype(F32), couple, ones], axis=1)
         rows_ref[e] = jnp.where(place < sizes_ref[e], whole, 0.0).astype(BF16)
@@ -65,7 +87,7 @@
         last_ref[e * n : (e + 1) * n, :] = rows_ref[count - depth + e, :, at]
 
 
-def vectors_kernel(width, count, group, sizes_ref, bands_ref, out_ref, *edge_refs):
+def vectors_kernel(width, count, group, sizes_ref, bands_ref, out_ref, first_ref, last_ref):
     n = width
     local = bands_ref.shape[0]
     place = lax.broadcasted_iota(jnp.int32, (n, local), 0)
@@ -74,12 +96,8 @@
         for e in range(begin, begin + group):
             part = turned[(e - begin) * n : (e - begin + 1) * n, :].astype(F32)
             out_ref[e * n : (e + 1) * n, :] = jnp.where(place < sizes_ref[e], part, 0.0).astype(BF16)
-    near = 0
-    for index, strip in enumerate(STRIPS):
-        far = near + strip
-        edge_refs[2 * index][...] = out_ref[near * n : far * n, :]
-        edge_refs[2 * index + 1][...] = out_ref[(count - far) * n : (count - near) * n, :]
-        near = far
+    first_ref[...] = out_ref[: DEGREE * n, :]
+    last_ref[...] = out_ref[(count - DEGREE) * n :, :]
 
 
 def advance(row, window, center, before, first):
@@ -154,12 +172,10 @@
     depth = DEGREE - 1
     me = me_ref[0]
     refs, outs = refs[:-8], refs[-8:]
-    all_ref = outs[1]
     half = len(edge_sizes)
     left_edge = [ref.at[k] for ref, size in zip(refs[:half], edge_sizes) for k in range(size)]
     right_edge = [ref.at[k] for ref, size in zip(refs[half : 2 * half], edge_sizes) for k in range(size)]
     refs = refs[2 * half :]
-    before = refs[4 * pieces :]
     out_ref, left_out_ref, right_out_ref, squares_ref, left_scr, right_scr, halo_left, halo_right = outs
     lanes = refs[0].shape[1]
     for index in range(pieces):
@@ -186,8 +202,9 @@
         keep = halo_right[0, :, 3 * n : 3 * n + 1].astype(F32)
         return jnp.concatenate([(turned * keep).astype(BF16), halo_right[0, :, n : 3 * n]], axis=1)
 
-    left_scr[0, : strip * n, :] = left_y_ref[...]
-    right_scr[0, 2 * n :, :] = right_y_ref[...]
+    near = -offset - strip
+    left_scr[0, : strip * n, :] = left_y_ref[(DEGREE + offset) * n : (DEGREE - near) * n, :]
+    right_scr[0, 2 * n :, :] = right_y_ref[near * n : (near + strip) * n, :]
     for step in range(DEGREE):
         left_scr[step, strip * n :, :] = left_edge[step][...]
         right_scr[step, : 2 * n, :] = right_edge[step][...]
@@ -223,67 +240,74 @@
         place = lax.broadcasted_iota(jnp.int32, (16, squares.shape[1]), 0)
         both = jnp.where(place == 0, high, jnp.where(place == 1, low, 0.0))
         out_ref[2 * strip * n :, :] = both.astype(BF16)
-        begin = 0
-        for ref in (*before, out_ref):
-            all_ref[begin : begin + ref.shape[0], :] = ref[...]
-            begin += ref.shape[0]
-
-
-def gram_kernel(chunks, blocks, shares, early, *refs):
-    outs = refs[-2:] if early else refs[-1:]
-    out_ref = outs[0]
-    half = blocks // 2
+
+
+def gram_kernel(chunks, half, shares, early, *refs):
+    if early:
+        refs, (out_ref, tails_ref, turned_ref) = refs[:-3], refs[-3:]
+    else:
+        early_ref, turned_ref, tails_ref, *refs, out_ref = refs
+    grid = [refs[c * half : (c + 1) * half] for c in range(chunks)]
     rows = out_ref.shape[1]
-    lower = refs[:half]
-    local = lower[0].shape[1]
-    length = lower[0].shape[0] - 16
-    totals = [None] * half
+    local = grid[0][0].shape[1]
+    sizes = [grid[c][0].shape[0] - (16 if c == chunks - 1 else 0) for c in range(chunks)]
+    places = [slice(sum(sizes[:c]), sum(sizes[: c + 1])) for c in range(chunks)]
+    tails = [grid[-1][r][sizes[-1] :, :] for r in range(half)]
     if early:
-        turned_ref = outs[1]
-        turned_ref[...] = jnp.transpose(lower[0][:length, :])
+        for c in range(chunks):
+            turned_ref[:, places[c]] = jnp.transpose(grid[c][0][: sizes[c], :])
         for r in range(half):
-            totals[r] = jnp.dot(turned_ref[...], lower[r][:length, :], preferred_element_type=F32)
-    else:
-        turned_ref = refs[half]
-        begin = 0
-        upper = [refs[half + 1 + c * half : half + 1 + (c + 1) * half] for c in range(chunks)]
+            tails_ref[r] = tails[r]
+    for r in range(half):
+        total = None
         for c in range(chunks):
-            size = upper[c][0].shape[0] - (16 if c == chunks - 1 else 0)
-            for r in range(half):
-                term = jnp.dot(
-                    turned_ref[:, begin : begin + size], upper[c][r][:size, :], preferred_element_type=F32
-                )
-                totals[r] = term if c == 0 else totals[r] + term
-            begin += size
-    base = 0 if early else half
-    for r in range(half):
-        at = (base + r) * local
-        out_ref[:, :, at : at + local] = totals[r].astype(BF16).reshape(shares, rows, local)
+            term = jnp.dot(turned_ref[:, places[c]], grid[c][r][: sizes[c], :], preferred_element_type=F32)
+            total = term if c == 0 else total + term
+        at = (r if early else half + r) * local
+        out_ref[:, :, at : at + local] = total.astype(BF16).reshape(shares, rows, local)
     if early:
         return
-    out_ref[:, :, : half * local] = refs[-2][...]
+    out_ref[:, :, : half * local] = early_ref[...]
     place = lax.broadcasted_iota(jnp.int32, (rows, LANES), 0)
     parts = local // LANES
     extra = jnp.zeros((rows, LANES), F32)
-    for r in range(blocks):
-        ref = lower[r] if r < half else upper[-1][r - half]
-        both = ref[ref.shape[0] - 16 :, :].astype(F32)
+    for r in range(2 * half):
+        both = (tails_ref[r] if r < half else tails[r - half]).astype(F32)
         for p in range(parts):
             for part in range(2):
                 line = both[part : part + 1, p * LANES : (p + 1) * LANES]
-                extra = jnp.where(place == part * blocks * parts + r * parts + p, line, extra)
+                extra = jnp.where(place == part * 2 * half * parts + r * parts + p, line, extra)
     for share in range(shares):
-        out_ref[share, :, blocks * local :] = extra.astype(BF16)
-
-
-def weights_kernel(total_columns, blocks, me_ref, got_ref, out_ref):
+        out_ref[share, :, 2 * half * local :] = extra.astype(BF16)
+
+
+def halves(squares, rows):
+    high = squares.astype(BF16).astype(F32)
+    spare = jnp.zeros((rows - 2 * squares.shape[0], LANES), F32)
+    return jnp.concatenate([high, squares - high, spare])
+
+
+def sums_kernel(got_ref, mine_ref, send_ref):
     shares, rows, wide = got_ref.shape
     bands = wide - LANES
-    local = bands // blocks
     parts = bands // LANES
     total = got_ref[0].astype(F32)
     for share in range(1, shares):
         total = total + got_ref[share].astype(F32)
+    tail = halves(total[:parts, bands:] + total[parts : 2 * parts, bands:], rows)
+    mine_ref[:, :bands] = total[:, :bands]
+    mine_ref[:, bands:] = tail
+    send_ref[:, :bands] = total[:, :bands].astype(BF16)
+    send_ref[:, bands:] = tail.astype(BF16)
+
+
+def weights_kernel(total_columns, blocks, me_ref, mine_ref, other_ref, out_ref):
+    rows, wide = mine_ref.shape
+    shares = out_ref.shape[0]
+    bands = wide - LANES
+    local = bands // blocks
+    parts = bands // LANES
+    total = mine_ref[...] + other_ref[...].astype(F32)
     tail = total[:, bands:]
     squares = tail[:parts, :] + tail[parts : 2 * parts, :]
     scales = lax.rsqrt(squares + epsilon_norm)
@@ -311,28 +335,20 @@
 
 def rotate_kernel(chunks, blocks, spans, weights_ref, *refs):
     out_ref = refs[-1]
-    half = blocks // 2
-    lower = refs[:half]
-    upper = [refs[half + c * half : half + (c + 1) * half] for c in range(chunks)]
-    local = lower[0].shape[1]
-    start = 0
+    grid = [refs[c * blocks : (c + 1) * blocks] for c in range(chunks)]
+    local = grid[0][0].shape[1]
     for c in range(chunks):
         for begin, size, column in spans[c]:
             total = None
             for r in range(blocks):
-                if r < half:
-                    part = lower[r][start + begin : start + begin + size, :]
-                else:
-                    part = upper[c][r - half][begin : begin + size, :]
                 term = lax.dot_general(
                     weights_ref[:, r * local : (r + 1) * local],
-                    part,
+                    grid[c][r][begin : begin + size, :],
                     (((1,), (1,)), ((), ())),
                     preferred_element_type=F32,
                 )
                 total = term if total is None else total + term
             out_ref[:, column : column + size] = total.astype(BF16)
-        start += sum(size for _, size, _ in spans[c])
 
 
 def lower_blocks(own):
@@ -361,27 +377,31 @@
         functools.partial(rows_kernel, n, lanes),
         out_shape=[jax.ShapeDtypeStruct((count, n, wide), BF16)]
         + [jax.ShapeDtypeStruct((depth * n, lanes), BF16)] * 2,
-        in_specs=[SMEM] * 3 + [VMEM] * 2,
+        in_specs=[SMEM] + [HBM] * 4,
         out_specs=[VMEM] * 3,
-        compiler_params=params(16),
+        scratch_shapes=[pltpu.SMEM((count,), jnp.int32)] * 2
+        + [pltpu.VMEM((count, n, n), BF16)] * 2
+        + [pltpu.SemaphoreType.DMA((2,))]
+        + [pltpu.SemaphoreType.DMA((math.gcd(count, 4),))] * 2,
+        compiler_params=params(60),
         cost_estimate=about(0.01),
         name="rows",
     )(band_me, basis_sizes, coupling_pattern, h_diag, h_couple)
     left_rows = from_behind(last_rows, "elem", 1)
     right_rows = from_behind(first_rows, "elem", -1)
 
-    start, *ends = pl.pallas_call(
+    halo = jax.ShapeDtypeStruct((DEGREE * n, local), BF16)
+    start, first_y, last_y = pl.pallas_call(
         functools.partial(vectors_kernel, n, count, math.lcm(n, LANES) // n),
-        out_shape=[jax.ShapeDtypeStruct((count * n, local), BF16)]
-        + [jax.ShapeDtypeStruct((strip * n, local), BF16) for strip in STRIPS for _ in range(2)],
+        out_shape=[jax.ShapeDtypeStruct((count * n, local), BF16), halo, halo],
         in_specs=[SMEM, VMEM],
-        out_specs=[VMEM] * (1 + 2 * len(STRIPS)),
+        out_specs=[VMEM] * 3,
         compiler_params=params(16),
         cost_estimate=about(0.01),
         name="vectors",
     )(basis_sizes, bands)
-    left_y = [from_behind(ends[2 * index + 1], "elem", 1) for index in range(len(STRIPS))]
-    right_y = [from_behind(ends[2 * index], "elem", -1) for index in range(len(STRIPS))]
+    left_y = from_behind(last_y, "elem", 1)
+    right_y = from_behind(first_y, "elem", -1)
 
     inner = (count - 2 * DEGREE) * n
     whole = jax.ShapeDtypeStruct((count * n, local), BF16)
@@ -414,7 +434,7 @@
     )(rows, older, newer)
     left_edge = [left_edge, left_more]
     right_edge = [right_edge, right_more]
-    across_rows = [after(side, chunk, left_y[0], right_y[0]) for side in across_rows]
+    across_rows = [after(side, chunk) for side in across_rows]
     both = [block for side in (*own_rows, *across_rows) for block in lower_blocks(side)]
     chunks, across = [chunk], [swap(chunk, "band", half)]
     spans = [[(0, inner, DEGREE * n)]]
@@ -427,38 +447,37 @@
         size = 2 * strip * n + (16 if last else 0)
         sizes = [edge.shape[0] for edge in left_edge]
         shape = jax.ShapeDtypeStruct((size, local), BF16)
-        full = jax.ShapeDtypeStruct((count * n + 16, local), BF16)
-        before = chunks if last else []
+        spare = [jax.ShapeDtypeStruct((8, LANES), F32)] * 2
         chunk, *others, squares = pl.pallas_call(
             functools.partial(strip_kernel, n, count, strip, offset, last, sizes, half),
-            out_shape=[shape, *([full, jax.ShapeDtypeStruct((8, LANES), F32)] if last else edges(DEGREE)), squares_shape],
-            in_specs=[SMEM] + [VMEM] * (4 + 2 * len(sizes) + 4 * half + len(before)),
+            out_shape=[shape, *(spare if last else edges(DEGREE)), squares_shape],
+            in_specs=[SMEM] + [VMEM] * (4 + 2 * len(sizes) + 4 * half),
             out_specs=[VMEM] * 4,
             scratch_shapes=[pltpu.VMEM((DEGREE + 1, (strip + 2) * n, local), BF16)] * 2
             + [pltpu.VMEM((depth, n, wide), BF16)] * 2,
             compiler_params=params(32),
             cost_estimate=about(3),
             name="strip",
-        )(band_me, left_y[index], right_y[index], rows, squares, *left_edge, *right_edge, *both, *before)
+        )(band_me, left_y, right_y, rows, squares, *left_edge, *right_edge, *both)
         left_edge, right_edge = [others[0]], [others[1]]
-        if last:
-            own = others[0]
-            chunk = after(chunk, across[index])
         chunks.append(chunk)
         across.append(swap(chunk, "band", half))
         first = offset + DEGREE
         spans.append([(0, strip * n, first * n), (strip * n, strip * n, (count - first - strip) * n)])
 
-    slice_rows = local // elem_size
+    group = elem_size // 2
+    groups = [list(range(begin, begin + group)) for begin in (0, group)]
+    slice_rows = local // group
     all_bands = local * band_size
 
-    def gram(early, blocks):
+    def gram(early, *blocks):
         wide = all_bands // 2 if early else all_bands + LANES
-        shapes = [jax.ShapeDtypeStruct((elem_size, slice_rows, wide), BF16)]
+        shapes = [jax.ShapeDtypeStruct((group, slice_rows, wide), BF16)]
         if early:
+            shapes.append(jax.ShapeDtypeStruct((half, 16, local), BF16))
             shapes.append(jax.ShapeDtypeStruct((local, count * n), BF16))
         return pl.pallas_call(
-            functools.partial(gram_kernel, len(chunks), band_size, elem_size, early),
+            functools.partial(gram_kernel, len(chunks), half, group, early),
             out_shape=shapes,
             in_specs=[VMEM] * len(blocks),
             out_specs=[VMEM] * len(shapes),
@@ -467,22 +486,34 @@
             name="gram_early" if early else "gram_late",
         )(*blocks)
 
-    lower = lower_blocks(after(own, across[-2]))
-    early, turned = gram(True, lower)
-    upper = [block for chunk in across for block in lower_blocks(chunk)]
-    (partial,) = gram(False, [*lower, turned, *upper, early])
-    got = lax.all_to_all(partial, "elem", 0, 0, tiled=True)
-    flat = [*lower, *upper]
-    mine = pl.pallas_call(
+    lower = [lower_blocks(chunk) for chunk in chunks]
+    early, tails, turned = gram(True, *[block for blocks in lower for block in blocks])
+    upper = [lower_blocks(chunk) for chunk in across[:-1]]
+    upper.append(lower_blocks(after(across[-1], upper[-1][-1], early)))
+    (late,) = gram(False, early, turned, tails, *[block for blocks in upper for block in blocks])
+    got = lax.all_to_all(late, "elem", 0, 0, tiled=True, axis_index_groups=groups)
+    sums = jax.ShapeDtypeStruct((slice_rows, all_bands + LANES), F32)
+    mine, send = pl.pallas_call(
+        sums_kernel,
+        out_shape=[sums, jax.ShapeDtypeStruct(sums.shape, BF16)],
+        in_specs=[VMEM],
+        out_specs=[VMEM] * 2,
+        compiler_params=params(8),
+        cost_estimate=about(0.01),
+        name="sums",
+    )(got)
+    other = from_behind(send, "elem", group)
+    weights = pl.pallas_call(
         functools.partial(weights_kernel, total_columns, band_size),
-        out_shape=jax.ShapeDtypeStruct((elem_size, slice_rows, all_bands), BF16),
-        in_specs=[SMEM, VMEM],
+        out_shape=jax.ShapeDtypeStruct((group, slice_rows, all_bands), BF16),
+        in_specs=[SMEM, VMEM, VMEM],
         out_specs=VMEM,
         compiler_params=params(8),
         cost_estimate=about(0.01),
         name="weights",
-    )(elem_me, got)
-    weights = lax.all_to_all(mine, "elem", 0, 0, tiled=True).reshape(local, all_bands)
+    )(elem_me % group, mine, other)
+    flat = [block for low, high in zip(lower, upper) for block in (*low, *high)]
+    weights = lax.all_to_all(weights, "elem", 0, 0, tiled=True, axis_index_groups=groups).reshape(local, all_bands)
     return pl.pallas_call(
         functools.partial(rotate_kernel, len(chunks), band_size, spans),
         out_shape=jax.ShapeDtypeStruct((local, count * n), BF16),
@@ -562,6 +593,7 @@
         band_size & (band_size - 1) == 0
         and wide % (band_size * LANES) == 0
         and local % LANES == 0
+        and elem_size % 2 == 0
         and local % elem_size == 0
         and rows % 16 == 0
         and rows * LANES >= 2 * local * band_size

time: 120 us -> 111 us (0.925)
  waiting for transfers between devices: 42.8 us -> 31.7 us
  blocking collectives: 18.2 us -> 26.1 us
  starting transfers between devices: 28.9 us -> 23.7 us
  Pallas kernels: 22.1 us -> 26.1 us
  local copies, waits for them, and re-layouts: 7.24 us -> 3.45 us
    all_to_all x1 -> x0, waiting for transfers between devices: 16.2 us -> none  [fast_shards(): got = lax.all_to_all(partial, 'elem', 0, 0, tiled=True)]
    all_to_all x1 -> x2, blocking collectives: 18.2 us -> 26.1 us  [the longest x1 15.6 us: fast_shards(): lax.all_to_all(late, 'elem', 0, 0, tiled=True, axis_index_groups=groups)]
    all_to_all x1 -> x0, starting transfers between devices: 5.56 us -> none  [fast_shards(): got = lax.all_to_all(partial, 'elem', 0, 0, tiled=True)]
    ppermute x6 -> x5, waiting for transfers between devices: 9.04 us -> 13.3 us  [from_behind(): return lax.ppermute(value, axis, pairs)]
    unnamed x30 -> x32, local copies, waits for them, and re-layouts: 7.24 us -> 3.45 us
    ppermute x13 -> x15, starting transfers between devices: 7.29 us -> 10.1 us  [swap(): lax.ppermute(value, axis, [(source, source ^ bit) for source in range(cou...]
    pallas_call x1, Pallas kernels: 2.13 us -> 4.74 us  [fast_shards(): pl.pallas_call(functools.partial(rows_kernel, n, lanes), out_shape=[jax.S...]
    ppermute x6 -> x5, starting transfers between devices: 16 us -> 13.6 us  [from_behind(): return lax.ppermute(value, axis, pairs)]
  transfers between devices with their start and end apart: 20 -> 20, of which waited for: 9 -> 10; matrix products, arithmetic and copies ran while one was open for 0% -> 0% of each run, Pallas kernels for 13% -> 14%
where the time goes in v3:
time: 111 us
  waiting for transfers between devices  31.7 us (29%)
  Pallas kernels  26.1 us (24%)
  blocking collectives  26.1 us (24%)
  starting transfers between devices  23.7 us (21%)
  local copies, waits for them, and re-layouts  3.45 us (3%)
    ppermute x15, waiting for transfers between devices, swap(): lax.ppermute(value, axis, [(source, source ^ bit) for source in range(cou...  18.4 us
    all_to_all x1, blocking collectives, fast_shards(): lax.all_to_all(late, 'elem', 0, 0, tiled=True, axis_index_groups=groups)  15.6 us
    ppermute x5, starting transfers between devices, from_behind(): return lax.ppermute(value, axis, pairs)  13.6 us
    ppermute x5, waiting for transfers between devices, from_behind(): return lax.ppermute(value, axis, pairs)  13.3 us
    all_to_all x1, blocking collectives, fast_shards(): lax.all_to_all(weights, 'elem', 0, 0, tiled=True, axis_index_groups=groups)  10.5 us
    ppermute x15, starting transfers between devices, swap(): lax.ppermute(value, axis, [(source, source ^ bit) for source in range(cou...  10.1 us
    pallas_call x2, Pallas kernels, fast_shards(): pl.pallas_call(functools.partial(strip_kernel, n, count, strip, offset, l...  6.1 us
    pallas_call x1, Pallas kernels, fast_shards(): pl.pallas_call(functools.partial(rows_kernel, n, lanes), out_shape=[jax.S...  4.74 us
  transfers between devices with their start and end apart: 20, of which 10 were waited for; matrix products, arithmetic and copies ran while one was open for 0% of the time, Pallas kernels for 14%

profile of v3, /device:TPU:0, one launch (start us, length us, event | category | flops | bytes accessed | tf_op | source)
XLA Modules:
  0.0 111.2 jit_solution(2499443184289662573)
XLA Ops:
  0.0 4.7 %rows.1 = (bf16[16,160,512]{2,1,0:T(8,128)(2,1)}, bf16[800,128]{1,0:T(8,128)(2,1)}, bf16[800,128]{1,0:T(8,128)(2,1)}) custom-call(s32[1]{0:T(128)} %bitcast.1.me_ref, s32[16]{0:T(128)} %sizes_ref.1, s32[16]{0:T(128)} %pattern_in.1, bf16[16,160,160]{2,1,0:T(8,128)(2,1)} %diag_in.1, bf16[16,160,160]{2,1,0:T(8,128)(2,1)} %couple_in.1), custom_call_target="tpu_custom_call" | custom-call | flops 11500000 | bytes 1 | tf_op jit(solution)/shard_map/rows/pallas_call | solution.py:376
  4.8 6.0 %collective-permute-start.5 = (bf16[800,128]{1,0:T(8,128)(2,1)}, bf16[800,128]{1,0:T(8,128)(2,1)S(1)}, u32[]{:S(2)}, u32[]{:S(2)}) collective-permute-start(bf16[800,128]{1,0:T(8,128)(2,1)} %get-tuple-element.49), channel_id=1, source_target_pairs={{0,28},{4,0},{8,4},{12,8},{16,12},{20,16},{24,20},{28,24},{1,29},{... | collective-permute-start | bytes 614408 | tf_op jit(solution)/shard_map/ppermute | solution.py:30
  11.9 4.9 %collective-permute-start.2 = (bf16[960,256]{1,0:T(8,128)(2,1)S(1)}, bf16[960,256]{1,0:T(8,128)(2,1)S(1)}, u32[]{:S(2)}, u32[]{:S(2)}) collective-permute-start(bf16[960,256]{1,0:T(8,128)(2,1)S(1)} %get-tuple-element.41), channel_id=1, source_target_pairs={{0,28},{4,0},{8,4},{12,8},{16,12},{20,16},{24,20},{28,24},{1,29},{... | collective-permute-start | bytes 1474568 | tf_op jit(solution)/shard_map/ppermute | solution.py:30
  16.8 1.7 %copy-done = bf16[16,160,512]{2,1,0:T(8,128)(2,1)S(1)} copy-done((bf16[16,160,512]{2,1,0:T(8,128)(2,1)S(1)}, bf16[16,160,512]{2,1,0:T(8,128)(2,1)}, u32[]{:S(2)}) %copy-start) | copy-done | bytes 2621464
  18.6 3.4 %interior_first.1 = (bf16[2,320,256]{2,1,0:T(8,128)(2,1)S(1)}, bf16[2,320,256]{2,1,0:T(8,128)(2,1)S(1)}, bf16[2560,256]{1,0:T(8,128)(2,1)S(1)}, bf16[2560,256]{1,0:T(8,128)(2,1)S(1)}) custom-call(bf16[16,160,512]{2,1,0:T(8,128)(2,1)S(1)} %copy-done, bf16[2560,256]{1,0:T(8,128)(2,1)S(1)} %get-tuple-element.36.refs_0_), custom_call_target="tpu_custom_call" | custom-call | flops 11500000 | bytes 1 | tf_op jit(solution)/shard_map/interior_first/pallas_call | solution.py:413
  22.0 1.6 %collective-permute-start.9 = (bf16[800,128]{1,0:T(8,128)(2,1)S(1)}, bf16[800,128]{1,0:T(8,128)(2,1)S(1)}, u32[]{:S(2)}, u32[]{:S(2)}) collective-permute-start(bf16[800,128]{1,0:T(8,128)(2,1)S(1)} %collective-permute-done.5.refs_6_.refs_4_), channel_id=1, source_target_pairs={{0,2},{1,3},{2,0},{3,1},{4,6},{5,7},{6,4},{7,5},{8,10},{9,11},{10,... | collective-permute-start | bytes 614408 | tf_op jit(solution)/shard_map/ppermute | solution.py:35
  23.6 4.7 %collective-permute-done.3.refs_4_.refs_2_ = bf16[800,128]{1,0:T(8,128)(2,1)S(1)} collective-permute-done((bf16[800,128]{1,0:T(8,128)(2,1)}, bf16[800,128]{1,0:T(8,128)(2,1)S(1)}, u32[]{:S(2)}, u32[]{:S(2)}) %collective-permute-start.3) | collective-permute-done | bytes 204832 | tf_op jit(solution)/shard_map/ppermute | solution.py:30
  28.3 1.5 %collective-permute-start.7 = (bf16[800,128]{1,0:T(8,128)(2,1)S(1)}, bf16[800,128]{1,0:T(8,128)(2,1)S(1)}, u32[]{:S(2)}, u32[]{:S(2)}) collective-permute-start(bf16[800,128]{1,0:T(8,128)(2,1)S(1)} %collective-permute-done.3.refs_4_.refs_2_), channel_id=1, source_target_pairs={{0,2},{1,3},{2,0},{3,1},{4,6},{5,7},{6,4},{7,5},{8,10},{9,11},{10,... | collective-permute-start | bytes 614408 | tf_op jit(solution)/shard_map/ppermute | solution.py:35
  29.8 4.0 %interior_rest.1 = (bf16[4,320,256]{2,1,0:T(8,128)(2,1)S(1)}, bf16[4,320,256]{2,1,0:T(8,128)(2,1)S(1)}, bf16[640,256]{1,0:T(8,128)(2,1)S(1)}, f32[1,256]{1,0:T(1,128)S(1)}) custom-call(bf16[16,160,512]{2,1,0:T(8,128)(2,1)S(1)} %copy-done, bf16[2560,256]{1,0:T(8,128)(2,1)S(1)} %get-tuple-element.37.refs_0_, bf16[2560,256]{1,0:T(8,128)(2,1)S(1)} %get-tuple-element.38.refs_1_), custom_call_target="tpu_custom_call" | custom-call | flops 11500000 | bytes 1 | tf_op jit(solution)/shard_map/interior_rest/pallas_call | solution.py:425
  35.7 1.5 %collective-permute-start.12 = (bf16[640,256]{1,0:T(8,128)(2,1)S(1)}, bf16[640,256]{1,0:T(8,128)(2,1)S(1)}, u32[]{:S(2)}, u32[]{:S(2)}) collective-permute-start(bf16[640,256]{1,0:T(8,128)(2,1)S(1)} %get-tuple-element.39.refs_0_), channel_id=1, source_target_pairs={{0,2},{1,3},{2,0},{3,1},{4,6},{5,7},{6,4},{7,5},{8,10},{9,11},{10,... | collective-permute-start | bytes 983048 | tf_op jit(solution)/shard_map/ppermute | solution.py:35
  39.7 2.7 %strip.2 = (bf16[960,256]{1,0:T(8,128)(2,1)S(1)}, bf16[6,320,256]{2,1,0:T(8,128)(2,1)S(1)}, bf16[6,320,256]{2,1,0:T(8,128)(2,1)S(1)}, f32[1,256]{1,0:T(1,128)S(1)}) custom-call(s32[1]{0:T(128)} %bitcast.1.me_ref, bf16[960,256]{1,0:T(8,128)(2,1)S(1)} %collective-permute-done.1.left_y_ref, bf16[960,256]{1,0:T(8,128)(2,1)S(1)} %collective-permute-done.2.right_y_ref, ...), custom_call_target="tpu_custom_call" | custom-call | flops 3449999872 | bytes 1 | tf_op jit(solution)/shard_map/strip/pallas_call | solution.py:451
  42.5 1.6 %collective-permute-start.15 = (bf16[960,256]{1,0:T(8,128)(2,1)S(1)}, bf16[960,256]{1,0:T(8,128)(2,1)S(1)}, u32[]{:S(2)}, u32[]{:S(2)}) collective-permute-start(bf16[960,256]{1,0:T(8,128)(2,1)S(1)} %get-tuple-element.53.refs_2_.refs_4_), channel_id=1, source_target_pairs={{0,2},{1,3},{2,0},{3,1},{4,6},{5,7},{6,4},{7,5},{8,10},{9,11},{10,... | collective-permute-start | bytes 1474568 | tf_op jit(solution)/shard_map/ppermute | solution.py:35
  44.1 2.2 %collective-permute-done.12.refs_3_.refs_2_ = bf16[640,256]{1,0:T(8,128)(2,1)S(1)} collective-permute-done((bf16[640,256]{1,0:T(8,128)(2,1)S(1)}, bf16[640,256]{1,0:T(8,128)(2,1)S(1)}, u32[]{:S(2)}, u32[]{:S(2)}) %collective-permute-start.12) | collective-permute-done | bytes 327712 | tf_op jit(solution)/shard_map/ppermute | solution.py:35
  46.3 3.4 %strip.3 = (bf16[976,256]{1,0:T(8,128)(2,1)S(1)}, f32[8,128]{1,0:T(8,128)}, f32[8,128]{1,0:T(8,128)}, f32[1,256]{1,0:T(1,128)}) custom-call(s32[1]{0:T(128)} %bitcast.1.me_ref, bf16[960,256]{1,0:T(8,128)(2,1)S(1)} %collective-permute-done.1.left_y_ref, bf16[960,256]{1,0:T(8,128)(2,1)S(1)} %collective-permute-done.2.right_y_ref, ...), custom_call_target="tpu_custom_call" | custom-call | flops 3449999872 | bytes 1 | tf_op jit(solution)/shard_map/strip/pallas_call | solution.py:451
  49.6 1.5 %collective-permute-start.17 = (bf16[976,256]{1,0:T(8,128)(2,1)S(1)}, bf16[976,256]{1,0:T(8,128)(2,1)S(1)}, u32[]{:S(2)}, u32[]{:S(2)}) collective-permute-start(bf16[976,256]{1,0:T(8,128)(2,1)S(1)} %get-tuple-element.58.refs_4_.refs_8_), channel_id=1, source_target_pairs={{0,2},{1,3},{2,0},{3,1},{4,6},{5,7},{6,4},{7,5},{8,10},{9,11},{10,... | collective-permute-start | bytes 1499144 | tf_op jit(solution)/shard_map/ppermute | solution.py:35
  51.4 5.4 %collective-permute-done.15.refs_5_.refs_6_ = bf16[960,256]{1,0:T(8,128)(2,1)S(1)} collective-permute-done((bf16[960,256]{1,0:T(8,128)(2,1)S(1)}, bf16[960,256]{1,0:T(8,128)(2,1)S(1)}, u32[]{:S(2)}, u32[]{:S(2)}) %collective-permute-start.15) | collective-permute-done | bytes 491552 | tf_op jit(solution)/shard_map/ppermute | solution.py:35
  57.3 1.8 %collective-permute-done.refs_1_ = bf16[640,256]{1,0:T(8,128)(2,1)S(1)} collective-permute-done((bf16[640,256]{1,0:T(8,128)(2,1)S(1)}, bf16[640,256]{1,0:T(8,128)(2,1)S(1)}, u32[]{:S(2)}, u32[]{:S(2)}) %collective-permute-start) | collective-permute-done | bytes 327712 | tf_op jit(solution)/shard_map/ppermute | solution.py:35
  60.5 6.3 %collective-permute-done.17.refs_7_.refs_10_ = bf16[976,256]{1,0:T(8,128)(2,1)S(1)} collective-permute-done((bf16[976,256]{1,0:T(8,128)(2,1)S(1)}, bf16[976,256]{1,0:T(8,128)(2,1)S(1)}, u32[]{:S(2)}, u32[]{:S(2)}) %collective-permute-start.17) | collective-permute-done | bytes 499744 | tf_op jit(solution)/shard_map/ppermute | solution.py:35
  67.2 1.8 %collective-permute-done.14.refs_4_.refs_3_ = bf16[640,256]{1,0:T(8,128)(2,1)S(1)} collective-permute-done((bf16[640,256]{1,0:T(8,128)(2,1)S(1)}, bf16[640,256]{1,0:T(8,128)(2,1)S(1)}, u32[]{:S(2)}, u32[]{:S(2)}) %collective-permute-start.14) | collective-permute-done | bytes 327712 | tf_op jit(solution)/shard_map/ppermute | solution.py:35
  70.0 15.6 %all_to_all.10.got_ref = bf16[4,64,1152]{2,1,0:T(8,128)(2,1)S(1)} all-to-all(bf16[4,64,1152]{2,1,0:T(8,128)(2,1)S(1)} %gram_late.1), channel_id=1, replica_groups={{0,4,8,12},{16,20,24,28},{1,5,9,13},{17,21,25,29},{2,6,10,14},{18,22,26..., dimensions={0} | all-to-all | bytes 1179648 | tf_op jit(solution)/shard_map/all_to_all | solution.py:494
  87.1 2.6 %collective-permute-start.19 = (bf16[64,1152]{1,0:T(8,128)(2,1)}, bf16[64,1152]{1,0:T(8,128)(2,1)}, u32[]{:S(2)}, u32[]{:S(2)}) collective-permute-start(bf16[64,1152]{1,0:T(8,128)(2,1)} %get-tuple-element.64), channel_id=1, source_target_pairs={{0,16},{4,20},{8,24},{12,28},{16,0},{20,4},{24,8},{28,12},{1,17},{... | collective-permute-start | bytes 442376 | tf_op jit(solution)/shard_map/ppermute | solution.py:30
  89.7 6.1 %collective-permute-done.19.other_ref = bf16[64,1152]{1,0:T(8,128)(2,1)} collective-permute-done((bf16[64,1152]{1,0:T(8,128)(2,1)}, bf16[64,1152]{1,0:T(8,128)(2,1)}, u32[]{:S(2)}, u32[]{:S(2)}) %collective-permute-start.19) | collective-permute-done | bytes 147488 | tf_op jit(solution)/shard_map/ppermute | solution.py:30
  97.8 10.5 %all_to_all.11 = bf16[4,64,1024]{2,1,0:T(8,128)(2,1)S(1)} all-to-all(bf16[4,64,1024]{2,1,0:T(8,128)(2,1)S(1)} %weights.1), channel_id=1, replica_groups={{0,4,8,12},{16,20,24,28},{1,5,9,13},{17,21,25,29},{2,6,10,14},{18,22,26..., dimensions={0} | all-to-all | bytes 1048576 | tf_op jit(solution)/shard_map/all_to_all | solution.py:516
  108.4 2.8 %rotate.1 = bf16[256,2560]{1,0:T(8,128)(2,1)} custom-call(bf16[256,1024]{1,0:T(8,128)(2,1)S(1)} %bitcast.3, bf16[640,256]{1,0:T(8,128)(2,1)S(1)} %copy-done.9, bf16[640,256]{1,0:T(8,128)(2,1)S(1)} %copy-done.11, bf16[640,256]{1,0:T(8,128)(2,1)S(1)} %copy-done.5, bf16[640,256]{1,0:T(8,128)(2,1)S(1)} %copy-done.7, ...), custom_call_target="tpu_custom_call" | custom-call | flops 11500000 | bytes 1 | tf_op jit(solution)/shard_map/rotate/pallas_call | solution.py:517
  (61 shorter events, 12.4 us)
Async XLA Ops:
  4.8 17.3 %collective-permute-start.5 = (bf16[800,128]{1,0:T(8,128)(2,1)}, bf16[800,128]{1,0:T(8,128)(2,1)S(1)}, u32[]{:S(2)}, u32[]{:S(2)}) collective-permute-start(bf16[800,128]{1,0:T(8,128)(2,1)} %get-tuple-element.49), channel_id=1, source_target_pairs={{0,28},{4,0},{8,4},{12,8},{16,12},{20,16},{24,20},{28,24},{1,29},{... | collective-permute-start | bytes 614408 | tf_op jit(solution)/shard_map/ppermute | solution.py:30
  10.8 17.5 %collective-permute-start.3 = (bf16[800,128]{1,0:T(8,128)(2,1)}, bf16[800,128]{1,0:T(8,128)(2,1)S(1)}, u32[]{:S(2)}, u32[]{:S(2)}) collective-permute-start(bf16[800,128]{1,0:T(8,128)(2,1)} %get-tuple-element.47), channel_id=1, source_target_pairs={{0,4},{4,8},{8,12},{12,16},{16,20},{20,24},{24,28},{28,0},{1,5},{5... | collective-permute-start | bytes 614408 | tf_op jit(solution)/shard_map/ppermute | solution.py:30
  11.8 26.8 %collective-permute-start.1 = (bf16[960,256]{1,0:T(8,128)(2,1)S(1)}, bf16[960,256]{1,0:T(8,128)(2,1)S(1)}, u32[]{:S(2)}, u32[]{:S(2)}) collective-permute-start(bf16[960,256]{1,0:T(8,128)(2,1)S(1)} %get-tuple-element.40), channel_id=1, source_target_pairs={{0,4},{4,8},{8,12},{12,16},{16,20},{20,24},{24,28},{28,0},{1,5},{5... | collective-permute-start | bytes 1474568 | tf_op jit(solution)/shard_map/ppermute | solution.py:30
  11.9 27.8 %collective-permute-start.2 = (bf16[960,256]{1,0:T(8,128)(2,1)S(1)}, bf16[960,256]{1,0:T(8,128)(2,1)S(1)}, u32[]{:S(2)}, u32[]{:S(2)}) collective-permute-start(bf16[960,256]{1,0:T(8,128)(2,1)S(1)} %get-tuple-element.41), channel_id=1, source_target_pairs={{0,28},{4,0},{8,4},{12,8},{16,12},{20,16},{24,20},{28,24},{1,29},{... | collective-permute-start | bytes 1474568 | tf_op jit(solution)/shard_map/ppermute | solution.py:30
  22.0 11.8 %collective-permute-start.9 = (bf16[800,128]{1,0:T(8,128)(2,1)S(1)}, bf16[800,128]{1,0:T(8,128)(2,1)S(1)}, u32[]{:S(2)}, u32[]{:S(2)}) collective-permute-start(bf16[800,128]{1,0:T(8,128)(2,1)S(1)} %collective-permute-done.5.refs_6_.refs_4_), channel_id=1, source_target_pairs={{0,2},{1,3},{2,0},{3,1},{4,6},{5,7},{6,4},{7,5},{8,10},{9,11},{10,... | collective-permute-start | bytes 614408 | tf_op jit(solution)/shard_map/ppermute | solution.py:35
  28.3 6.9 %collective-permute-start.7 = (bf16[800,128]{1,0:T(8,128)(2,1)S(1)}, bf16[800,128]{1,0:T(8,128)(2,1)S(1)}, u32[]{:S(2)}, u32[]{:S(2)}) collective-permute-start(bf16[800,128]{1,0:T(8,128)(2,1)S(1)} %collective-permute-done.3.refs_4_.refs_2_), channel_id=1, source_target_pairs={{0,2},{1,3},{2,0},{3,1},{4,6},{5,7},{6,4},{7,5},{8,10},{9,11},{10,... | collective-permute-start | bytes 614408 | tf_op jit(solution)/shard_map/ppermute | solution.py:35
  29.8 5.4 %collective-permute-start.6 = (bf16[800,128]{1,0:T(8,128)(2,1)S(1)}, bf16[800,128]{1,0:T(8,128)(2,1)S(1)}, u32[]{:S(2)}, u32[]{:S(2)}) collective-permute-start(bf16[800,128]{1,0:T(8,128)(2,1)S(1)} %collective-permute-done.5.refs_6_.refs_4_), channel_id=1, source_target_pairs={{0,1},{1,0},{2,3},{3,2},{4,5},{5,4},{6,7},{7,6},{8,9},{9,8},{10,11... | collective-permute-start | bytes 614408 | tf_op jit(solution)/shard_map/ppermute | solution.py:35
  33.8 25.3 %copy-start.8 = (bf16[640,256]{1,0:T(8,128)(2,1)}, bf16[640,256]{1,0:T(8,128)(2,1)S(1)}, u32[]{:S(2)}) copy-start(bf16[640,256]{1,0:T(8,128)(2,1)S(1)} %get-tuple-element.39.refs_0_) | copy-start | bytes 983044
  33.8 1.9 %collective-permute-start.4 = (bf16[800,128]{1,0:T(8,128)(2,1)S(1)}, bf16[800,128]{1,0:T(8,128)(2,1)S(1)}, u32[]{:S(2)}, u32[]{:S(2)}) collective-permute-start(bf16[800,128]{1,0:T(8,128)(2,1)S(1)} %collective-permute-done.3.refs_4_.refs_2_), channel_id=1, source_target_pairs={{0,1},{1,0},{2,3},{3,2},{4,5},{5,4},{6,7},{7,6},{8,9},{9,8},{10,11... | collective-permute-start | bytes 614408 | tf_op jit(solution)/shard_map/ppermute | solution.py:35
  35.2 4.5 %collective-permute-start.10 = (bf16[800,128]{1,0:T(8,128)(2,1)S(1)}, bf16[800,128]{1,0:T(8,128)(2,1)S(1)}, u32[]{:S(2)}, u32[]{:S(2)}) collective-permute-start(bf16[800,128]{1,0:T(8,128)(2,1)S(1)} %collective-permute-done.9.refs_10_.refs_8_), channel_id=1, source_target_pairs={{0,1},{1,0},{2,3},{3,2},{4,5},{5,4},{6,7},{7,6},{8,9},{9,8},{10,11... | collective-permute-start | bytes 614408 | tf_op jit(solution)/shard_map/ppermute | solution.py:35
  35.2 4.5 %collective-permute-start.8 = (bf16[800,128]{1,0:T(8,128)(2,1)S(1)}, bf16[800,128]{1,0:T(8,128)(2,1)S(1)}, u32[]{:S(2)}, u32[]{:S(2)}) collective-permute-start(bf16[800,128]{1,0:T(8,128)(2,1)S(1)} %collective-permute-done.7.refs_8_.refs_6_), channel_id=1, source_target_pairs={{0,1},{1,0},{2,3},{3,2},{4,5},{5,4},{6,7},{7,6},{8,9},{9,8},{10,11... | collective-permute-start | bytes 614408 | tf_op jit(solution)/shard_map/ppermute | solution.py:35
  35.7 10.6 %collective-permute-start.12 = (bf16[640,256]{1,0:T(8,128)(2,1)S(1)}, bf16[640,256]{1,0:T(8,128)(2,1)S(1)}, u32[]{:S(2)}, u32[]{:S(2)}) collective-permute-start(bf16[640,256]{1,0:T(8,128)(2,1)S(1)} %get-tuple-element.39.refs_0_), channel_id=1, source_target_pairs={{0,2},{1,3},{2,0},{3,1},{4,6},{5,7},{6,4},{7,5},{8,10},{9,11},{10,... | collective-permute-start | bytes 983048 | tf_op jit(solution)/shard_map/ppermute | solution.py:35
  42.5 14.3 %collective-permute-start.15 = (bf16[960,256]{1,0:T(8,128)(2,1)S(1)}, bf16[960,256]{1,0:T(8,128)(2,1)S(1)}, u32[]{:S(2)}, u32[]{:S(2)}) collective-permute-start(bf16[960,256]{1,0:T(8,128)(2,1)S(1)} %get-tuple-element.53.refs_2_.refs_4_), channel_id=1, source_target_pairs={{0,2},{1,3},{2,0},{3,1},{4,6},{5,7},{6,4},{7,5},{8,10},{9,11},{10,... | collective-permute-start | bytes 1474568 | tf_op jit(solution)/shard_map/ppermute | solution.py:35
  46.3 22.8 %copy-start.4 = (bf16[640,256]{1,0:T(8,128)(2,1)}, bf16[640,256]{1,0:T(8,128)(2,1)S(1)}, u32[]{:S(2)}) copy-start(bf16[640,256]{1,0:T(8,128)(2,1)S(1)} %collective-permute-done.12.refs_3_.refs_2_) | copy-start | bytes 983044
  49.6 9.5 %collective-permute-start.13 = (bf16[976,256]{1,0:T(8,128)(2,1)S(1)}, bf16[976,256]{1,0:T(8,128)(2,1)S(1)}, u32[]{:S(2)}, u32[]{:S(2)}) collective-permute-start(bf16[976,256]{1,0:T(8,128)(2,1)S(1)} %get-tuple-element.58.refs_4_.refs_8_), channel_id=1, source_target_pairs={{0,1},{1,0},{2,3},{3,2},{4,5},{5,4},{6,7},{7,6},{8,9},{9,8},{10,11... | collective-permute-start | bytes 1499144 | tf_op jit(solution)/shard_map/ppermute | solution.py:35
  49.6 17.1 %collective-permute-start.17 = (bf16[976,256]{1,0:T(8,128)(2,1)S(1)}, bf16[976,256]{1,0:T(8,128)(2,1)S(1)}, u32[]{:S(2)}, u32[]{:S(2)}) collective-permute-start(bf16[976,256]{1,0:T(8,128)(2,1)S(1)} %get-tuple-element.58.refs_4_.refs_8_), channel_id=1, source_target_pairs={{0,2},{1,3},{2,0},{3,1},{4,6},{5,7},{6,4},{7,5},{8,10},{9,11},{10,... | collective-permute-start | bytes 1499144 | tf_op jit(solution)/shard_map/ppermute | solution.py:35
  51.2 8.0 %collective-permute-start.11 = (bf16[960,256]{1,0:T(8,128)(2,1)S(1)}, bf16[960,256]{1,0:T(8,128)(2,1)S(1)}, u32[]{:S(2)}, u32[]{:S(2)}) collective-permute-start(bf16[960,256]{1,0:T(8,128)(2,1)S(1)} %get-tuple-element.53.refs_2_.refs_4_), channel_id=1, source_target_pairs={{0,1},{1,0},{2,3},{3,2},{4,5},{5,4},{6,7},{7,6},{8,9},{9,8},{10,11... | collective-permute-start | bytes 1474568 | tf_op jit(solution)/shard_map/ppermute | solution.py:35
  56.8 9.9 %collective-permute-start.16 = (bf16[960,256]{1,0:T(8,128)(2,1)S(1)}, bf16[960,256]{1,0:T(8,128)(2,1)S(1)}, u32[]{:S(2)}, u32[]{:S(2)}) collective-permute-start(bf16[960,256]{1,0:T(8,128)(2,1)S(1)} %collective-permute-done.15.refs_5_.refs_6_), channel_id=1, source_target_pairs={{0,1},{1,0},{2,3},{3,2},{4,5},{5,4},{6,7},{7,6},{8,9},{9,8},{10,11... | collective-permute-start | bytes 1474568 | tf_op jit(solution)/shard_map/ppermute | solution.py:35
  56.8 2.3 %collective-permute-start = (bf16[640,256]{1,0:T(8,128)(2,1)S(1)}, bf16[640,256]{1,0:T(8,128)(2,1)S(1)}, u32[]{:S(2)}, u32[]{:S(2)}) collective-permute-start(bf16[640,256]{1,0:T(8,128)(2,1)S(1)} %get-tuple-element.39.refs_0_), channel_id=1, source_target_pairs={{0,1},{1,0},{2,3},{3,2},{4,5},{5,4},{6,7},{7,6},{8,9},{9,8},{10,11... | collective-permute-start | bytes 983048 | tf_op jit(solution)/shard_map/ppermute | solution.py:35
  66.7 2.4 %collective-permute-start.18 = (bf16[976,256]{1,0:T(8,128)(2,1)S(1)}, bf16[976,256]{1,0:T(8,128)(2,1)S(1)}, u32[]{:S(2)}, u32[]{:S(2)}) collective-permute-start(bf16[976,256]{1,0:T(8,128)(2,1)S(1)} %collective-permute-done.17.refs_7_.refs_10_), channel_id=1, source_target_pairs={{0,1},{1,0},{2,3},{3,2},{4,5},{5,4},{6,7},{7,6},{8,9},{9,8},{10,11... | collective-permute-start | bytes 1499144 | tf_op jit(solution)/shard_map/ppermute | solution.py:35
  66.7 2.3 %collective-permute-start.14 = (bf16[640,256]{1,0:T(8,128)(2,1)S(1)}, bf16[640,256]{1,0:T(8,128)(2,1)S(1)}, u32[]{:S(2)}, u32[]{:S(2)}) collective-permute-start(bf16[640,256]{1,0:T(8,128)(2,1)S(1)} %collective-permute-done.12.refs_3_.refs_2_), channel_id=1, source_target_pairs={{0,1},{1,0},{2,3},{3,2},{4,5},{5,4},{6,7},{7,6},{8,9},{9,8},{10,11... | collective-permute-start | bytes 983048 | tf_op jit(solution)/shard_map/ppermute | solution.py:35
  87.1 8.7 %collective-permute-start.19 = (bf16[64,1152]{1,0:T(8,128)(2,1)}, bf16[64,1152]{1,0:T(8,128)(2,1)}, u32[]{:S(2)}, u32[]{:S(2)}) collective-permute-start(bf16[64,1152]{1,0:T(8,128)(2,1)} %get-tuple-element.64), channel_id=1, source_target_pairs={{0,16},{4,20},{8,24},{12,28},{16,0},{20,4},{24,8},{28,12},{1,17},{... | collective-permute-start | bytes 442376 | tf_op jit(solution)/shard_map/ppermute | solution.py:30
  89.7 18.7 %copy-start.9 = (bf16[640,256]{1,0:T(8,128)(2,1)S(1)}, bf16[640,256]{1,0:T(8,128)(2,1)}, u32[]{:S(2)}) copy-start(bf16[640,256]{1,0:T(8,128)(2,1)} %copy-done.8) | copy-start | bytes 983044
  89.7 18.7 %copy-start.11 = (bf16[640,256]{1,0:T(8,128)(2,1)S(1)}, bf16[640,256]{1,0:T(8,128)(2,1)}, u32[]{:S(2)}) copy-start(bf16[640,256]{1,0:T(8,128)(2,1)} %copy-done.10) | copy-start | bytes 983044
  (12 other events, 96.5 us)

commit v4 on v3

--- a/solution.py
+++ b/solution.py
@@ -47,47 +47,58 @@
     return pl.CostEstimate(flops=int(microseconds * 1.15e9), bytes_accessed=1, transcendentals=0)
 
 
-def rows_kernel(
-    width, lanes, me_ref, sizes_in, pattern_in, diag_in, couple_in, rows_ref, first_ref, last_ref, *scratch
-):
-    sizes_ref, pattern_ref, diag_ref, couple_ref, scalar_sems, diag_sems, couple_sems = scratch
-    parts = diag_sems.shape[0]
-    each = diag_in.shape[0] // parts
-    scalars = [
-        pltpu.make_async_copy(sizes_in, sizes_ref, scalar_sems.at[0]),
-        pltpu.make_async_copy(pattern_in, pattern_ref, scalar_sems.at[1]),
-    ]
-    blocks = []
-    for part in range(parts):
-        at = pl.ds(part * each, each)
-        blocks.append(pltpu.make_async_copy(couple_in.at[at], couple_ref.at[at], couple_sems.at[part]))
-        blocks.append(pltpu.make_async_copy(diag_in.at[at], diag_ref.at[at], diag_sems.at[part]))
-    for copy in scalars + blocks:
+def joined(behind, diag, couple, size, wide):
+    n = diag.shape[0]
+    whole = jnp.concatenate([behind, diag.astype(F32), couple, jnp.ones((n, wide - 3 * n), F32)], axis=1)
+    place = lax.broadcasted_iota(jnp.int32, (n, wide), 0)
+    return jnp.where(place < size, whole, 0.0).astype(BF16)
+
+
+def rows_kernel(sizes_ref, pattern_ref, diag_ref, couple_ref, rows_ref):
+    count, n, wide = rows_ref.shape
+    behind = jnp.zeros((n, n), F32)
+    for e in range(count):
+        couple = couple_ref[e].astype(F32) * pattern_ref[e].astype(F32)
+        rows_ref[e] = joined(behind, diag_ref[e], couple, sizes_ref[e], wide)
+        behind = jnp.transpose(couple)
+
+
+def ends_kernel(wide, me_ref, sizes_in, pattern_in, diag_in, couple_in, first_ref, last_ref, *scratch):
+    sizes_ref, pattern_ref, diag_ref, couple_ref, row_ref, sems = scratch
+    count, n, _ = diag_in.shape
+    depth = DEGREE - 1
+    lanes = first_ref.shape[1]
+    low, high, before = pl.ds(0, depth), pl.ds(count - depth, depth), pl.ds(count - depth - 1, depth + 1)
+    pairs = [(sizes_in, sizes_ref), (pattern_in, pattern_ref)]
+    pairs += [(couple_in.at[low], couple_ref.at[low]), (diag_in.at[low], diag_ref.at[low])]
+    pairs += [(couple_in.at[before], couple_ref.at[before]), (diag_in.at[high], diag_ref.at[high])]
+    copies = [pltpu.make_async_copy(source, target, sems.at[k]) for k, (source, target) in enumerate(pairs)]
+    for copy in copies:
         copy.start()
-    for copy in scalars:
+    at = pl.ds(pl.multiple_of(me_ref[0] * lanes, lanes), lanes)
+
+    def coupled(e):
+        return couple_ref[e].astype(F32) * pattern_ref[e].astype(F32)
+
+    for copy in copies[:4]:
         copy.wait()
-    n = width
-    count = rows_ref.shape[0]
-    depth = DEGREE - 1
-    wide = rows_ref.shape[2]
-    place = lax.broadcasted_iota(jnp.int32, (n, wide), 0)
     behind = jnp.zeros((n, n), F32)
-    ones = jnp.ones((n, wide - 3 * n), F32)
-    for e in range(count):
-        if e % each == 0:
-            blocks[2 * (e // each)].wait()
-            blocks[2 * (e // each) + 1].wait()
-        couple = couple_ref[e].astype(F32) * pattern_ref[e].astype(F32)
-        whole = jnp.concatenate([behind, diag_ref[e].astype(F32), couple, ones], axis=1)
-        rows_ref[e] = jnp.where(place < sizes_ref[e], whole, 0.0).astype(BF16)
+    for e in range(depth):
+        couple = coupled(e)
+        row_ref[e] = joined(behind, diag_ref[e], couple, sizes_ref[e], wide)
+        first_ref[e * n : (e + 1) * n, :] = row_ref[e, :, at]
         behind = jnp.transpose(couple)
-    at = pl.ds(pl.multiple_of(me_ref[0] * lanes, lanes), lanes)
+    for copy in copies[4:]:
+        copy.wait()
+    behind = jnp.transpose(coupled(count - depth - 1))
     for e in range(depth):
-        first_ref[e * n : (e + 1) * n, :] = rows_ref[e, :, at]
-        last_ref[e * n : (e + 1) * n, :] = rows_ref[count - depth + e, :, at]
-
-
-def vectors_kernel(width, count, group, sizes_ref, bands_ref, out_ref, first_ref, last_ref):
+        couple = coupled(count - depth + e)
+        row_ref[depth + e] = joined(behind, diag_ref[count - depth + e], couple, sizes_ref[count - depth + e], wide)
+        last_ref[e * n : (e + 1) * n, :] = row_ref[depth + e, :, at]
+        behind = jnp.transpose(couple)
+
+
+def vectors_kernel(width, count, group, sizes_ref, bands_ref, out_ref, *edge_refs):
     n = width
     local = bands_ref.shape[0]
     place = lax.broadcasted_iota(jnp.int32, (n, local), 0)
@@ -96,8 +107,12 @@
         for e in range(begin, begin + group):
             part = turned[(e - begin) * n : (e - begin + 1) * n, :].astype(F32)
             out_ref[e * n : (e + 1) * n, :] = jnp.where(place < sizes_ref[e], part, 0.0).astype(BF16)
-    first_ref[...] = out_ref[: DEGREE * n, :]
-    last_ref[...] = out_ref[(count - DEGREE) * n :, :]
+    near = 0
+    for index, strip in enumerate(STRIPS):
+        far = near + strip
+        edge_refs[2 * index][...] = out_ref[near * n : far * n, :]
+        edge_refs[2 * index + 1][...] = out_ref[(count - far) * n : (count - near) * n, :]
+        near = far
 
 
 def advance(row, window, center, before, first):
@@ -202,9 +217,8 @@
         keep = halo_right[0, :, 3 * n : 3 * n + 1].astype(F32)
         return jnp.concatenate([(turned * keep).astype(BF16), halo_right[0, :, n : 3 * n]], axis=1)
 
-    near = -offset - strip
-    left_scr[0, : strip * n, :] = left_y_ref[(DEGREE + offset) * n : (DEGREE - near) * n, :]
-    right_scr[0, 2 * n :, :] = right_y_ref[near * n : (near + strip) * n, :]
+    left_scr[0, : strip * n, :] = left_y_ref[...]
+    right_scr[0, 2 * n :, :] = right_y_ref[...]
     for step in range(DEGREE):
         left_scr[step, strip * n :, :] = left_edge[step][...]
         right_scr[step, : 2 * n, :] = right_edge[step][...]
@@ -373,35 +387,40 @@
     elem_me = lax.axis_index("elem").astype(jnp.int32).reshape(1)
     band_me = lax.axis_index("band").astype(jnp.int32).reshape(1)
 
-    rows, first_rows, last_rows = pl.pallas_call(
-        functools.partial(rows_kernel, n, lanes),
-        out_shape=[jax.ShapeDtypeStruct((count, n, wide), BF16)]
-        + [jax.ShapeDtypeStruct((depth * n, lanes), BF16)] * 2,
+    first_rows, last_rows = pl.pallas_call(
+        functools.partial(ends_kernel, wide),
+        out_shape=[jax.ShapeDtypeStruct((depth * n, lanes), BF16)] * 2,
         in_specs=[SMEM] + [HBM] * 4,
-        out_specs=[VMEM] * 3,
+        out_specs=[VMEM] * 2,
         scratch_shapes=[pltpu.SMEM((count,), jnp.int32)] * 2
         + [pltpu.VMEM((count, n, n), BF16)] * 2
-        + [pltpu.SemaphoreType.DMA((2,))]
-        + [pltpu.SemaphoreType.DMA((math.gcd(count, 4),))] * 2,
+        + [pltpu.VMEM((2 * depth, n, wide), BF16), pltpu.SemaphoreType.DMA((6,))],
         compiler_params=params(60),
         cost_estimate=about(0.01),
+        name="ends",
+    )(band_me, basis_sizes, coupling_pattern, h_diag, h_couple)
+    rows = pl.pallas_call(
+        rows_kernel,
+        out_shape=jax.ShapeDtypeStruct((count, n, wide), BF16),
+        in_specs=[SMEM] * 2 + [VMEM] * 2,
+        out_specs=VMEM,
+        compiler_params=params(16),
+        cost_estimate=about(0.01),
         name="rows",
-    )(band_me, basis_sizes, coupling_pattern, h_diag, h_couple)
+    )(basis_sizes, after(coupling_pattern, first_rows), h_diag, h_couple)
     left_rows = from_behind(last_rows, "elem", 1)
     right_rows = from_behind(first_rows, "elem", -1)
 
-    halo = jax.ShapeDtypeStruct((DEGREE * n, local), BF16)
-    start, first_y, last_y = pl.pallas_call(
+    start, *ends = pl.pallas_call(
         functools.partial(vectors_kernel, n, count, math.lcm(n, LANES) // n),
-        out_shape=[jax.ShapeDtypeStruct((count * n, local), BF16), halo, halo],
+        out_shape=[jax.ShapeDtypeStruct((count * n, local), BF16)]
+        + [jax.ShapeDtypeStruct((strip * n, local), BF16) for strip in STRIPS for _ in range(2)],
         in_specs=[SMEM, VMEM],
-        out_specs=[VMEM] * 3,
+        out_specs=[VMEM] * (1 + 2 * len(STRIPS)),
         compiler_params=params(16),
         cost_estimate=about(0.01),
         name="vectors",
     )(basis_sizes, bands)
-    left_y = from_behind(last_y, "elem", 1)
-    right_y = from_behind(first_y, "elem", -1)
 
     inner = (count - 2 * DEGREE) * n
     whole = jax.ShapeDtypeStruct((count * n, local), BF16)
@@ -419,6 +438,8 @@
         cost_estimate=about(0.01),
         name="interior_first",
     )(rows, start)
+    left_y = [from_behind(after(ends[1], even), "elem", 1)]
+    right_y = [from_behind(after(ends[0], even), "elem", -1)]
     own_rows = [after(side, even) for side in (left_rows, right_rows)]
     across_rows = [swap(side, "band", half) for side in own_rows]
     older, newer = (odd, even) if SPLIT % 2 == 0 else (even, odd)
@@ -434,7 +455,10 @@
     )(rows, older, newer)
     left_edge = [left_edge, left_more]
     right_edge = [right_edge, right_more]
-    across_rows = [after(side, chunk) for side in across_rows]
+    across_rows = [after(side, chunk, left_y[0], right_y[0]) for side in across_rows]
+    for index in range(1, len(STRIPS)):
+        left_y.append(from_behind(after(ends[2 * index + 1], chunk), "elem", 1))
+        right_y.append(from_behind(after(ends[2 * index], chunk), "elem", -1))
     both = [block for side in (*own_rows, *across_rows) for block in lower_blocks(side)]
     chunks, across = [chunk], [swap(chunk, "band", half)]
     spans = [[(0, inner, DEGREE * n)]]
@@ -458,7 +482,7 @@
             compiler_params=params(32),
             cost_estimate=about(3),
             name="strip",
-        )(band_me, left_y, right_y, rows, squares, *left_edge, *right_edge, *both)
+        )(band_me, left_y[index], right_y[index], rows, squares, *left_edge, *right_edge, *both)
         left_edge, right_edge = [others[0]], [others[1]]
         chunks.append(chunk)
         across.append(swap(chunk, "band", half))

time: 111 us -> 106 us (0.955)
  blocking collectives: 26.1 us -> 23 us
  local copies, waits for them, and re-layouts: 3.45 us -> 1.78 us
  waiting for transfers between devices: 31.7 us -> 30.5 us
    all_to_all x1, blocking collectives: 15.6 us -> 12.4 us  [fast_shards(): lax.all_to_all(late, 'elem', 0, 0, tiled=True, axis_index_groups=groups)]
    ppermute x15, starting transfers between devices: 10.1 us -> 6.93 us  [swap(): lax.ppermute(value, axis, [(source, source ^ bit) for source in range(cou...]
    ppermute x15, waiting for transfers between devices: 18.4 us -> 15.3 us  [swap(): lax.ppermute(value, axis, [(source, source ^ bit) for source in range(cou...]
    ppermute x5 -> x7, starting transfers between devices: 13.6 us -> 16.6 us  [from_behind(): return lax.ppermute(value, axis, pairs)]
    ppermute x5 -> x7, waiting for transfers between devices: 13.3 us -> 15.2 us  [from_behind(): return lax.ppermute(value, axis, pairs)]
    unnamed x32 -> x34, local copies, waits for them, and re-layouts: 3.45 us -> 1.78 us
    pallas_call x1 -> x2, Pallas kernels: 4.74 us -> 5.19 us  [the longest x1 3.14 us: fast_shards(): pl.pallas_call(functools.partial(ends_kernel, wide), out_shape=[jax.Shape...]
  transfers between devices with their start and end apart: 20 -> 22, of which waited for: 10 -> 9; matrix products, arithmetic and copies ran while one was open for 0% -> 0% of each run, Pallas kernels for 14% -> 17%
where the time goes in v4:
time: 106 us
  waiting for transfers between devices  30.5 us (29%)
  Pallas kernels  26.5 us (25%)
  starting transfers between devices  23.5 us (22%)
  blocking collectives  23 us (22%)
  local copies, waits for them, and re-layouts  1.78 us (2%)
    ppermute x7, starting transfers between devices, from_behind(): return lax.ppermute(value, axis, pairs)  16.6 us
    ppermute x15, waiting for transfers between devices, swap(): lax.ppermute(value, axis, [(source, source ^ bit) for source in range(cou...  15.3 us
    ppermute x7, waiting for transfers between devices, from_behind(): return lax.ppermute(value, axis, pairs)  15.2 us
    all_to_all x1, blocking collectives, fast_shards(): lax.all_to_all(late, 'elem', 0, 0, tiled=True, axis_index_groups=groups)  12.4 us
    all_to_all x1, blocking collectives, fast_shards(): lax.all_to_all(weights, 'elem', 0, 0, tiled=True, axis_index_groups=groups)  10.7 us
    ppermute x15, starting transfers between devices, swap(): lax.ppermute(value, axis, [(source, source ^ bit) for source in range(cou...  6.93 us
    pallas_call x2, Pallas kernels, fast_shards(): pl.pallas_call(functools.partial(strip_kernel, n, count, strip, offset, l...  6.1 us
    pallas_call x1, Pallas kernels, fast_shards(): pl.pallas_call(functools.partial(interior_kernel, n, count, SPLIT, DEGREE...  3.97 us
  transfers between devices with their start and end apart: 22, of which 9 were waited for; matrix products, arithmetic and copies ran while one was open for 0% of the time, Pallas kernels for 17%

profile of v4, /device:TPU:0, one launch (start us, length us, event | category | flops | bytes accessed | tf_op | source)
XLA Modules:
  0.0 105.5 jit_solution(1267719757413497823)
XLA Ops:
  0.0 3.1 %ends.1 = (bf16[800,128]{1,0:T(8,128)(2,1)}, bf16[800,128]{1,0:T(8,128)(2,1)}) custom-call(s32[1]{0:T(128)} %bitcast.1.me_ref, s32[16]{0:T(128)} %sizes_ref.3, s32[16]{0:T(128)} %pattern_ref, bf16[16,160,160]{2,1,0:T(8,128)(2,1)} %diag_ref.1, bf16[16,160,160]{2,1,0:T(8,128)(2,1)} %couple_ref.1), custom_call_target="tpu_custom_call" | custom-call | flops 11500000 | bytes 1 | tf_op jit(solution)/shard_map/ends/pallas_call | solution.py:390
  3.2 6.0 %collective-permute-start.5 = (bf16[800,128]{1,0:T(8,128)(2,1)}, bf16[800,128]{1,0:T(8,128)(2,1)S(1)}, u32[]{:S(2)}, u32[]{:S(2)}) collective-permute-start(bf16[800,128]{1,0:T(8,128)(2,1)} %get-tuple-element.41), channel_id=1, source_target_pairs={{0,28},{4,0},{8,4},{12,8},{16,12},{20,16},{24,20},{28,24},{1,29},{... | collective-permute-start | bytes 614408 | tf_op jit(solution)/shard_map/ppermute | solution.py:30
  10.3 2.1 %rows.1.rows_ref = bf16[16,160,512]{2,1,0:T(8,128)(2,1)S(1)} custom-call(s32[16]{0:T(128)S(1)} %copy-done.15, s32[16]{0:T(128)S(1)} %copy-done.16, bf16[16,160,160]{2,1,0:T(8,128)(2,1)S(1)} %copy-done, bf16[16,160,160]{2,1,0:T(8,128)(2,1)S(1)} %copy-done.1), custom_call_target="tpu_custom_call" | custom-call | flops 11500000 | bytes 1 | tf_op jit(solution)/shard_map/rows/pallas_call | solution.py:402
  12.3 3.4 %interior_first.1 = (bf16[2,320,256]{2,1,0:T(8,128)(2,1)S(1)}, bf16[2,320,256]{2,1,0:T(8,128)(2,1)S(1)}, bf16[2560,256]{1,0:T(8,128)(2,1)S(1)}, bf16[2560,256]{1,0:T(8,128)(2,1)S(1)}) custom-call(bf16[16,160,512]{2,1,0:T(8,128)(2,1)S(1)} %rows.1.rows_ref, bf16[2560,256]{1,0:T(8,128)(2,1)S(1)} %get-tuple-element.43.refs_0_), custom_call_target="tpu_custom_call" | custom-call | flops 11500000 | bytes 1 | tf_op jit(solution)/shard_map/interior_first/pallas_call | solution.py:432
  15.8 4.8 %collective-permute-start.2 = (bf16[480,256]{1,0:T(8,128)(2,1)S(1)}, bf16[480,256]{1,0:T(8,128)(2,1)S(1)}, u32[]{:S(2)}, u32[]{:S(2)}) collective-permute-start(bf16[480,256]{1,0:T(8,128)(2,1)S(1)} %get-tuple-element.50), channel_id=1, source_target_pairs={{0,28},{4,0},{8,4},{12,8},{16,12},{20,16},{24,20},{28,24},{1,29},{... | collective-permute-start | bytes 737288 | tf_op jit(solution)/shard_map/ppermute | solution.py:30
  20.6 1.5 %collective-permute-start.9 = (bf16[800,128]{1,0:T(8,128)(2,1)S(1)}, bf16[800,128]{1,0:T(8,128)(2,1)S(1)}, u32[]{:S(2)}, u32[]{:S(2)}) collective-permute-start(bf16[800,128]{1,0:T(8,128)(2,1)S(1)} %collective-permute-done.5.refs_6_.refs_4_), channel_id=1, source_target_pairs={{0,2},{1,3},{2,0},{3,1},{4,6},{5,7},{6,4},{7,5},{8,10},{9,11},{10,... | collective-permute-start | bytes 614408 | tf_op jit(solution)/shard_map/ppermute | solution.py:35
  22.6 4.0 %interior_rest.1 = (bf16[4,320,256]{2,1,0:T(8,128)(2,1)S(1)}, bf16[4,320,256]{2,1,0:T(8,128)(2,1)S(1)}, bf16[640,256]{1,0:T(8,128)(2,1)S(1)}, f32[1,256]{1,0:T(1,128)S(1)}) custom-call(bf16[16,160,512]{2,1,0:T(8,128)(2,1)S(1)} %rows.1.rows_ref, bf16[2560,256]{1,0:T(8,128)(2,1)S(1)} %get-tuple-element.44.refs_0_, bf16[2560,256]{1,0:T(8,128)(2,1)S(1)} %get-tuple-element.45.refs_1_), custom_call_target="tpu_custom_call" | custom-call | flops 11500000 | bytes 1 | tf_op jit(solution)/shard_map/interior_rest/pallas_call | solution.py:446
  27.2 2.0 %collective-permute-done.2.right_y_ref = bf16[480,256]{1,0:T(8,128)(2,1)S(1)} collective-permute-done((bf16[480,256]{1,0:T(8,128)(2,1)S(1)}, bf16[480,256]{1,0:T(8,128)(2,1)S(1)}, u32[]{:S(2)}, u32[]{:S(2)}) %collective-permute-start.2) | collective-permute-done | bytes 245792 | tf_op jit(solution)/shard_map/ppermute | solution.py:30
  29.2 1.8 %collective-permute-done.7.refs_8_.refs_6_ = bf16[800,128]{1,0:T(8,128)(2,1)S(1)} collective-permute-done((bf16[800,128]{1,0:T(8,128)(2,1)S(1)}, bf16[800,128]{1,0:T(8,128)(2,1)S(1)}, u32[]{:S(2)}, u32[]{:S(2)}) %collective-permute-start.7) | collective-permute-done | bytes 204832 | tf_op jit(solution)/shard_map/ppermute | solution.py:35
  31.5 1.5 %collective-permute-start.14 = (bf16[640,256]{1,0:T(8,128)(2,1)S(1)}, bf16[640,256]{1,0:T(8,128)(2,1)S(1)}, u32[]{:S(2)}, u32[]{:S(2)}) collective-permute-start(bf16[640,256]{1,0:T(8,128)(2,1)S(1)} %get-tuple-element.46.refs_0_), channel_id=1, source_target_pairs={{0,2},{1,3},{2,0},{3,1},{4,6},{5,7},{6,4},{7,5},{8,10},{9,11},{10,... | collective-permute-start | bytes 983048 | tf_op jit(solution)/shard_map/ppermute | solution.py:35
  33.0 4.7 %collective-permute-start.13 = (bf16[480,256]{1,0:T(8,128)(2,1)S(1)}, bf16[480,256]{1,0:T(8,128)(2,1)S(1)}, u32[]{:S(2)}, u32[]{:S(2)}) collective-permute-start(bf16[480,256]{1,0:T(8,128)(2,1)S(1)} %get-tuple-element.65), channel_id=1, source_target_pairs={{0,28},{4,0},{8,4},{12,8},{16,12},{20,16},{24,20},{28,24},{1,29},{... | collective-permute-start | bytes 737288 | tf_op jit(solution)/shard_map/ppermute | solution.py:30
  37.8 2.7 %strip.2 = (bf16[960,256]{1,0:T(8,128)(2,1)S(1)}, bf16[6,320,256]{2,1,0:T(8,128)(2,1)S(1)}, bf16[6,320,256]{2,1,0:T(8,128)(2,1)S(1)}, f32[1,256]{1,0:T(1,128)S(1)}) custom-call(s32[1]{0:T(128)} %bitcast.1.me_ref, bf16[480,256]{1,0:T(8,128)(2,1)S(1)} %collective-permute-done.1.left_y_ref, bf16[480,256]{1,0:T(8,128)(2,1)S(1)} %collective-permute-done.2.right_y_ref, ...), custom_call_target="tpu_custom_call" | custom-call | flops 3449999872 | bytes 1 | tf_op jit(solution)/shard_map/strip/pallas_call | solution.py:475
  41.1 2.3 %collective-permute-done.12.left_y_ref = bf16[480,256]{1,0:T(8,128)(2,1)S(1)} collective-permute-done((bf16[480,256]{1,0:T(8,128)(2,1)S(1)}, bf16[480,256]{1,0:T(8,128)(2,1)S(1)}, u32[]{:S(2)}, u32[]{:S(2)}) %collective-permute-start.12) | collective-permute-done | bytes 245792 | tf_op jit(solution)/shard_map/ppermute | solution.py:30
  43.4 2.7 %collective-permute-done.13.right_y_ref = bf16[480,256]{1,0:T(8,128)(2,1)S(1)} collective-permute-done((bf16[480,256]{1,0:T(8,128)(2,1)S(1)}, bf16[480,256]{1,0:T(8,128)(2,1)S(1)}, u32[]{:S(2)}, u32[]{:S(2)}) %collective-permute-start.13) | collective-permute-done | bytes 245792 | tf_op jit(solution)/shard_map/ppermute | solution.py:30
  46.1 3.3 %strip.3 = (bf16[976,256]{1,0:T(8,128)(2,1)S(1)}, f32[8,128]{1,0:T(8,128)}, f32[8,128]{1,0:T(8,128)}, f32[1,256]{1,0:T(1,128)}) custom-call(s32[1]{0:T(128)} %bitcast.1.me_ref, bf16[480,256]{1,0:T(8,128)(2,1)S(1)} %collective-permute-done.12.left_y_ref, bf16[480,256]{1,0:T(8,128)(2,1)S(1)} %collective-permute-done.13.right_y_ref, ...), custom_call_target="tpu_custom_call" | custom-call | flops 3449999872 | bytes 1 | tf_op jit(solution)/shard_map/strip/pallas_call | solution.py:475
  50.2 2.9 %collective-permute-done.17.refs_5_.refs_6_ = bf16[960,256]{1,0:T(8,128)(2,1)S(1)} collective-permute-done((bf16[960,256]{1,0:T(8,128)(2,1)S(1)}, bf16[960,256]{1,0:T(8,128)(2,1)S(1)}, u32[]{:S(2)}, u32[]{:S(2)}) %collective-permute-start.17) | collective-permute-done | bytes 491552 | tf_op jit(solution)/shard_map/ppermute | solution.py:35
  53.6 1.8 %collective-permute-done.refs_1_ = bf16[640,256]{1,0:T(8,128)(2,1)S(1)} collective-permute-done((bf16[640,256]{1,0:T(8,128)(2,1)S(1)}, bf16[640,256]{1,0:T(8,128)(2,1)S(1)}, u32[]{:S(2)}, u32[]{:S(2)}) %collective-permute-start) | collective-permute-done | bytes 327712 | tf_op jit(solution)/shard_map/ppermute | solution.py:35
  55.4 1.3 %gram_early.1 = (bf16[4,64,512]{2,1,0:T(8,128)(2,1)S(1)}, bf16[2,16,256]{2,1,0:T(8,128)(2,1)S(1)}, bf16[256,2560]{1,0:T(8,128)(2,1)S(1)}) custom-call(bf16[640,256]{1,0:T(8,128)(2,1)S(1)} %get-tuple-element.46.refs_0_, bf16[640,256]{1,0:T(8,128)(2,1)S(1)} %collective-permute-done.refs_1_, bf16[960,256]{1,0:T(8,128)(2,1)S(1)} %get-tuple-element.61.refs_2_.refs_4_, ...), custom_call_target="tpu_custom_call" | custom-call | flops 11500000 | bytes 1 | tf_op jit(solution)/shard_map/gram_early/pallas_call | solution.py:503
  56.7 6.9 %collective-permute-done.19.refs_7_.refs_10_ = bf16[976,256]{1,0:T(8,128)(2,1)S(1)} collective-permute-done((bf16[976,256]{1,0:T(8,128)(2,1)S(1)}, bf16[976,256]{1,0:T(8,128)(2,1)S(1)}, u32[]{:S(2)}, u32[]{:S(2)}) %collective-permute-start.19) | collective-permute-done | bytes 499744 | tf_op jit(solution)/shard_map/ppermute | solution.py:35
  64.1 1.8 %collective-permute-done.16.refs_4_.refs_3_ = bf16[640,256]{1,0:T(8,128)(2,1)S(1)} collective-permute-done((bf16[640,256]{1,0:T(8,128)(2,1)S(1)}, bf16[640,256]{1,0:T(8,128)(2,1)S(1)}, u32[]{:S(2)}, u32[]{:S(2)}) %collective-permute-start.16) | collective-permute-done | bytes 327712 | tf_op jit(solution)/shard_map/ppermute | solution.py:35
  66.9 12.4 %all_to_all.10.got_ref = bf16[4,64,1152]{2,1,0:T(8,128)(2,1)S(1)} all-to-all(bf16[4,64,1152]{2,1,0:T(8,128)(2,1)S(1)} %gram_late.1), channel_id=1, replica_groups={{0,4,8,12},{16,20,24,28},{1,5,9,13},{17,21,25,29},{2,6,10,14},{18,22,26..., dimensions={0} | all-to-all | bytes 1179648 | tf_op jit(solution)/shard_map/all_to_all | solution.py:518
  81.8 8.2 %collective-permute-done.21.other_ref = bf16[64,1152]{1,0:T(8,128)(2,1)} collective-permute-done((bf16[64,1152]{1,0:T(8,128)(2,1)}, bf16[64,1152]{1,0:T(8,128)(2,1)}, u32[]{:S(2)}, u32[]{:S(2)}) %collective-permute-start.21) | collective-permute-done | bytes 147488 | tf_op jit(solution)/shard_map/ppermute | solution.py:30
  92.0 10.7 %all_to_all.11 = bf16[4,64,1024]{2,1,0:T(8,128)(2,1)S(1)} all-to-all(bf16[4,64,1024]{2,1,0:T(8,128)(2,1)S(1)} %weights.1), channel_id=1, replica_groups={{0,4,8,12},{16,20,24,28},{1,5,9,13},{17,21,25,29},{2,6,10,14},{18,22,26..., dimensions={0} | all-to-all | bytes 1048576 | tf_op jit(solution)/shard_map/all_to_all | solution.py:540
  102.7 2.8 %rotate.1 = bf16[256,2560]{1,0:T(8,128)(2,1)} custom-call(bf16[256,1024]{1,0:T(8,128)(2,1)S(1)} %bitcast.3, bf16[640,256]{1,0:T(8,128)(2,1)S(1)} %copy-done.9, bf16[640,256]{1,0:T(8,128)(2,1)S(1)} %copy-done.11, bf16[640,256]{1,0:T(8,128)(2,1)S(1)} %copy-done.5, bf16[640,256]{1,0:T(8,128)(2,1)S(1)} %copy-done.7, ...), custom_call_target="tpu_custom_call" | custom-call | flops 11500000 | bytes 1 | tf_op jit(solution)/shard_map/rotate/pallas_call | solution.py:541
  (68 shorter events, 10.5 us)
Async XLA Ops:
  3.2 17.4 %collective-permute-start.5 = (bf16[800,128]{1,0:T(8,128)(2,1)}, bf16[800,128]{1,0:T(8,128)(2,1)S(1)}, u32[]{:S(2)}, u32[]{:S(2)}) collective-permute-start(bf16[800,128]{1,0:T(8,128)(2,1)} %get-tuple-element.41), channel_id=1, source_target_pairs={{0,28},{4,0},{8,4},{12,8},{16,12},{20,16},{24,20},{28,24},{1,29},{... | collective-permute-start | bytes 614408 | tf_op jit(solution)/shard_map/ppermute | solution.py:30
  9.2 12.9 %collective-permute-start.3 = (bf16[800,128]{1,0:T(8,128)(2,1)}, bf16[800,128]{1,0:T(8,128)(2,1)S(1)}, u32[]{:S(2)}, u32[]{:S(2)}) collective-permute-start(bf16[800,128]{1,0:T(8,128)(2,1)} %get-tuple-element.56), channel_id=1, source_target_pairs={{0,4},{4,8},{8,12},{12,16},{16,20},{20,24},{24,28},{28,0},{1,5},{5... | collective-permute-start | bytes 614408 | tf_op jit(solution)/shard_map/ppermute | solution.py:30
  15.8 10.9 %collective-permute-start.1 = (bf16[480,256]{1,0:T(8,128)(2,1)S(1)}, bf16[480,256]{1,0:T(8,128)(2,1)S(1)}, u32[]{:S(2)}, u32[]{:S(2)}) collective-permute-start(bf16[480,256]{1,0:T(8,128)(2,1)S(1)} %get-tuple-element.48), channel_id=1, source_target_pairs={{0,4},{4,8},{8,12},{12,16},{16,20},{20,24},{24,28},{28,0},{1,5},{5... | collective-permute-start | bytes 737288 | tf_op jit(solution)/shard_map/ppermute | solution.py:30
  15.8 13.3 %collective-permute-start.2 = (bf16[480,256]{1,0:T(8,128)(2,1)S(1)}, bf16[480,256]{1,0:T(8,128)(2,1)S(1)}, u32[]{:S(2)}, u32[]{:S(2)}) collective-permute-start(bf16[480,256]{1,0:T(8,128)(2,1)S(1)} %get-tuple-element.50), channel_id=1, source_target_pairs={{0,28},{4,0},{8,4},{12,8},{16,12},{20,16},{24,20},{28,24},{1,29},{... | collective-permute-start | bytes 737288 | tf_op jit(solution)/shard_map/ppermute | solution.py:30
  20.6 8.6 %collective-permute-start.9 = (bf16[800,128]{1,0:T(8,128)(2,1)S(1)}, bf16[800,128]{1,0:T(8,128)(2,1)S(1)}, u32[]{:S(2)}, u32[]{:S(2)}) collective-permute-start(bf16[800,128]{1,0:T(8,128)(2,1)S(1)} %collective-permute-done.5.refs_6_.refs_4_), channel_id=1, source_target_pairs={{0,2},{1,3},{2,0},{3,1},{4,6},{5,7},{6,4},{7,5},{8,10},{9,11},{10,... | collective-permute-start | bytes 614408 | tf_op jit(solution)/shard_map/ppermute | solution.py:35
  22.1 8.8 %collective-permute-start.7 = (bf16[800,128]{1,0:T(8,128)(2,1)S(1)}, bf16[800,128]{1,0:T(8,128)(2,1)S(1)}, u32[]{:S(2)}, u32[]{:S(2)}) collective-permute-start(bf16[800,128]{1,0:T(8,128)(2,1)S(1)} %collective-permute-done.3.refs_4_.refs_2_), channel_id=1, source_target_pairs={{0,2},{1,3},{2,0},{3,1},{4,6},{5,7},{6,4},{7,5},{8,10},{9,11},{10,... | collective-permute-start | bytes 614408 | tf_op jit(solution)/shard_map/ppermute | solution.py:35
  26.6 28.8 %copy-start.8 = (bf16[640,256]{1,0:T(8,128)(2,1)}, bf16[640,256]{1,0:T(8,128)(2,1)S(1)}, u32[]{:S(2)}) copy-start(bf16[640,256]{1,0:T(8,128)(2,1)S(1)} %get-tuple-element.46.refs_0_) | copy-start | bytes 983044
  26.6 6.4 %collective-permute-start.4 = (bf16[800,128]{1,0:T(8,128)(2,1)S(1)}, bf16[800,128]{1,0:T(8,128)(2,1)S(1)}, u32[]{:S(2)}, u32[]{:S(2)}) collective-permute-start(bf16[800,128]{1,0:T(8,128)(2,1)S(1)} %collective-permute-done.3.refs_4_.refs_2_), channel_id=1, source_target_pairs={{0,1},{1,0},{2,3},{3,2},{4,5},{5,4},{6,7},{7,6},{8,9},{9,8},{10,11... | collective-permute-start | bytes 614408 | tf_op jit(solution)/shard_map/ppermute | solution.py:35
  26.7 6.3 %collective-permute-start.6 = (bf16[800,128]{1,0:T(8,128)(2,1)S(1)}, bf16[800,128]{1,0:T(8,128)(2,1)S(1)}, u32[]{:S(2)}, u32[]{:S(2)}) collective-permute-start(bf16[800,128]{1,0:T(8,128)(2,1)S(1)} %collective-permute-done.5.refs_6_.refs_4_), channel_id=1, source_target_pairs={{0,1},{1,0},{2,3},{3,2},{4,5},{5,4},{6,7},{7,6},{8,9},{9,8},{10,11... | collective-permute-start | bytes 614408 | tf_op jit(solution)/shard_map/ppermute | solution.py:35
  31.0 6.8 %collective-permute-start.8 = (bf16[800,128]{1,0:T(8,128)(2,1)S(1)}, bf16[800,128]{1,0:T(8,128)(2,1)S(1)}, u32[]{:S(2)}, u32[]{:S(2)}) collective-permute-start(bf16[800,128]{1,0:T(8,128)(2,1)S(1)} %collective-permute-done.7.refs_8_.refs_6_), channel_id=1, source_target_pairs={{0,1},{1,0},{2,3},{3,2},{4,5},{5,4},{6,7},{7,6},{8,9},{9,8},{10,11... | collective-permute-start | bytes 614408 | tf_op jit(solution)/shard_map/ppermute | solution.py:35
  31.0 6.8 %collective-permute-start.10 = (bf16[800,128]{1,0:T(8,128)(2,1)S(1)}, bf16[800,128]{1,0:T(8,128)(2,1)S(1)}, u32[]{:S(2)}, u32[]{:S(2)}) collective-permute-start(bf16[800,128]{1,0:T(8,128)(2,1)S(1)} %collective-permute-done.9.refs_10_.refs_8_), channel_id=1, source_target_pairs={{0,1},{1,0},{2,3},{3,2},{4,5},{5,4},{6,7},{7,6},{8,9},{9,8},{10,11... | collective-permute-start | bytes 614408 | tf_op jit(solution)/shard_map/ppermute | solution.py:35
  31.5 9.6 %collective-permute-start.14 = (bf16[640,256]{1,0:T(8,128)(2,1)S(1)}, bf16[640,256]{1,0:T(8,128)(2,1)S(1)}, u32[]{:S(2)}, u32[]{:S(2)}) collective-permute-start(bf16[640,256]{1,0:T(8,128)(2,1)S(1)} %get-tuple-element.46.refs_0_), channel_id=1, source_target_pairs={{0,2},{1,3},{2,0},{3,1},{4,6},{5,7},{6,4},{7,5},{8,10},{9,11},{10,... | collective-permute-start | bytes 983048 | tf_op jit(solution)/shard_map/ppermute | solution.py:35
  33.0 10.4 %collective-permute-start.12 = (bf16[480,256]{1,0:T(8,128)(2,1)S(1)}, bf16[480,256]{1,0:T(8,128)(2,1)S(1)}, u32[]{:S(2)}, u32[]{:S(2)}) collective-permute-start(bf16[480,256]{1,0:T(8,128)(2,1)S(1)} %get-tuple-element.63), channel_id=1, source_target_pairs={{0,4},{4,8},{8,12},{12,16},{16,20},{20,24},{24,28},{28,0},{1,5},{5... | collective-permute-start | bytes 737288 | tf_op jit(solution)/shard_map/ppermute | solution.py:30
  33.0 13.1 %collective-permute-start.13 = (bf16[480,256]{1,0:T(8,128)(2,1)S(1)}, bf16[480,256]{1,0:T(8,128)(2,1)S(1)}, u32[]{:S(2)}, u32[]{:S(2)}) collective-permute-start(bf16[480,256]{1,0:T(8,128)(2,1)S(1)} %get-tuple-element.65), channel_id=1, source_target_pairs={{0,28},{4,0},{8,4},{12,8},{16,12},{20,16},{24,20},{28,24},{1,29},{... | collective-permute-start | bytes 737288 | tf_op jit(solution)/shard_map/ppermute | solution.py:30
  40.5 12.6 %collective-permute-start.17 = (bf16[960,256]{1,0:T(8,128)(2,1)S(1)}, bf16[960,256]{1,0:T(8,128)(2,1)S(1)}, u32[]{:S(2)}, u32[]{:S(2)}) collective-permute-start(bf16[960,256]{1,0:T(8,128)(2,1)S(1)} %get-tuple-element.61.refs_2_.refs_4_), channel_id=1, source_target_pairs={{0,2},{1,3},{2,0},{3,1},{4,6},{5,7},{6,4},{7,5},{8,10},{9,11},{10,... | collective-permute-start | bytes 1474568 | tf_op jit(solution)/shard_map/ppermute | solution.py:35
  41.1 24.8 %copy-start.4 = (bf16[640,256]{1,0:T(8,128)(2,1)}, bf16[640,256]{1,0:T(8,128)(2,1)S(1)}, u32[]{:S(2)}) copy-start(bf16[640,256]{1,0:T(8,128)(2,1)S(1)} %collective-permute-done.14.refs_3_.refs_2_) | copy-start | bytes 983044
  49.5 6.0 %collective-permute-start.15 = (bf16[976,256]{1,0:T(8,128)(2,1)S(1)}, bf16[976,256]{1,0:T(8,128)(2,1)S(1)}, u32[]{:S(2)}, u32[]{:S(2)}) collective-permute-start(bf16[976,256]{1,0:T(8,128)(2,1)S(1)} %get-tuple-element.70.refs_4_.refs_8_), channel_id=1, source_target_pairs={{0,1},{1,0},{2,3},{3,2},{4,5},{5,4},{6,7},{7,6},{8,9},{9,8},{10,11... | collective-permute-start | bytes 1499144 | tf_op jit(solution)/shard_map/ppermute | solution.py:35
  49.5 14.1 %collective-permute-start.19 = (bf16[976,256]{1,0:T(8,128)(2,1)S(1)}, bf16[976,256]{1,0:T(8,128)(2,1)S(1)}, u32[]{:S(2)}, u32[]{:S(2)}) collective-permute-start(bf16[976,256]{1,0:T(8,128)(2,1)S(1)} %get-tuple-element.70.refs_4_.refs_8_), channel_id=1, source_target_pairs={{0,2},{1,3},{2,0},{3,1},{4,6},{5,7},{6,4},{7,5},{8,10},{9,11},{10,... | collective-permute-start | bytes 1499144 | tf_op jit(solution)/shard_map/ppermute | solution.py:35
  50.0 5.5 %collective-permute-start.11 = (bf16[960,256]{1,0:T(8,128)(2,1)S(1)}, bf16[960,256]{1,0:T(8,128)(2,1)S(1)}, u32[]{:S(2)}, u32[]{:S(2)}) collective-permute-start(bf16[960,256]{1,0:T(8,128)(2,1)S(1)} %get-tuple-element.61.refs_2_.refs_4_), channel_id=1, source_target_pairs={{0,1},{1,0},{2,3},{3,2},{4,5},{5,4},{6,7},{7,6},{8,9},{9,8},{10,11... | collective-permute-start | bytes 1474568 | tf_op jit(solution)/shard_map/ppermute | solution.py:35
  53.1 10.5 %collective-permute-start.18 = (bf16[960,256]{1,0:T(8,128)(2,1)S(1)}, bf16[960,256]{1,0:T(8,128)(2,1)S(1)}, u32[]{:S(2)}, u32[]{:S(2)}) collective-permute-start(bf16[960,256]{1,0:T(8,128)(2,1)S(1)} %collective-permute-done.17.refs_5_.refs_6_), channel_id=1, source_target_pairs={{0,1},{1,0},{2,3},{3,2},{4,5},{5,4},{6,7},{7,6},{8,9},{9,8},{10,11... | collective-permute-start | bytes 1474568 | tf_op jit(solution)/shard_map/ppermute | solution.py:35
  53.1 2.3 %collective-permute-start = (bf16[640,256]{1,0:T(8,128)(2,1)S(1)}, bf16[640,256]{1,0:T(8,128)(2,1)S(1)}, u32[]{:S(2)}, u32[]{:S(2)}) collective-permute-start(bf16[640,256]{1,0:T(8,128)(2,1)S(1)} %get-tuple-element.46.refs_0_), channel_id=1, source_target_pairs={{0,1},{1,0},{2,3},{3,2},{4,5},{5,4},{6,7},{7,6},{8,9},{9,8},{10,11... | collective-permute-start | bytes 983048 | tf_op jit(solution)/shard_map/ppermute | solution.py:35
  63.6 2.4 %collective-permute-start.20 = (bf16[976,256]{1,0:T(8,128)(2,1)S(1)}, bf16[976,256]{1,0:T(8,128)(2,1)S(1)}, u32[]{:S(2)}, u32[]{:S(2)}) collective-permute-start(bf16[976,256]{1,0:T(8,128)(2,1)S(1)} %collective-permute-done.19.refs_7_.refs_10_), channel_id=1, source_target_pairs={{0,1},{1,0},{2,3},{3,2},{4,5},{5,4},{6,7},{7,6},{8,9},{9,8},{10,11... | collective-permute-start | bytes 1499144 | tf_op jit(solution)/shard_map/ppermute | solution.py:35
  63.6 2.3 %collective-permute-start.16 = (bf16[640,256]{1,0:T(8,128)(2,1)S(1)}, bf16[640,256]{1,0:T(8,128)(2,1)S(1)}, u32[]{:S(2)}, u32[]{:S(2)}) collective-permute-start(bf16[640,256]{1,0:T(8,128)(2,1)S(1)} %collective-permute-done.14.refs_3_.refs_2_), channel_id=1, source_target_pairs={{0,1},{1,0},{2,3},{3,2},{4,5},{5,4},{6,7},{7,6},{8,9},{9,8},{10,11... | collective-permute-start | bytes 983048 | tf_op jit(solution)/shard_map/ppermute | solution.py:35
  80.7 9.3 %collective-permute-start.21 = (bf16[64,1152]{1,0:T(8,128)(2,1)}, bf16[64,1152]{1,0:T(8,128)(2,1)}, u32[]{:S(2)}, u32[]{:S(2)}) collective-permute-start(bf16[64,1152]{1,0:T(8,128)(2,1)} %get-tuple-element.76), channel_id=1, source_target_pairs={{0,16},{4,20},{8,24},{12,28},{16,0},{20,4},{24,8},{28,12},{1,17},{... | collective-permute-start | bytes 442376 | tf_op jit(solution)/shard_map/ppermute | solution.py:30
  (15 other events, 155.0 us)

commit v5 on v4

--- a/solution.py
+++ b/solution.py
@@ -301,18 +301,15 @@
     return jnp.concatenate([high, squares - high, spare])
 
 
-def sums_kernel(got_ref, mine_ref, send_ref):
+def sums_kernel(got_ref, out_ref):
     shares, rows, wide = got_ref.shape
     bands = wide - LANES
     parts = bands // LANES
     total = got_ref[0].astype(F32)
     for share in range(1, shares):
         total = total + got_ref[share].astype(F32)
-    tail = halves(total[:parts, bands:] + total[parts : 2 * parts, bands:], rows)
-    mine_ref[:, :bands] = total[:, :bands]
-    mine_ref[:, bands:] = tail
-    send_ref[:, :bands] = total[:, :bands].astype(BF16)
-    send_ref[:, bands:] = tail.astype(BF16)
+    out_ref[:, :bands] = total[:, :bands].astype(BF16)
+    out_ref[:, bands:] = halves(total[:parts, bands:] + total[parts : 2 * parts, bands:], rows).astype(BF16)
 
 
 def weights_kernel(total_columns, blocks, me_ref, mine_ref, other_ref, out_ref):
@@ -321,7 +318,7 @@
     bands = wide - LANES
     local = bands // blocks
     parts = bands // LANES
-    total = mine_ref[...] + other_ref[...].astype(F32)
+    total = mine_ref[...].astype(F32) + other_ref[...].astype(F32)
     tail = total[:, bands:]
     squares = tail[:parts, :] + tail[parts : 2 * parts, :]
     scales = lax.rsqrt(squares + epsilon_norm)
@@ -516,17 +513,16 @@
     upper.append(lower_blocks(after(across[-1], upper[-1][-1], early)))
     (late,) = gram(False, early, turned, tails, *[block for blocks in upper for block in blocks])
     got = lax.all_to_all(late, "elem", 0, 0, tiled=True, axis_index_groups=groups)
-    sums = jax.ShapeDtypeStruct((slice_rows, all_bands + LANES), F32)
-    mine, send = pl.pallas_call(
+    mine = pl.pallas_call(
         sums_kernel,
-        out_shape=[sums, jax.ShapeDtypeStruct(sums.shape, BF16)],
+        out_shape=jax.ShapeDtypeStruct((slice_rows, all_bands + LANES), BF16),
         in_specs=[VMEM],
-        out_specs=[VMEM] * 2,
+        out_specs=VMEM,
         compiler_params=params(8),
         cost_estimate=about(0.01),
         name="sums",
     )(got)
-    other = from_behind(send, "elem", group)
+    other = from_behind(mine, "elem", group)
     weights = pl.pallas_call(
         functools.partial(weights_kernel, total_columns, band_size),
         out_shape=jax.ShapeDtypeStruct((group, slice_rows, all_bands), BF16),

time: 106 us -> 104 us (0.981)
  local copies, waits for them, and re-layouts: 1.78 us -> 0.06 us
    unnamed x34 -> x30, local copies, waits for them, and re-layouts: 1.78 us -> 0.06 us
where the time goes in v5:
time: 104 us
  waiting for transfers between devices  30.4 us (29%)
  Pallas kernels  26.6 us (26%)
  starting transfers between devices  23.5 us (23%)
  blocking collectives  23 us (22%)
    ppermute x7, starting transfers between devices, from_behind(): return lax.ppermute(value, axis, pairs)  16.6 us
    ppermute x15, waiting for transfers between devices, swap(): lax.ppermute(value, axis, [(source, source ^ bit) for source in range(cou...  15.2 us
    ppermute x7, waiting for transfers between devices, from_behind(): return lax.ppermute(value, axis, pairs)  15.2 us
    all_to_all x1, blocking collectives, fast_shards(): lax.all_to_all(late, 'elem', 0, 0, tiled=True, axis_index_groups=groups)  12.4 us
    all_to_all x1, blocking collectives, fast_shards(): lax.all_to_all(weights, 'elem', 0, 0, tiled=True, axis_index_groups=groups)  10.7 us
    ppermute x15, starting transfers between devices, swap(): lax.ppermute(value, axis, [(source, source ^ bit) for source in range(cou...  6.93 us
    pallas_call x2, Pallas kernels, fast_shards(): pl.pallas_call(functools.partial(strip_kernel, n, count, strip, offset, l...  6.1 us
    pallas_call x1, Pallas kernels, fast_shards(): pl.pallas_call(functools.partial(interior_kernel, n, count, SPLIT, DEGREE...  3.98 us
  transfers between devices with their start and end apart: 22, of which 9 were waited for; matrix products, arithmetic and copies ran while one was open for 0% of the time, Pallas kernels for 17%

profile of v5, /device:TPU:0, one launch (start us, length us, event | category | flops | bytes accessed | tf_op | source)
XLA Modules:
  0.0 103.9 jit_solution(7126985244512009069)
XLA Ops:
  0.0 3.1 %ends.1 = (bf16[800,128]{1,0:T(8,128)(2,1)}, bf16[800,128]{1,0:T(8,128)(2,1)}) custom-call(s32[1]{0:T(128)} %bitcast.1.me_ref, s32[16]{0:T(128)} %sizes_ref.3, s32[16]{0:T(128)} %pattern_ref, bf16[16,160,160]{2,1,0:T(8,128)(2,1)} %diag_ref.1, bf16[16,160,160]{2,1,0:T(8,128)(2,1)} %couple_ref.1), custom_call_target="tpu_custom_call" | custom-call | flops 11500000 | bytes 1 | tf_op jit(solution)/shard_map/ends/pallas_call | solution.py:387
  3.2 6.0 %collective-permute-start.5 = (bf16[800,128]{1,0:T(8,128)(2,1)}, bf16[800,128]{1,0:T(8,128)(2,1)S(1)}, u32[]{:S(2)}, u32[]{:S(2)}) collective-permute-start(bf16[800,128]{1,0:T(8,128)(2,1)} %get-tuple-element.39), channel_id=1, source_target_pairs={{0,28},{4,0},{8,4},{12,8},{16,12},{20,16},{24,20},{28,24},{1,29},{... | collective-permute-start | bytes 614408 | tf_op jit(solution)/shard_map/ppermute | solution.py:30
  10.3 2.1 %rows.1.rows_ref = bf16[16,160,512]{2,1,0:T(8,128)(2,1)S(1)} custom-call(s32[16]{0:T(128)S(1)} %copy-done.13, s32[16]{0:T(128)S(1)} %copy-done.14, bf16[16,160,160]{2,1,0:T(8,128)(2,1)S(1)} %copy-done, bf16[16,160,160]{2,1,0:T(8,128)(2,1)S(1)} %copy-done.1), custom_call_target="tpu_custom_call" | custom-call | flops 11500000 | bytes 1 | tf_op jit(solution)/shard_map/rows/pallas_call | solution.py:399
  12.3 3.4 %interior_first.1 = (bf16[2,320,256]{2,1,0:T(8,128)(2,1)S(1)}, bf16[2,320,256]{2,1,0:T(8,128)(2,1)S(1)}, bf16[2560,256]{1,0:T(8,128)(2,1)S(1)}, bf16[2560,256]{1,0:T(8,128)(2,1)S(1)}) custom-call(bf16[16,160,512]{2,1,0:T(8,128)(2,1)S(1)} %rows.1.rows_ref, bf16[2560,256]{1,0:T(8,128)(2,1)S(1)} %get-tuple-element.41.refs_0_), custom_call_target="tpu_custom_call" | custom-call | flops 11500000 | bytes 1 | tf_op jit(solution)/shard_map/interior_first/pallas_call | solution.py:429
  15.9 4.8 %collective-permute-start.2 = (bf16[480,256]{1,0:T(8,128)(2,1)S(1)}, bf16[480,256]{1,0:T(8,128)(2,1)S(1)}, u32[]{:S(2)}, u32[]{:S(2)}) collective-permute-start(bf16[480,256]{1,0:T(8,128)(2,1)S(1)} %get-tuple-element.48), channel_id=1, source_target_pairs={{0,28},{4,0},{8,4},{12,8},{16,12},{20,16},{24,20},{28,24},{1,29},{... | collective-permute-start | bytes 737288 | tf_op jit(solution)/shard_map/ppermute | solution.py:30
  20.6 1.5 %collective-permute-start.9 = (bf16[800,128]{1,0:T(8,128)(2,1)S(1)}, bf16[800,128]{1,0:T(8,128)(2,1)S(1)}, u32[]{:S(2)}, u32[]{:S(2)}) collective-permute-start(bf16[800,128]{1,0:T(8,128)(2,1)S(1)} %collective-permute-done.5.refs_6_.refs_4_), channel_id=1, source_target_pairs={{0,2},{1,3},{2,0},{3,1},{4,6},{5,7},{6,4},{7,5},{8,10},{9,11},{10,... | collective-permute-start | bytes 614408 | tf_op jit(solution)/shard_map/ppermute | solution.py:35
  22.7 4.0 %interior_rest.1 = (bf16[4,320,256]{2,1,0:T(8,128)(2,1)S(1)}, bf16[4,320,256]{2,1,0:T(8,128)(2,1)S(1)}, bf16[640,256]{1,0:T(8,128)(2,1)S(1)}, f32[1,256]{1,0:T(1,128)S(1)}) custom-call(bf16[16,160,512]{2,1,0:T(8,128)(2,1)S(1)} %rows.1.rows_ref, bf16[2560,256]{1,0:T(8,128)(2,1)S(1)} %get-tuple-element.42.refs_0_, bf16[2560,256]{1,0:T(8,128)(2,1)S(1)} %get-tuple-element.43.refs_1_), custom_call_target="tpu_custom_call" | custom-call | flops 11500000 | bytes 1 | tf_op jit(solution)/shard_map/interior_rest/pallas_call | solution.py:443
  27.2 2.0 %collective-permute-done.2.right_y_ref = bf16[480,256]{1,0:T(8,128)(2,1)S(1)} collective-permute-done((bf16[480,256]{1,0:T(8,128)(2,1)S(1)}, bf16[480,256]{1,0:T(8,128)(2,1)S(1)}, u32[]{:S(2)}, u32[]{:S(2)}) %collective-permute-start.2) | collective-permute-done | bytes 245792 | tf_op jit(solution)/shard_map/ppermute | solution.py:30
  29.2 1.8 %collective-permute-done.7.refs_8_.refs_6_ = bf16[800,128]{1,0:T(8,128)(2,1)S(1)} collective-permute-done((bf16[800,128]{1,0:T(8,128)(2,1)S(1)}, bf16[800,128]{1,0:T(8,128)(2,1)S(1)}, u32[]{:S(2)}, u32[]{:S(2)}) %collective-permute-start.7) | collective-permute-done | bytes 204832 | tf_op jit(solution)/shard_map/ppermute | solution.py:35
  31.5 1.5 %collective-permute-start.14 = (bf16[640,256]{1,0:T(8,128)(2,1)S(1)}, bf16[640,256]{1,0:T(8,128)(2,1)S(1)}, u32[]{:S(2)}, u32[]{:S(2)}) collective-permute-start(bf16[640,256]{1,0:T(8,128)(2,1)S(1)} %get-tuple-element.44.refs_0_), channel_id=1, source_target_pairs={{0,2},{1,3},{2,0},{3,1},{4,6},{5,7},{6,4},{7,5},{8,10},{9,11},{10,... | collective-permute-start | bytes 983048 | tf_op jit(solution)/shard_map/ppermute | solution.py:35
  33.0 4.7 %collective-permute-start.13 = (bf16[480,256]{1,0:T(8,128)(2,1)S(1)}, bf16[480,256]{1,0:T(8,128)(2,1)S(1)}, u32[]{:S(2)}, u32[]{:S(2)}) collective-permute-start(bf16[480,256]{1,0:T(8,128)(2,1)S(1)} %get-tuple-element.63), channel_id=1, source_target_pairs={{0,28},{4,0},{8,4},{12,8},{16,12},{20,16},{24,20},{28,24},{1,29},{... | collective-permute-start | bytes 737288 | tf_op jit(solution)/shard_map/ppermute | solution.py:30
  37.8 2.7 %strip.2 = (bf16[960,256]{1,0:T(8,128)(2,1)S(1)}, bf16[6,320,256]{2,1,0:T(8,128)(2,1)S(1)}, bf16[6,320,256]{2,1,0:T(8,128)(2,1)S(1)}, f32[1,256]{1,0:T(1,128)S(1)}) custom-call(s32[1]{0:T(128)} %bitcast.1.me_ref, bf16[480,256]{1,0:T(8,128)(2,1)S(1)} %collective-permute-done.1.left_y_ref, bf16[480,256]{1,0:T(8,128)(2,1)S(1)} %collective-permute-done.2.right_y_ref, ...), custom_call_target="tpu_custom_call" | custom-call | flops 3449999872 | bytes 1 | tf_op jit(solution)/shard_map/strip/pallas_call | solution.py:472
  41.1 2.3 %collective-permute-done.12.left_y_ref = bf16[480,256]{1,0:T(8,128)(2,1)S(1)} collective-permute-done((bf16[480,256]{1,0:T(8,128)(2,1)S(1)}, bf16[480,256]{1,0:T(8,128)(2,1)S(1)}, u32[]{:S(2)}, u32[]{:S(2)}) %collective-permute-start.12) | collective-permute-done | bytes 245792 | tf_op jit(solution)/shard_map/ppermute | solution.py:30
  43.4 2.7 %collective-permute-done.13.right_y_ref = bf16[480,256]{1,0:T(8,128)(2,1)S(1)} collective-permute-done((bf16[480,256]{1,0:T(8,128)(2,1)S(1)}, bf16[480,256]{1,0:T(8,128)(2,1)S(1)}, u32[]{:S(2)}, u32[]{:S(2)}) %collective-permute-start.13) | collective-permute-done | bytes 245792 | tf_op jit(solution)/shard_map/ppermute | solution.py:30
  46.1 3.4 %strip.3 = (bf16[976,256]{1,0:T(8,128)(2,1)S(1)}, f32[8,128]{1,0:T(8,128)}, f32[8,128]{1,0:T(8,128)}, f32[1,256]{1,0:T(1,128)}) custom-call(s32[1]{0:T(128)} %bitcast.1.me_ref, bf16[480,256]{1,0:T(8,128)(2,1)S(1)} %collective-permute-done.12.left_y_ref, bf16[480,256]{1,0:T(8,128)(2,1)S(1)} %collective-permute-done.13.right_y_ref, ...), custom_call_target="tpu_custom_call" | custom-call | flops 3449999872 | bytes 1 | tf_op jit(solution)/shard_map/strip/pallas_call | solution.py:472
  50.2 2.9 %collective-permute-done.17.refs_5_.refs_6_ = bf16[960,256]{1,0:T(8,128)(2,1)S(1)} collective-permute-done((bf16[960,256]{1,0:T(8,128)(2,1)S(1)}, bf16[960,256]{1,0:T(8,128)(2,1)S(1)}, u32[]{:S(2)}, u32[]{:S(2)}) %collective-permute-start.17) | collective-permute-done | bytes 491552 | tf_op jit(solution)/shard_map/ppermute | solution.py:35
  53.6 1.8 %collective-permute-done.refs_1_ = bf16[640,256]{1,0:T(8,128)(2,1)S(1)} collective-permute-done((bf16[640,256]{1,0:T(8,128)(2,1)S(1)}, bf16[640,256]{1,0:T(8,128)(2,1)S(1)}, u32[]{:S(2)}, u32[]{:S(2)}) %collective-permute-start) | collective-permute-done | bytes 327712 | tf_op jit(solution)/shard_map/ppermute | solution.py:35
  55.4 1.3 %gram_early.1 = (bf16[4,64,512]{2,1,0:T(8,128)(2,1)S(1)}, bf16[2,16,256]{2,1,0:T(8,128)(2,1)S(1)}, bf16[256,2560]{1,0:T(8,128)(2,1)S(1)}) custom-call(bf16[640,256]{1,0:T(8,128)(2,1)S(1)} %get-tuple-element.44.refs_0_, bf16[640,256]{1,0:T(8,128)(2,1)S(1)} %collective-permute-done.refs_1_, bf16[960,256]{1,0:T(8,128)(2,1)S(1)} %get-tuple-element.59.refs_2_.refs_4_, ...), custom_call_target="tpu_custom_call" | custom-call | flops 11500000 | bytes 1 | tf_op jit(solution)/shard_map/gram_early/pallas_call | solution.py:500
  56.7 6.9 %collective-permute-done.19.refs_7_.refs_10_ = bf16[976,256]{1,0:T(8,128)(2,1)S(1)} collective-permute-done((bf16[976,256]{1,0:T(8,128)(2,1)S(1)}, bf16[976,256]{1,0:T(8,128)(2,1)S(1)}, u32[]{:S(2)}, u32[]{:S(2)}) %collective-permute-start.19) | collective-permute-done | bytes 499744 | tf_op jit(solution)/shard_map/ppermute | solution.py:35
  64.1 1.8 %collective-permute-done.16.refs_4_.refs_3_ = bf16[640,256]{1,0:T(8,128)(2,1)S(1)} collective-permute-done((bf16[640,256]{1,0:T(8,128)(2,1)S(1)}, bf16[640,256]{1,0:T(8,128)(2,1)S(1)}, u32[]{:S(2)}, u32[]{:S(2)}) %collective-permute-start.16) | collective-permute-done | bytes 327712 | tf_op jit(solution)/shard_map/ppermute | solution.py:35
  66.9 12.4 %all_to_all.10.got_ref = bf16[4,64,1152]{2,1,0:T(8,128)(2,1)S(1)} all-to-all(bf16[4,64,1152]{2,1,0:T(8,128)(2,1)S(1)} %gram_late.1), channel_id=1, replica_groups={{0,4,8,12},{16,20,24,28},{1,5,9,13},{17,21,25,29},{2,6,10,14},{18,22,26..., dimensions={0} | all-to-all | bytes 1179648 | tf_op jit(solution)/shard_map/all_to_all | solution.py:515
  81.0 8.2 %collective-permute-done.21.other_ref = bf16[64,1152]{1,0:T(8,128)(2,1)} collective-permute-done((bf16[64,1152]{1,0:T(8,128)(2,1)}, bf16[64,1152]{1,0:T(8,128)(2,1)}, u32[]{:S(2)}, u32[]{:S(2)}) %collective-permute-start.21) | collective-permute-done | bytes 147488 | tf_op jit(solution)/shard_map/ppermute | solution.py:30
  90.4 10.7 %all_to_all.11 = bf16[4,64,1024]{2,1,0:T(8,128)(2,1)S(1)} all-to-all(bf16[4,64,1024]{2,1,0:T(8,128)(2,1)S(1)} %weights.1), channel_id=1, replica_groups={{0,4,8,12},{16,20,24,28},{1,5,9,13},{17,21,25,29},{2,6,10,14},{18,22,26..., dimensions={0} | all-to-all | bytes 1048576 | tf_op jit(solution)/shard_map/all_to_all | solution.py:536
  101.1 2.8 %rotate.1 = bf16[256,2560]{1,0:T(8,128)(2,1)} custom-call(bf16[256,1024]{1,0:T(8,128)(2,1)S(1)} %bitcast.3, bf16[640,256]{1,0:T(8,128)(2,1)S(1)} %copy-done.9, bf16[640,256]{1,0:T(8,128)(2,1)S(1)} %copy-done.11, bf16[640,256]{1,0:T(8,128)(2,1)S(1)} %copy-done.5, bf16[640,256]{1,0:T(8,128)(2,1)S(1)} %copy-done.7, ...), custom_call_target="tpu_custom_call" | custom-call | flops 11500000 | bytes 1 | tf_op jit(solution)/shard_map/rotate/pallas_call | solution.py:537
  (64 shorter events, 8.9 us)
Async XLA Ops:
  3.2 17.4 %collective-permute-start.5 = (bf16[800,128]{1,0:T(8,128)(2,1)}, bf16[800,128]{1,0:T(8,128)(2,1)S(1)}, u32[]{:S(2)}, u32[]{:S(2)}) collective-permute-start(bf16[800,128]{1,0:T(8,128)(2,1)} %get-tuple-element.39), channel_id=1, source_target_pairs={{0,28},{4,0},{8,4},{12,8},{16,12},{20,16},{24,20},{28,24},{1,29},{... | collective-permute-start | bytes 614408 | tf_op jit(solution)/shard_map/ppermute | solution.py:30
  9.2 12.9 %collective-permute-start.3 = (bf16[800,128]{1,0:T(8,128)(2,1)}, bf16[800,128]{1,0:T(8,128)(2,1)S(1)}, u32[]{:S(2)}, u32[]{:S(2)}) collective-permute-start(bf16[800,128]{1,0:T(8,128)(2,1)} %get-tuple-element.54), channel_id=1, source_target_pairs={{0,4},{4,8},{8,12},{12,16},{16,20},{20,24},{24,28},{28,0},{1,5},{5... | collective-permute-start | bytes 614408 | tf_op jit(solution)/shard_map/ppermute | solution.py:30
  15.8 10.9 %collective-permute-start.1 = (bf16[480,256]{1,0:T(8,128)(2,1)S(1)}, bf16[480,256]{1,0:T(8,128)(2,1)S(1)}, u32[]{:S(2)}, u32[]{:S(2)}) collective-permute-start(bf16[480,256]{1,0:T(8,128)(2,1)S(1)} %get-tuple-element.46), channel_id=1, source_target_pairs={{0,4},{4,8},{8,12},{12,16},{16,20},{20,24},{24,28},{28,0},{1,5},{5... | collective-permute-start | bytes 737288 | tf_op jit(solution)/shard_map/ppermute | solution.py:30
  15.9 13.3 %collective-permute-start.2 = (bf16[480,256]{1,0:T(8,128)(2,1)S(1)}, bf16[480,256]{1,0:T(8,128)(2,1)S(1)}, u32[]{:S(2)}, u32[]{:S(2)}) collective-permute-start(bf16[480,256]{1,0:T(8,128)(2,1)S(1)} %get-tuple-element.48), channel_id=1, source_target_pairs={{0,28},{4,0},{8,4},{12,8},{16,12},{20,16},{24,20},{28,24},{1,29},{... | collective-permute-start | bytes 737288 | tf_op jit(solution)/shard_map/ppermute | solution.py:30
  20.6 8.6 %collective-permute-start.9 = (bf16[800,128]{1,0:T(8,128)(2,1)S(1)}, bf16[800,128]{1,0:T(8,128)(2,1)S(1)}, u32[]{:S(2)}, u32[]{:S(2)}) collective-permute-start(bf16[800,128]{1,0:T(8,128)(2,1)S(1)} %collective-permute-done.5.refs_6_.refs_4_), channel_id=1, source_target_pairs={{0,2},{1,3},{2,0},{3,1},{4,6},{5,7},{6,4},{7,5},{8,10},{9,11},{10,... | collective-permute-start | bytes 614408 | tf_op jit(solution)/shard_map/ppermute | solution.py:35
  22.2 8.8 %collective-permute-start.7 = (bf16[800,128]{1,0:T(8,128)(2,1)S(1)}, bf16[800,128]{1,0:T(8,128)(2,1)S(1)}, u32[]{:S(2)}, u32[]{:S(2)}) collective-permute-start(bf16[800,128]{1,0:T(8,128)(2,1)S(1)} %collective-permute-done.3.refs_4_.refs_2_), channel_id=1, source_target_pairs={{0,2},{1,3},{2,0},{3,1},{4,6},{5,7},{6,4},{7,5},{8,10},{9,11},{10,... | collective-permute-start | bytes 614408 | tf_op jit(solution)/shard_map/ppermute | solution.py:35
  26.6 28.8 %copy-start.8 = (bf16[640,256]{1,0:T(8,128)(2,1)}, bf16[640,256]{1,0:T(8,128)(2,1)S(1)}, u32[]{:S(2)}) copy-start(bf16[640,256]{1,0:T(8,128)(2,1)S(1)} %get-tuple-element.44.refs_0_) | copy-start | bytes 983044
  26.7 6.4 %collective-permute-start.4 = (bf16[800,128]{1,0:T(8,128)(2,1)S(1)}, bf16[800,128]{1,0:T(8,128)(2,1)S(1)}, u32[]{:S(2)}, u32[]{:S(2)}) collective-permute-start(bf16[800,128]{1,0:T(8,128)(2,1)S(1)} %collective-permute-done.3.refs_4_.refs_2_), channel_id=1, source_target_pairs={{0,1},{1,0},{2,3},{3,2},{4,5},{5,4},{6,7},{7,6},{8,9},{9,8},{10,11... | collective-permute-start | bytes 614408 | tf_op jit(solution)/shard_map/ppermute | solution.py:35
  26.7 6.3 %collective-permute-start.6 = (bf16[800,128]{1,0:T(8,128)(2,1)S(1)}, bf16[800,128]{1,0:T(8,128)(2,1)S(1)}, u32[]{:S(2)}, u32[]{:S(2)}) collective-permute-start(bf16[800,128]{1,0:T(8,128)(2,1)S(1)} %collective-permute-done.5.refs_6_.refs_4_), channel_id=1, source_target_pairs={{0,1},{1,0},{2,3},{3,2},{4,5},{5,4},{6,7},{7,6},{8,9},{9,8},{10,11... | collective-permute-start | bytes 614408 | tf_op jit(solution)/shard_map/ppermute | solution.py:35
  31.0 6.8 %collective-permute-start.8 = (bf16[800,128]{1,0:T(8,128)(2,1)S(1)}, bf16[800,128]{1,0:T(8,128)(2,1)S(1)}, u32[]{:S(2)}, u32[]{:S(2)}) collective-permute-start(bf16[800,128]{1,0:T(8,128)(2,1)S(1)} %collective-permute-done.7.refs_8_.refs_6_), channel_id=1, source_target_pairs={{0,1},{1,0},{2,3},{3,2},{4,5},{5,4},{6,7},{7,6},{8,9},{9,8},{10,11... | collective-permute-start | bytes 614408 | tf_op jit(solution)/shard_map/ppermute | solution.py:35
  31.0 6.8 %collective-permute-start.10 = (bf16[800,128]{1,0:T(8,128)(2,1)S(1)}, bf16[800,128]{1,0:T(8,128)(2,1)S(1)}, u32[]{:S(2)}, u32[]{:S(2)}) collective-permute-start(bf16[800,128]{1,0:T(8,128)(2,1)S(1)} %collective-permute-done.9.refs_10_.refs_8_), channel_id=1, source_target_pairs={{0,1},{1,0},{2,3},{3,2},{4,5},{5,4},{6,7},{7,6},{8,9},{9,8},{10,11... | collective-permute-start | bytes 614408 | tf_op jit(solution)/shard_map/ppermute | solution.py:35
  31.5 9.6 %collective-permute-start.14 = (bf16[640,256]{1,0:T(8,128)(2,1)S(1)}, bf16[640,256]{1,0:T(8,128)(2,1)S(1)}, u32[]{:S(2)}, u32[]{:S(2)}) collective-permute-start(bf16[640,256]{1,0:T(8,128)(2,1)S(1)} %get-tuple-element.44.refs_0_), channel_id=1, source_target_pairs={{0,2},{1,3},{2,0},{3,1},{4,6},{5,7},{6,4},{7,5},{8,10},{9,11},{10,... | collective-permute-start | bytes 983048 | tf_op jit(solution)/shard_map/ppermute | solution.py:35
  33.0 10.4 %collective-permute-start.12 = (bf16[480,256]{1,0:T(8,128)(2,1)S(1)}, bf16[480,256]{1,0:T(8,128)(2,1)S(1)}, u32[]{:S(2)}, u32[]{:S(2)}) collective-permute-start(bf16[480,256]{1,0:T(8,128)(2,1)S(1)} %get-tuple-element.61), channel_id=1, source_target_pairs={{0,4},{4,8},{8,12},{12,16},{16,20},{20,24},{24,28},{28,0},{1,5},{5... | collective-permute-start | bytes 737288 | tf_op jit(solution)/shard_map/ppermute | solution.py:30
  33.0 13.1 %collective-permute-start.13 = (bf16[480,256]{1,0:T(8,128)(2,1)S(1)}, bf16[480,256]{1,0:T(8,128)(2,1)S(1)}, u32[]{:S(2)}, u32[]{:S(2)}) collective-permute-start(bf16[480,256]{1,0:T(8,128)(2,1)S(1)} %get-tuple-element.63), channel_id=1, source_target_pairs={{0,28},{4,0},{8,4},{12,8},{16,12},{20,16},{24,20},{28,24},{1,29},{... | collective-permute-start | bytes 737288 | tf_op jit(solution)/shard_map/ppermute | solution.py:30
  40.5 12.6 %collective-permute-start.17 = (bf16[960,256]{1,0:T(8,128)(2,1)S(1)}, bf16[960,256]{1,0:T(8,128)(2,1)S(1)}, u32[]{:S(2)}, u32[]{:S(2)}) collective-permute-start(bf16[960,256]{1,0:T(8,128)(2,1)S(1)} %get-tuple-element.59.refs_2_.refs_4_), channel_id=1, source_target_pairs={{0,2},{1,3},{2,0},{3,1},{4,6},{5,7},{6,4},{7,5},{8,10},{9,11},{10,... | collective-permute-start | bytes 1474568 | tf_op jit(solution)/shard_map/ppermute | solution.py:35
  41.1 24.8 %copy-start.4 = (bf16[640,256]{1,0:T(8,128)(2,1)}, bf16[640,256]{1,0:T(8,128)(2,1)S(1)}, u32[]{:S(2)}) copy-start(bf16[640,256]{1,0:T(8,128)(2,1)S(1)} %collective-permute-done.14.refs_3_.refs_2_) | copy-start | bytes 983044
  49.5 6.0 %collective-permute-start.15 = (bf16[976,256]{1,0:T(8,128)(2,1)S(1)}, bf16[976,256]{1,0:T(8,128)(2,1)S(1)}, u32[]{:S(2)}, u32[]{:S(2)}) collective-permute-start(bf16[976,256]{1,0:T(8,128)(2,1)S(1)} %get-tuple-element.68.refs_4_.refs_8_), channel_id=1, source_target_pairs={{0,1},{1,0},{2,3},{3,2},{4,5},{5,4},{6,7},{7,6},{8,9},{9,8},{10,11... | collective-permute-start | bytes 1499144 | tf_op jit(solution)/shard_map/ppermute | solution.py:35
  49.5 14.1 %collective-permute-start.19 = (bf16[976,256]{1,0:T(8,128)(2,1)S(1)}, bf16[976,256]{1,0:T(8,128)(2,1)S(1)}, u32[]{:S(2)}, u32[]{:S(2)}) collective-permute-start(bf16[976,256]{1,0:T(8,128)(2,1)S(1)} %get-tuple-element.68.refs_4_.refs_8_), channel_id=1, source_target_pairs={{0,2},{1,3},{2,0},{3,1},{4,6},{5,7},{6,4},{7,5},{8,10},{9,11},{10,... | collective-permute-start | bytes 1499144 | tf_op jit(solution)/shard_map/ppermute | solution.py:35
  50.0 5.4 %collective-permute-start.11 = (bf16[960,256]{1,0:T(8,128)(2,1)S(1)}, bf16[960,256]{1,0:T(8,128)(2,1)S(1)}, u32[]{:S(2)}, u32[]{:S(2)}) collective-permute-start(bf16[960,256]{1,0:T(8,128)(2,1)S(1)} %get-tuple-element.59.refs_2_.refs_4_), channel_id=1, source_target_pairs={{0,1},{1,0},{2,3},{3,2},{4,5},{5,4},{6,7},{7,6},{8,9},{9,8},{10,11... | collective-permute-start | bytes 1474568 | tf_op jit(solution)/shard_map/ppermute | solution.py:35
  53.1 10.5 %collective-permute-start.18 = (bf16[960,256]{1,0:T(8,128)(2,1)S(1)}, bf16[960,256]{1,0:T(8,128)(2,1)S(1)}, u32[]{:S(2)}, u32[]{:S(2)}) collective-permute-start(bf16[960,256]{1,0:T(8,128)(2,1)S(1)} %collective-permute-done.17.refs_5_.refs_6_), channel_id=1, source_target_pairs={{0,1},{1,0},{2,3},{3,2},{4,5},{5,4},{6,7},{7,6},{8,9},{9,8},{10,11... | collective-permute-start | bytes 1474568 | tf_op jit(solution)/shard_map/ppermute | solution.py:35
  53.1 2.3 %collective-permute-start = (bf16[640,256]{1,0:T(8,128)(2,1)S(1)}, bf16[640,256]{1,0:T(8,128)(2,1)S(1)}, u32[]{:S(2)}, u32[]{:S(2)}) collective-permute-start(bf16[640,256]{1,0:T(8,128)(2,1)S(1)} %get-tuple-element.44.refs_0_), channel_id=1, source_target_pairs={{0,1},{1,0},{2,3},{3,2},{4,5},{5,4},{6,7},{7,6},{8,9},{9,8},{10,11... | collective-permute-start | bytes 983048 | tf_op jit(solution)/shard_map/ppermute | solution.py:35
  63.6 2.4 %collective-permute-start.20 = (bf16[976,256]{1,0:T(8,128)(2,1)S(1)}, bf16[976,256]{1,0:T(8,128)(2,1)S(1)}, u32[]{:S(2)}, u32[]{:S(2)}) collective-permute-start(bf16[976,256]{1,0:T(8,128)(2,1)S(1)} %collective-permute-done.19.refs_7_.refs_10_), channel_id=1, source_target_pairs={{0,1},{1,0},{2,3},{3,2},{4,5},{5,4},{6,7},{7,6},{8,9},{9,8},{10,11... | collective-permute-start | bytes 1499144 | tf_op jit(solution)/shard_map/ppermute | solution.py:35
  63.6 2.3 %collective-permute-start.16 = (bf16[640,256]{1,0:T(8,128)(2,1)S(1)}, bf16[640,256]{1,0:T(8,128)(2,1)S(1)}, u32[]{:S(2)}, u32[]{:S(2)}) collective-permute-start(bf16[640,256]{1,0:T(8,128)(2,1)S(1)} %collective-permute-done.14.refs_3_.refs_2_), channel_id=1, source_target_pairs={{0,1},{1,0},{2,3},{3,2},{4,5},{5,4},{6,7},{7,6},{8,9},{9,8},{10,11... | collective-permute-start | bytes 983048 | tf_op jit(solution)/shard_map/ppermute | solution.py:35
  80.0 9.3 %collective-permute-start.21 = (bf16[64,1152]{1,0:T(8,128)(2,1)}, bf16[64,1152]{1,0:T(8,128)(2,1)}, u32[]{:S(2)}, u32[]{:S(2)}) collective-permute-start(bf16[64,1152]{1,0:T(8,128)(2,1)} %sums.1.mine_ref), channel_id=1, source_target_pairs={{0,16},{4,20},{8,24},{12,28},{16,0},{20,4},{24,8},{28,12},{1,17},{... | collective-permute-start | bytes 442376 | tf_op jit(solution)/shard_map/ppermute | solution.py:30
  (13 other events, 148.8 us)

commit v6 on v5

--- a/solution.py
+++ b/solution.py
@@ -63,11 +63,15 @@
         behind = jnp.transpose(couple)
 
 
-def ends_kernel(wide, me_ref, sizes_in, pattern_in, diag_in, couple_in, first_ref, last_ref, *scratch):
-    sizes_ref, pattern_ref, diag_ref, couple_ref, row_ref, sems = scratch
+def packed_width(blocks, width):
+    return -(-(blocks * width + DEGREE - 1) // LANES) * LANES
+
+
+def ends_kernel(me_ref, sizes_in, pattern_in, diag_in, couple_in, first_ref, last_ref, *scratch):
+    sizes_ref, pattern_ref, diag_ref, couple_ref, whole_first, whole_last, sems = scratch
     count, n, _ = diag_in.shape
     depth = DEGREE - 1
-    lanes = first_ref.shape[1]
+    share = first_ref.shape[0]
     low, high, before = pl.ds(0, depth), pl.ds(count - depth, depth), pl.ds(count - depth - 1, depth + 1)
     pairs = [(sizes_in, sizes_ref), (pattern_in, pattern_ref)]
     pairs += [(couple_in.at[low], couple_ref.at[low]), (diag_in.at[low], diag_ref.at[low])]
@@ -75,27 +79,30 @@
     copies = [pltpu.make_async_copy(source, target, sems.at[k]) for k, (source, target) in enumerate(pairs)]
     for copy in copies:
         copy.start()
-    at = pl.ds(pl.multiple_of(me_ref[0] * lanes, lanes), lanes)
-
-    def coupled(e):
-        return couple_ref[e].astype(F32) * pattern_ref[e].astype(F32)
+    place = lax.broadcasted_iota(jnp.int32, (n, n), 0)
+
+    def pack(target, out_ref, coupled, elements):
+        blocks = []
+        for e in coupled:
+            block = couple_ref[e].astype(F32) * pattern_ref[e].astype(F32)
+            blocks.append(jnp.where(place < sizes_ref[e], block, 0.0))
+        for e in elements:
+            blocks.append(jnp.where(place < sizes_ref[e], diag_ref[e].astype(F32), 0.0))
+        rest = (n, target.shape[1] - len(blocks) * n)
+        row, lane = lax.broadcasted_iota(jnp.int32, rest, 0), lax.broadcasted_iota(jnp.int32, rest, 1)
+        extra = jnp.zeros(rest, F32)
+        for index, e in enumerate(elements):
+            extra = jnp.where((lane == index) & (row < sizes_ref[e]), 1.0, extra)
+        target[...] = jnp.concatenate([*blocks, extra], axis=1)
+        own = pl.ds(pl.multiple_of(me_ref[0] * share, 8), share)
+        out_ref[...] = target[own, :].astype(BF16)
 
     for copy in copies[:4]:
         copy.wait()
-    behind = jnp.zeros((n, n), F32)
-    for e in range(depth):
-        couple = coupled(e)
-        row_ref[e] = joined(behind, diag_ref[e], couple, sizes_ref[e], wide)
-        first_ref[e * n : (e + 1) * n, :] = row_ref[e, :, at]
-        behind = jnp.transpose(couple)
+    pack(whole_first, first_ref, range(depth), range(depth))
     for copy in copies[4:]:
         copy.wait()
-    behind = jnp.transpose(coupled(count - depth - 1))
-    for e in range(depth):
-        couple = coupled(count - depth + e)
-        row_ref[depth + e] = joined(behind, diag_ref[count - depth + e], couple, sizes_ref[count - depth + e], wide)
-        last_ref[e * n : (e + 1) * n, :] = row_ref[depth + e, :, at]
-        behind = jnp.transpose(couple)
+    pack(whole_last, last_ref, range(count - depth - 1, count), range(count - depth, count))
 
 
 def vectors_kernel(width, count, group, sizes_ref, bands_ref, out_ref, *edge_refs):
@@ -186,36 +193,46 @@
     n = width
     depth = DEGREE - 1
     me = me_ref[0]
-    refs, outs = refs[:-8], refs[-8:]
+    refs, outs = refs[:-10], refs[-10:]
     half = len(edge_sizes)
     left_edge = [ref.at[k] for ref, size in zip(refs[:half], edge_sizes) for k in range(size)]
     right_edge = [ref.at[k] for ref, size in zip(refs[half : 2 * half], edge_sizes) for k in range(size)]
     refs = refs[2 * half :]
-    out_ref, left_out_ref, right_out_ref, squares_ref, left_scr, right_scr, halo_left, halo_right = outs
-    lanes = refs[0].shape[1]
+    out_ref, left_out_ref, right_out_ref, squares_ref, left_scr, right_scr, *scratch = outs
+    halo_left, halo_right, packed_left, packed_right = scratch
+    share = refs[0].shape[0]
     for index in range(pieces):
         for side in range(2):
-            at = pl.ds(pl.multiple_of((me ^ (side * pieces + index)) * lanes, lanes), lanes)
-            halo_left[:, :, at] = refs[2 * side * pieces + index][...].reshape(depth, n, lanes)
-            halo_right[:, :, at] = refs[(2 * side + 1) * pieces + index][...].reshape(depth, n, lanes)
+            at = pl.ds(pl.multiple_of((me ^ (side * pieces + index)) * share, 8), share)
+            packed_left[at, :] = refs[2 * side * pieces + index][...].astype(F32)
+            packed_right[at, :] = refs[(2 * side + 1) * pieces + index][...].astype(F32)
+
+    def piece(ref, block):
+        return ref[:, block * n : (block + 1) * n]
+
+    def valid(ref, blocks, index):
+        return ref[:, blocks * n + index : blocks * n + index + 1]
+
+    for index in range(max(depth + offset + 1, 0), depth):
+        turned = jnp.transpose(piece(packed_left, index)) * valid(packed_left, 2 * depth + 1, index)
+        parts = [turned, piece(packed_left, depth + 1 + index), piece(packed_left, index + 1)]
+        halo_left[index, :, : 3 * n] = jnp.concatenate(parts, axis=1).astype(BF16)
+    turned = jnp.transpose(piece(packed_left, depth)) * rows_ref[0, :, 3 * n : 3 * n + 1].astype(F32)
+    halo_left[depth, :, : 3 * n] = jnp.concatenate([turned.astype(BF16), rows_ref[0, :, n : 3 * n]], axis=1)
+    for index in range(min(-offset - 1, depth)):
+        if index:
+            coupled = piece(packed_right, index - 1)
+        else:
+            coupled = rows_ref[count - 1, :, 2 * n : 3 * n].astype(F32)
+        turned = jnp.transpose(coupled) * valid(packed_right, 2 * depth, index)
+        parts = [turned, piece(packed_right, depth + index), piece(packed_right, index)]
+        halo_right[index, :, : 3 * n] = jnp.concatenate(parts, axis=1).astype(BF16)
 
     def left_row(e):
-        if e < 0:
-            return halo_left[depth + e, :, : 3 * n]
-        if e > 0:
-            return rows_ref[e, :, : 3 * n]
-        turned = jnp.transpose(halo_left[depth - 1, :, 2 * n : 3 * n].astype(F32))
-        keep = rows_ref[0, :, 3 * n : 3 * n + 1].astype(F32)
-        return jnp.concatenate([(turned * keep).astype(BF16), rows_ref[0, :, n : 3 * n]], axis=1)
+        return halo_left[depth + e, :, : 3 * n] if e <= 0 else rows_ref[e, :, : 3 * n]
 
     def right_row(e):
-        if e < count:
-            return rows_ref[e, :, : 3 * n]
-        if e > count:
-            return halo_right[e - count, :, : 3 * n]
-        turned = jnp.transpose(rows_ref[count - 1, :, 2 * n : 3 * n].astype(F32))
-        keep = halo_right[0, :, 3 * n : 3 * n + 1].astype(F32)
-        return jnp.concatenate([(turned * keep).astype(BF16), halo_right[0, :, n : 3 * n]], axis=1)
+        return rows_ref[e, :, : 3 * n] if e < count else halo_right[e - count, :, : 3 * n]
 
     left_scr[0, : strip * n, :] = left_y_ref[...]
     right_scr[0, 2 * n :, :] = right_y_ref[...]
@@ -379,19 +396,20 @@
     total_columns = elem_size * count * n
     depth = DEGREE - 1
     wide = -(-(3 * n + 1) // LANES) * LANES
-    lanes = wide // band_size
     half = band_size // 2
     elem_me = lax.axis_index("elem").astype(jnp.int32).reshape(1)
     band_me = lax.axis_index("band").astype(jnp.int32).reshape(1)
 
+    packs = packed_width(2 * depth, n), packed_width(2 * depth + 1, n)
     first_rows, last_rows = pl.pallas_call(
-        functools.partial(ends_kernel, wide),
-        out_shape=[jax.ShapeDtypeStruct((depth * n, lanes), BF16)] * 2,
+        ends_kernel,
+        out_shape=[jax.ShapeDtypeStruct((n // band_size, pack), BF16) for pack in packs],
         in_specs=[SMEM] + [HBM] * 4,
         out_specs=[VMEM] * 2,
         scratch_shapes=[pltpu.SMEM((count,), jnp.int32)] * 2
         + [pltpu.VMEM((count, n, n), BF16)] * 2
-        + [pltpu.VMEM((2 * depth, n, wide), BF16), pltpu.SemaphoreType.DMA((6,))],
+        + [pltpu.VMEM((n, pack), F32) for pack in packs]
+        + [pltpu.SemaphoreType.DMA((6,))],
         compiler_params=params(60),
         cost_estimate=about(0.01),
         name="ends",
@@ -475,7 +493,8 @@
             in_specs=[SMEM] + [VMEM] * (4 + 2 * len(sizes) + 4 * half),
             out_specs=[VMEM] * 4,
             scratch_shapes=[pltpu.VMEM((DEGREE + 1, (strip + 2) * n, local), BF16)] * 2
-            + [pltpu.VMEM((depth, n, wide), BF16)] * 2,
+            + [pltpu.VMEM((depth + 1, n, wide), BF16)] * 2
+            + [pltpu.VMEM((n, packs[1]), F32), pltpu.VMEM((n, packs[0]), F32)],
             compiler_params=params(32),
             cost_estimate=about(3),
             name="strip",
@@ -611,7 +630,7 @@
     wide = -(-(3 * n + 1) // LANES) * LANES
     fits = (
         band_size & (band_size - 1) == 0
-        and wide % (band_size * LANES) == 0
+        and n % (8 * band_size) == 0
         and local % LANES == 0
         and elem_size % 2 == 0
         and local % elem_size == 0

time: 104 us -> 102 us (0.981)
  waiting for transfers between devices: 30.4 us -> 26.7 us
  starting transfers between devices: 23.5 us -> 25.1 us
    ppermute x15, waiting for transfers between devices: 15.2 us -> 12.8 us  [swap(): lax.ppermute(value, axis, [(source, source ^ bit) for source in range(cou...]
    ppermute x7, waiting for transfers between devices: 15.2 us -> 13.9 us  [from_behind(): return lax.ppermute(value, axis, pairs)]
    ppermute x7, starting transfers between devices: 16.6 us -> 17.7 us  [from_behind(): return lax.ppermute(value, axis, pairs)]
  transfers between devices with their start and end apart: 22 -> 22, of which waited for: 9 -> 8; matrix products, arithmetic and copies ran while one was open for 0% -> 0% of each run, Pallas kernels for 17% -> 18%
where the time goes in v6:
time: 102 us
  Pallas kernels  26.9 us (26%)
  waiting for transfers between devices  26.7 us (26%)
  starting transfers between devices  25.1 us (25%)
  blocking collectives  23 us (23%)
    ppermute x7, starting transfers between devices, from_behind(): return lax.ppermute(value, axis, pairs)  17.7 us
    ppermute x7, waiting for transfers between devices, from_behind(): return lax.ppermute(value, axis, pairs)  13.9 us
    ppermute x15, waiting for transfers between devices, swap(): lax.ppermute(value, axis, [(source, source ^ bit) for source in range(cou...  12.8 us
    all_to_all x1, blocking collectives, fast_shards(): lax.all_to_all(late, 'elem', 0, 0, tiled=True, axis_index_groups=groups)  12.4 us
    all_to_all x1, blocking collectives, fast_shards(): lax.all_to_all(weights, 'elem', 0, 0, tiled=True, axis_index_groups=groups)  10.7 us
    ppermute x15, starting transfers between devices, swap(): lax.ppermute(value, axis, [(source, source ^ bit) for source in range(cou...  7.36 us
    pallas_call x2, Pallas kernels, fast_shards(): pl.pallas_call(functools.partial(strip_kernel, n, count, strip, offset, l...  6.79 us
    pallas_call x1, Pallas kernels, fast_shards(): pl.pallas_call(functools.partial(interior_kernel, n, count, SPLIT, DEGREE...  3.98 us
  transfers between devices with their start and end apart: 22, of which 8 were waited for; matrix products, arithmetic and copies ran while one was open for 0% of the time, Pallas kernels for 18%

profile of v6, /device:TPU:0, one launch (start us, length us, event | category | flops | bytes accessed | tf_op | source)
XLA Modules:
  0.0 102.0 jit_solution(904426341917292709)
XLA Ops:
  0.0 2.8 %ends.1 = (bf16[40,1664]{1,0:T(8,128)(2,1)}, bf16[40,1792]{1,0:T(8,128)(2,1)}) custom-call(s32[1]{0:T(128)} %bitcast.1.me_ref, s32[16]{0:T(128)} %sizes_ref.3, s32[16]{0:T(128)} %pattern_ref, bf16[16,160,160]{2,1,0:T(8,128)(2,1)} %diag_ref.1, bf16[16,160,160]{2,1,0:T(8,128)(2,1)} %couple_ref.1), custom_call_target="tpu_custom_call" | custom-call | flops 11500000 | bytes 1 | tf_op jit(solution)/shard_map/ends/pallas_call | solution.py:404
  2.8 3.0 %collective-permute-start.3 = (bf16[40,1792]{1,0:T(8,128)(2,1)}, bf16[40,1792]{1,0:T(8,128)(2,1)S(1)}, u32[]{:S(2)}, u32[]{:S(2)}) collective-permute-start(bf16[40,1792]{1,0:T(8,128)(2,1)} %get-tuple-element.54), channel_id=1, source_target_pairs={{0,4},{4,8},{8,12},{12,16},{16,20},{20,24},{24,28},{28,0},{1,5},{5... | collective-permute-start | bytes 430088 | tf_op jit(solution)/shard_map/ppermute | solution.py:30
  5.8 3.1 %collective-permute-start.5 = (bf16[40,1664]{1,0:T(8,128)(2,1)}, bf16[40,1664]{1,0:T(8,128)(2,1)S(1)}, u32[]{:S(2)}, u32[]{:S(2)}) collective-permute-start(bf16[40,1664]{1,0:T(8,128)(2,1)} %get-tuple-element.39), channel_id=1, source_target_pairs={{0,28},{4,0},{8,4},{12,8},{16,12},{20,16},{24,20},{28,24},{1,29},{... | collective-permute-start | bytes 399368 | tf_op jit(solution)/shard_map/ppermute | solution.py:30
  10.0 2.1 %rows.1.rows_ref = bf16[16,160,512]{2,1,0:T(8,128)(2,1)S(1)} custom-call(s32[16]{0:T(128)S(1)} %copy-done.13, s32[16]{0:T(128)S(1)} %copy-done.14, bf16[16,160,160]{2,1,0:T(8,128)(2,1)S(1)} %copy-done, bf16[16,160,160]{2,1,0:T(8,128)(2,1)S(1)} %copy-done.1), custom_call_target="tpu_custom_call" | custom-call | flops 11500000 | bytes 1 | tf_op jit(solution)/shard_map/rows/pallas_call | solution.py:417
  12.0 3.4 %interior_first.1 = (bf16[2,320,256]{2,1,0:T(8,128)(2,1)S(1)}, bf16[2,320,256]{2,1,0:T(8,128)(2,1)S(1)}, bf16[2560,256]{1,0:T(8,128)(2,1)S(1)}, bf16[2560,256]{1,0:T(8,128)(2,1)S(1)}) custom-call(bf16[16,160,512]{2,1,0:T(8,128)(2,1)S(1)} %rows.1.rows_ref, bf16[2560,256]{1,0:T(8,128)(2,1)S(1)} %get-tuple-element.41.refs_0_), custom_call_target="tpu_custom_call" | custom-call | flops 11500000 | bytes 1 | tf_op jit(solution)/shard_map/interior_first/pallas_call | solution.py:447
  15.6 4.7 %collective-permute-start.2 = (bf16[480,256]{1,0:T(8,128)(2,1)S(1)}, bf16[480,256]{1,0:T(8,128)(2,1)S(1)}, u32[]{:S(2)}, u32[]{:S(2)}) collective-permute-start(bf16[480,256]{1,0:T(8,128)(2,1)S(1)} %get-tuple-element.48), channel_id=1, source_target_pairs={{0,28},{4,0},{8,4},{12,8},{16,12},{20,16},{24,20},{28,24},{1,29},{... | collective-permute-start | bytes 737288 | tf_op jit(solution)/shard_map/ppermute | solution.py:30
  20.3 1.7 %collective-permute-start.7 = (bf16[40,1792]{1,0:T(8,128)(2,1)S(1)}, bf16[40,1792]{1,0:T(8,128)(2,1)S(1)}, u32[]{:S(2)}, u32[]{:S(2)}) collective-permute-start(bf16[40,1792]{1,0:T(8,128)(2,1)S(1)} %collective-permute-done.3.refs_4_.refs_2_), channel_id=1, source_target_pairs={{0,2},{1,3},{2,0},{3,1},{4,6},{5,7},{6,4},{7,5},{8,10},{9,11},{10,... | collective-permute-start | bytes 430088 | tf_op jit(solution)/shard_map/ppermute | solution.py:35
  22.3 4.0 %interior_rest.1 = (bf16[4,320,256]{2,1,0:T(8,128)(2,1)S(1)}, bf16[4,320,256]{2,1,0:T(8,128)(2,1)S(1)}, bf16[640,256]{1,0:T(8,128)(2,1)S(1)}, f32[1,256]{1,0:T(1,128)S(1)}) custom-call(bf16[16,160,512]{2,1,0:T(8,128)(2,1)S(1)} %rows.1.rows_ref, bf16[2560,256]{1,0:T(8,128)(2,1)S(1)} %get-tuple-element.42.refs_0_, bf16[2560,256]{1,0:T(8,128)(2,1)S(1)} %get-tuple-element.43.refs_1_), custom_call_target="tpu_custom_call" | custom-call | flops 11500000 | bytes 1 | tf_op jit(solution)/shard_map/interior_rest/pallas_call | solution.py:461
  26.4 1.9 %collective-permute-done.2.right_y_ref = bf16[480,256]{1,0:T(8,128)(2,1)S(1)} collective-permute-done((bf16[480,256]{1,0:T(8,128)(2,1)S(1)}, bf16[480,256]{1,0:T(8,128)(2,1)S(1)}, u32[]{:S(2)}, u32[]{:S(2)}) %collective-permute-start.2) | collective-permute-done | bytes 245792 | tf_op jit(solution)/shard_map/ppermute | solution.py:30
  28.8 1.5 %collective-permute-start.14 = (bf16[640,256]{1,0:T(8,128)(2,1)S(1)}, bf16[640,256]{1,0:T(8,128)(2,1)S(1)}, u32[]{:S(2)}, u32[]{:S(2)}) collective-permute-start(bf16[640,256]{1,0:T(8,128)(2,1)S(1)} %get-tuple-element.44.refs_0_), channel_id=1, source_target_pairs={{0,2},{1,3},{2,0},{3,1},{4,6},{5,7},{6,4},{7,5},{8,10},{9,11},{10,... | collective-permute-start | bytes 983048 | tf_op jit(solution)/shard_map/ppermute | solution.py:35
  30.6 4.4 %collective-permute-start.13 = (bf16[480,256]{1,0:T(8,128)(2,1)S(1)}, bf16[480,256]{1,0:T(8,128)(2,1)S(1)}, u32[]{:S(2)}, u32[]{:S(2)}) collective-permute-start(bf16[480,256]{1,0:T(8,128)(2,1)S(1)} %get-tuple-element.63), channel_id=1, source_target_pairs={{0,28},{4,0},{8,4},{12,8},{16,12},{20,16},{24,20},{28,24},{1,29},{... | collective-permute-start | bytes 737288 | tf_op jit(solution)/shard_map/ppermute | solution.py:30
  35.1 2.8 %strip.2 = (bf16[960,256]{1,0:T(8,128)(2,1)S(1)}, bf16[6,320,256]{2,1,0:T(8,128)(2,1)S(1)}, bf16[6,320,256]{2,1,0:T(8,128)(2,1)S(1)}, f32[1,256]{1,0:T(1,128)S(1)}) custom-call(s32[1]{0:T(128)} %bitcast.1.me_ref, bf16[480,256]{1,0:T(8,128)(2,1)S(1)} %collective-permute-done.1.left_y_ref, bf16[480,256]{1,0:T(8,128)(2,1)S(1)} %collective-permute-done.2.right_y_ref, ...), custom_call_target="tpu_custom_call" | custom-call | flops 3449999872 | bytes 1 | tf_op jit(solution)/shard_map/strip/pallas_call | solution.py:490
  39.0 2.5 %collective-permute-done.12.left_y_ref = bf16[480,256]{1,0:T(8,128)(2,1)S(1)} collective-permute-done((bf16[480,256]{1,0:T(8,128)(2,1)S(1)}, bf16[480,256]{1,0:T(8,128)(2,1)S(1)}, u32[]{:S(2)}, u32[]{:S(2)}) %collective-permute-start.12) | collective-permute-done | bytes 245792 | tf_op jit(solution)/shard_map/ppermute | solution.py:30
  41.5 2.4 %collective-permute-done.13.right_y_ref = bf16[480,256]{1,0:T(8,128)(2,1)S(1)} collective-permute-done((bf16[480,256]{1,0:T(8,128)(2,1)S(1)}, bf16[480,256]{1,0:T(8,128)(2,1)S(1)}, u32[]{:S(2)}, u32[]{:S(2)}) %collective-permute-start.13) | collective-permute-done | bytes 245792 | tf_op jit(solution)/shard_map/ppermute | solution.py:30
  43.9 3.9 %strip.3 = (bf16[976,256]{1,0:T(8,128)(2,1)S(1)}, f32[8,128]{1,0:T(8,128)}, f32[8,128]{1,0:T(8,128)}, f32[1,256]{1,0:T(1,128)}) custom-call(s32[1]{0:T(128)} %bitcast.1.me_ref, bf16[480,256]{1,0:T(8,128)(2,1)S(1)} %collective-permute-done.12.left_y_ref, bf16[480,256]{1,0:T(8,128)(2,1)S(1)} %collective-permute-done.13.right_y_ref, ...), custom_call_target="tpu_custom_call" | custom-call | flops 3449999872 | bytes 1 | tf_op jit(solution)/shard_map/strip/pallas_call | solution.py:490
  49.0 1.8 %collective-permute-done.17.refs_5_.refs_6_ = bf16[960,256]{1,0:T(8,128)(2,1)S(1)} collective-permute-done((bf16[960,256]{1,0:T(8,128)(2,1)S(1)}, bf16[960,256]{1,0:T(8,128)(2,1)S(1)}, u32[]{:S(2)}, u32[]{:S(2)}) %collective-permute-start.17) | collective-permute-done | bytes 491552 | tf_op jit(solution)/shard_map/ppermute | solution.py:35
  51.3 1.8 %collective-permute-done.refs_1_ = bf16[640,256]{1,0:T(8,128)(2,1)S(1)} collective-permute-done((bf16[640,256]{1,0:T(8,128)(2,1)S(1)}, bf16[640,256]{1,0:T(8,128)(2,1)S(1)}, u32[]{:S(2)}, u32[]{:S(2)}) %collective-permute-start) | collective-permute-done | bytes 327712 | tf_op jit(solution)/shard_map/ppermute | solution.py:35
  54.4 7.3 %collective-permute-done.19.refs_7_.refs_10_ = bf16[976,256]{1,0:T(8,128)(2,1)S(1)} collective-permute-done((bf16[976,256]{1,0:T(8,128)(2,1)S(1)}, bf16[976,256]{1,0:T(8,128)(2,1)S(1)}, u32[]{:S(2)}, u32[]{:S(2)}) %collective-permute-start.19) | collective-permute-done | bytes 499744 | tf_op jit(solution)/shard_map/ppermute | solution.py:35
  62.2 1.8 %collective-permute-done.16.refs_4_.refs_3_ = bf16[640,256]{1,0:T(8,128)(2,1)S(1)} collective-permute-done((bf16[640,256]{1,0:T(8,128)(2,1)S(1)}, bf16[640,256]{1,0:T(8,128)(2,1)S(1)}, u32[]{:S(2)}, u32[]{:S(2)}) %collective-permute-start.16) | collective-permute-done | bytes 327712 | tf_op jit(solution)/shard_map/ppermute | solution.py:35
  65.0 12.4 %all_to_all.10.got_ref = bf16[4,64,1152]{2,1,0:T(8,128)(2,1)S(1)} all-to-all(bf16[4,64,1152]{2,1,0:T(8,128)(2,1)S(1)} %gram_late.1), channel_id=1, replica_groups={{0,4,8,12},{16,20,24,28},{1,5,9,13},{17,21,25,29},{2,6,10,14},{18,22,26..., dimensions={0} | all-to-all | bytes 1179648 | tf_op jit(solution)/shard_map/all_to_all | solution.py:534
  78.1 2.1 %collective-permute-start.21 = (bf16[64,1152]{1,0:T(8,128)(2,1)}, bf16[64,1152]{1,0:T(8,128)(2,1)}, u32[]{:S(2)}, u32[]{:S(2)}) collective-permute-start(bf16[64,1152]{1,0:T(8,128)(2,1)} %sums.1.mine_ref), channel_id=1, source_target_pairs={{0,16},{4,20},{8,24},{12,28},{16,0},{20,4},{24,8},{28,12},{1,17},{... | collective-permute-start | bytes 442376 | tf_op jit(solution)/shard_map/ppermute | solution.py:30
  80.3 7.1 %collective-permute-done.21.other_ref = bf16[64,1152]{1,0:T(8,128)(2,1)} collective-permute-done((bf16[64,1152]{1,0:T(8,128)(2,1)}, bf16[64,1152]{1,0:T(8,128)(2,1)}, u32[]{:S(2)}, u32[]{:S(2)}) %collective-permute-start.21) | collective-permute-done | bytes 147488 | tf_op jit(solution)/shard_map/ppermute | solution.py:30
  88.5 10.7 %all_to_all.11 = bf16[4,64,1024]{2,1,0:T(8,128)(2,1)S(1)} all-to-all(bf16[4,64,1024]{2,1,0:T(8,128)(2,1)S(1)} %weights.1), channel_id=1, replica_groups={{0,4,8,12},{16,20,24,28},{1,5,9,13},{17,21,25,29},{2,6,10,14},{18,22,26..., dimensions={0} | all-to-all | bytes 1048576 | tf_op jit(solution)/shard_map/all_to_all | solution.py:555
  99.2 2.8 %rotate.1 = bf16[256,2560]{1,0:T(8,128)(2,1)} custom-call(bf16[256,1024]{1,0:T(8,128)(2,1)S(1)} %bitcast.3, bf16[640,256]{1,0:T(8,128)(2,1)S(1)} %copy-done.9, bf16[640,256]{1,0:T(8,128)(2,1)S(1)} %copy-done.11, bf16[640,256]{1,0:T(8,128)(2,1)S(1)} %copy-done.5, bf16[640,256]{1,0:T(8,128)(2,1)S(1)} %copy-done.7, ...), custom_call_target="tpu_custom_call" | custom-call | flops 11500000 | bytes 1 | tf_op jit(solution)/shard_map/rotate/pallas_call | solution.py:556
  (64 shorter events, 9.7 us)
Async XLA Ops:
  2.8 17.4 %collective-permute-start.3 = (bf16[40,1792]{1,0:T(8,128)(2,1)}, bf16[40,1792]{1,0:T(8,128)(2,1)S(1)}, u32[]{:S(2)}, u32[]{:S(2)}) collective-permute-start(bf16[40,1792]{1,0:T(8,128)(2,1)} %get-tuple-element.54), channel_id=1, source_target_pairs={{0,4},{4,8},{8,12},{12,16},{16,20},{20,24},{24,28},{28,0},{1,5},{5... | collective-permute-start | bytes 430088 | tf_op jit(solution)/shard_map/ppermute | solution.py:30
  5.8 16.1 %collective-permute-start.5 = (bf16[40,1664]{1,0:T(8,128)(2,1)}, bf16[40,1664]{1,0:T(8,128)(2,1)S(1)}, u32[]{:S(2)}, u32[]{:S(2)}) collective-permute-start(bf16[40,1664]{1,0:T(8,128)(2,1)} %get-tuple-element.39), channel_id=1, source_target_pairs={{0,28},{4,0},{8,4},{12,8},{16,12},{20,16},{24,20},{28,24},{1,29},{... | collective-permute-start | bytes 399368 | tf_op jit(solution)/shard_map/ppermute | solution.py:30
  15.5 10.9 %collective-permute-start.1 = (bf16[480,256]{1,0:T(8,128)(2,1)S(1)}, bf16[480,256]{1,0:T(8,128)(2,1)S(1)}, u32[]{:S(2)}, u32[]{:S(2)}) collective-permute-start(bf16[480,256]{1,0:T(8,128)(2,1)S(1)} %get-tuple-element.46), channel_id=1, source_target_pairs={{0,4},{4,8},{8,12},{12,16},{16,20},{20,24},{24,28},{28,0},{1,5},{5... | collective-permute-start | bytes 737288 | tf_op jit(solution)/shard_map/ppermute | solution.py:30
  15.6 12.7 %collective-permute-start.2 = (bf16[480,256]{1,0:T(8,128)(2,1)S(1)}, bf16[480,256]{1,0:T(8,128)(2,1)S(1)}, u32[]{:S(2)}, u32[]{:S(2)}) collective-permute-start(bf16[480,256]{1,0:T(8,128)(2,1)S(1)} %get-tuple-element.48), channel_id=1, source_target_pairs={{0,28},{4,0},{8,4},{12,8},{16,12},{20,16},{24,20},{28,24},{1,29},{... | collective-permute-start | bytes 737288 | tf_op jit(solution)/shard_map/ppermute | solution.py:30
  20.3 8.0 %collective-permute-start.7 = (bf16[40,1792]{1,0:T(8,128)(2,1)S(1)}, bf16[40,1792]{1,0:T(8,128)(2,1)S(1)}, u32[]{:S(2)}, u32[]{:S(2)}) collective-permute-start(bf16[40,1792]{1,0:T(8,128)(2,1)S(1)} %collective-permute-done.3.refs_4_.refs_2_), channel_id=1, source_target_pairs={{0,2},{1,3},{2,0},{3,1},{4,6},{5,7},{6,4},{7,5},{8,10},{9,11},{10,... | collective-permute-start | bytes 430088 | tf_op jit(solution)/shard_map/ppermute | solution.py:35
  21.9 6.9 %collective-permute-start.9 = (bf16[40,1664]{1,0:T(8,128)(2,1)S(1)}, bf16[40,1664]{1,0:T(8,128)(2,1)S(1)}, u32[]{:S(2)}, u32[]{:S(2)}) collective-permute-start(bf16[40,1664]{1,0:T(8,128)(2,1)S(1)} %collective-permute-done.5.refs_6_.refs_4_), channel_id=1, source_target_pairs={{0,2},{1,3},{2,0},{3,1},{4,6},{5,7},{6,4},{7,5},{8,10},{9,11},{10,... | collective-permute-start | bytes 399368 | tf_op jit(solution)/shard_map/ppermute | solution.py:35
  26.3 26.8 %copy-start.8 = (bf16[640,256]{1,0:T(8,128)(2,1)}, bf16[640,256]{1,0:T(8,128)(2,1)S(1)}, u32[]{:S(2)}) copy-start(bf16[640,256]{1,0:T(8,128)(2,1)S(1)} %get-tuple-element.44.refs_0_) | copy-start | bytes 983044
  26.3 4.3 %collective-permute-start.4 = (bf16[40,1792]{1,0:T(8,128)(2,1)S(1)}, bf16[40,1792]{1,0:T(8,128)(2,1)S(1)}, u32[]{:S(2)}, u32[]{:S(2)}) collective-permute-start(bf16[40,1792]{1,0:T(8,128)(2,1)S(1)} %collective-permute-done.3.refs_4_.refs_2_), channel_id=1, source_target_pairs={{0,1},{1,0},{2,3},{3,2},{4,5},{5,4},{6,7},{7,6},{8,9},{9,8},{10,11... | collective-permute-start | bytes 430088 | tf_op jit(solution)/shard_map/ppermute | solution.py:35
  28.3 6.8 %collective-permute-start.8 = (bf16[40,1792]{1,0:T(8,128)(2,1)S(1)}, bf16[40,1792]{1,0:T(8,128)(2,1)S(1)}, u32[]{:S(2)}, u32[]{:S(2)}) collective-permute-start(bf16[40,1792]{1,0:T(8,128)(2,1)S(1)} %collective-permute-done.7.refs_8_.refs_6_), channel_id=1, source_target_pairs={{0,1},{1,0},{2,3},{3,2},{4,5},{5,4},{6,7},{7,6},{8,9},{9,8},{10,11... | collective-permute-start | bytes 430088 | tf_op jit(solution)/shard_map/ppermute | solution.py:35
  28.3 2.0 %collective-permute-start.6 = (bf16[40,1664]{1,0:T(8,128)(2,1)S(1)}, bf16[40,1664]{1,0:T(8,128)(2,1)S(1)}, u32[]{:S(2)}, u32[]{:S(2)}) collective-permute-start(bf16[40,1664]{1,0:T(8,128)(2,1)S(1)} %collective-permute-done.5.refs_6_.refs_4_), channel_id=1, source_target_pairs={{0,1},{1,0},{2,3},{3,2},{4,5},{5,4},{6,7},{7,6},{8,9},{9,8},{10,11... | collective-permute-start | bytes 399368 | tf_op jit(solution)/shard_map/ppermute | solution.py:35
  28.8 6.3 %collective-permute-start.10 = (bf16[40,1664]{1,0:T(8,128)(2,1)S(1)}, bf16[40,1664]{1,0:T(8,128)(2,1)S(1)}, u32[]{:S(2)}, u32[]{:S(2)}) collective-permute-start(bf16[40,1664]{1,0:T(8,128)(2,1)S(1)} %collective-permute-done.9.refs_10_.refs_8_), channel_id=1, source_target_pairs={{0,1},{1,0},{2,3},{3,2},{4,5},{5,4},{6,7},{7,6},{8,9},{9,8},{10,11... | collective-permute-start | bytes 399368 | tf_op jit(solution)/shard_map/ppermute | solution.py:35
  28.8 10.2 %collective-permute-start.14 = (bf16[640,256]{1,0:T(8,128)(2,1)S(1)}, bf16[640,256]{1,0:T(8,128)(2,1)S(1)}, u32[]{:S(2)}, u32[]{:S(2)}) collective-permute-start(bf16[640,256]{1,0:T(8,128)(2,1)S(1)} %get-tuple-element.44.refs_0_), channel_id=1, source_target_pairs={{0,2},{1,3},{2,0},{3,1},{4,6},{5,7},{6,4},{7,5},{8,10},{9,11},{10,... | collective-permute-start | bytes 983048 | tf_op jit(solution)/shard_map/ppermute | solution.py:35
  30.3 11.2 %collective-permute-start.12 = (bf16[480,256]{1,0:T(8,128)(2,1)S(1)}, bf16[480,256]{1,0:T(8,128)(2,1)S(1)}, u32[]{:S(2)}, u32[]{:S(2)}) collective-permute-start(bf16[480,256]{1,0:T(8,128)(2,1)S(1)} %get-tuple-element.61), channel_id=1, source_target_pairs={{0,4},{4,8},{8,12},{12,16},{16,20},{20,24},{24,28},{28,0},{1,5},{5... | collective-permute-start | bytes 737288 | tf_op jit(solution)/shard_map/ppermute | solution.py:30
  30.6 13.3 %collective-permute-start.13 = (bf16[480,256]{1,0:T(8,128)(2,1)S(1)}, bf16[480,256]{1,0:T(8,128)(2,1)S(1)}, u32[]{:S(2)}, u32[]{:S(2)}) collective-permute-start(bf16[480,256]{1,0:T(8,128)(2,1)S(1)} %get-tuple-element.63), channel_id=1, source_target_pairs={{0,28},{4,0},{8,4},{12,8},{16,12},{20,16},{24,20},{28,24},{1,29},{... | collective-permute-start | bytes 737288 | tf_op jit(solution)/shard_map/ppermute | solution.py:30
  37.9 12.9 %collective-permute-start.17 = (bf16[960,256]{1,0:T(8,128)(2,1)S(1)}, bf16[960,256]{1,0:T(8,128)(2,1)S(1)}, u32[]{:S(2)}, u32[]{:S(2)}) collective-permute-start(bf16[960,256]{1,0:T(8,128)(2,1)S(1)} %get-tuple-element.59.refs_2_.refs_4_), channel_id=1, source_target_pairs={{0,2},{1,3},{2,0},{3,1},{4,6},{5,7},{6,4},{7,5},{8,10},{9,11},{10,... | collective-permute-start | bytes 1474568 | tf_op jit(solution)/shard_map/ppermute | solution.py:35
  39.0 25.0 %copy-start.4 = (bf16[640,256]{1,0:T(8,128)(2,1)}, bf16[640,256]{1,0:T(8,128)(2,1)S(1)}, u32[]{:S(2)}) copy-start(bf16[640,256]{1,0:T(8,128)(2,1)S(1)} %collective-permute-done.14.refs_3_.refs_2_) | copy-start | bytes 983044
  47.9 5.2 %collective-permute-start.15 = (bf16[976,256]{1,0:T(8,128)(2,1)S(1)}, bf16[976,256]{1,0:T(8,128)(2,1)S(1)}, u32[]{:S(2)}, u32[]{:S(2)}) collective-permute-start(bf16[976,256]{1,0:T(8,128)(2,1)S(1)} %get-tuple-element.68.refs_4_.refs_8_), channel_id=1, source_target_pairs={{0,1},{1,0},{2,3},{3,2},{4,5},{5,4},{6,7},{7,6},{8,9},{9,8},{10,11... | collective-permute-start | bytes 1499144 | tf_op jit(solution)/shard_map/ppermute | solution.py:35
  47.9 13.8 %collective-permute-start.19 = (bf16[976,256]{1,0:T(8,128)(2,1)S(1)}, bf16[976,256]{1,0:T(8,128)(2,1)S(1)}, u32[]{:S(2)}, u32[]{:S(2)}) collective-permute-start(bf16[976,256]{1,0:T(8,128)(2,1)S(1)} %get-tuple-element.68.refs_4_.refs_8_), channel_id=1, source_target_pairs={{0,2},{1,3},{2,0},{3,1},{4,6},{5,7},{6,4},{7,5},{8,10},{9,11},{10,... | collective-permute-start | bytes 1499144 | tf_op jit(solution)/shard_map/ppermute | solution.py:35
  48.8 4.4 %collective-permute-start.11 = (bf16[960,256]{1,0:T(8,128)(2,1)S(1)}, bf16[960,256]{1,0:T(8,128)(2,1)S(1)}, u32[]{:S(2)}, u32[]{:S(2)}) collective-permute-start(bf16[960,256]{1,0:T(8,128)(2,1)S(1)} %get-tuple-element.59.refs_2_.refs_4_), channel_id=1, source_target_pairs={{0,1},{1,0},{2,3},{3,2},{4,5},{5,4},{6,7},{7,6},{8,9},{9,8},{10,11... | collective-permute-start | bytes 1474568 | tf_op jit(solution)/shard_map/ppermute | solution.py:35
  50.8 10.9 %collective-permute-start.18 = (bf16[960,256]{1,0:T(8,128)(2,1)S(1)}, bf16[960,256]{1,0:T(8,128)(2,1)S(1)}, u32[]{:S(2)}, u32[]{:S(2)}) collective-permute-start(bf16[960,256]{1,0:T(8,128)(2,1)S(1)} %collective-permute-done.17.refs_5_.refs_6_), channel_id=1, source_target_pairs={{0,1},{1,0},{2,3},{3,2},{4,5},{5,4},{6,7},{7,6},{8,9},{9,8},{10,11... | collective-permute-start | bytes 1474568 | tf_op jit(solution)/shard_map/ppermute | solution.py:35
  50.8 2.3 %collective-permute-start = (bf16[640,256]{1,0:T(8,128)(2,1)S(1)}, bf16[640,256]{1,0:T(8,128)(2,1)S(1)}, u32[]{:S(2)}, u32[]{:S(2)}) collective-permute-start(bf16[640,256]{1,0:T(8,128)(2,1)S(1)} %get-tuple-element.44.refs_0_), channel_id=1, source_target_pairs={{0,1},{1,0},{2,3},{3,2},{4,5},{5,4},{6,7},{7,6},{8,9},{9,8},{10,11... | collective-permute-start | bytes 983048 | tf_op jit(solution)/shard_map/ppermute | solution.py:35
  61.7 2.4 %collective-permute-start.20 = (bf16[976,256]{1,0:T(8,128)(2,1)S(1)}, bf16[976,256]{1,0:T(8,128)(2,1)S(1)}, u32[]{:S(2)}, u32[]{:S(2)}) collective-permute-start(bf16[976,256]{1,0:T(8,128)(2,1)S(1)} %collective-permute-done.19.refs_7_.refs_10_), channel_id=1, source_target_pairs={{0,1},{1,0},{2,3},{3,2},{4,5},{5,4},{6,7},{7,6},{8,9},{9,8},{10,11... | collective-permute-start | bytes 1499144 | tf_op jit(solution)/shard_map/ppermute | solution.py:35
  61.7 2.3 %collective-permute-start.16 = (bf16[640,256]{1,0:T(8,128)(2,1)S(1)}, bf16[640,256]{1,0:T(8,128)(2,1)S(1)}, u32[]{:S(2)}, u32[]{:S(2)}) collective-permute-start(bf16[640,256]{1,0:T(8,128)(2,1)S(1)} %collective-permute-done.14.refs_3_.refs_2_), channel_id=1, source_target_pairs={{0,1},{1,0},{2,3},{3,2},{4,5},{5,4},{6,7},{7,6},{8,9},{9,8},{10,11... | collective-permute-start | bytes 983048 | tf_op jit(solution)/shard_map/ppermute | solution.py:35
  78.1 9.3 %collective-permute-start.21 = (bf16[64,1152]{1,0:T(8,128)(2,1)}, bf16[64,1152]{1,0:T(8,128)(2,1)}, u32[]{:S(2)}, u32[]{:S(2)}) collective-permute-start(bf16[64,1152]{1,0:T(8,128)(2,1)} %sums.1.mine_ref), channel_id=1, source_target_pairs={{0,16},{4,20},{8,24},{12,28},{16,0},{20,4},{24,8},{28,12},{1,17},{... | collective-permute-start | bytes 442376 | tf_op jit(solution)/shard_map/ppermute | solution.py:30
  (13 other events, 142.5 us)

commit v7 on v6

--- a/solution.py
+++ b/solution.py
@@ -453,8 +453,8 @@
         cost_estimate=about(0.01),
         name="interior_first",
     )(rows, start)
-    left_y = [from_behind(after(ends[1], even), "elem", 1)]
-    right_y = [from_behind(after(ends[0], even), "elem", -1)]
+    left_y = [from_behind(ends[1], "elem", 1)]
+    right_y = [from_behind(ends[0], "elem", -1)]
     own_rows = [after(side, even) for side in (left_rows, right_rows)]
     across_rows = [swap(side, "band", half) for side in own_rows]
     older, newer = (odd, even) if SPLIT % 2 == 0 else (even, odd)

time: 102 us -> 101 us (level)
  starting transfers between devices: 25.1 us -> 23.8 us
    ppermute x15, waiting for transfers between devices: 12.8 us -> 14.1 us  [swap(): lax.ppermute(value, axis, [(source, source ^ bit) for source in range(cou...]
    ppermute x7, waiting for transfers between devices: 13.9 us -> 12.8 us  [from_behind(): return lax.ppermute(value, axis, pairs)]
  transfers between devices with their start and end apart: 22 -> 22, of which waited for: 8 -> 9; matrix products, arithmetic and copies ran while one was open for 0% -> 0% of each run, Pallas kernels for 18% -> 18%
where the time goes in v7:
time: 101 us
  Pallas kernels  26.9 us (27%)
  waiting for transfers between devices  26.9 us (27%)
  starting transfers between devices  23.8 us (24%)
  blocking collectives  23 us (23%)
    ppermute x7, starting transfers between devices, from_behind(): return lax.ppermute(value, axis, pairs)  17 us
    ppermute x15, waiting for transfers between devices, swap(): lax.ppermute(value, axis, [(source, source ^ bit) for source in range(cou...  14.1 us
    ppermute x7, waiting for transfers between devices, from_behind(): return lax.ppermute(value, axis, pairs)  12.8 us
    all_to_all x1, blocking collectives, fast_shards(): lax.all_to_all(late, 'elem', 0, 0, tiled=True, axis_index_groups=groups)  12.4 us
    all_to_all x1, blocking collectives, fast_shards(): lax.all_to_all(weights, 'elem', 0, 0, tiled=True, axis_index_groups=groups)  10.7 us
    ppermute x15, starting transfers between devices, swap(): lax.ppermute(value, axis, [(source, source ^ bit) for source in range(cou...  6.81 us
    pallas_call x2, Pallas kernels, fast_shards(): pl.pallas_call(functools.partial(strip_kernel, n, count, strip, offset, l...  6.7 us
    pallas_call x1, Pallas kernels, fast_shards(): pl.pallas_call(functools.partial(interior_kernel, n, count, SPLIT, DEGREE...  3.97 us
  transfers between devices with their start and end apart: 22, of which 9 were waited for; matrix products, arithmetic and copies ran while one was open for 0% of the time, Pallas kernels for 18%

profile of v7, /device:TPU:0, one launch (start us, length us, event | category | flops | bytes accessed | tf_op | source)
XLA Modules:
  0.0 101.0 jit_solution(6915714177469485554)
XLA Ops:
  0.0 2.8 %ends.1 = (bf16[40,1664]{1,0:T(8,128)(2,1)}, bf16[40,1792]{1,0:T(8,128)(2,1)}) custom-call(s32[1]{0:T(128)} %bitcast.1.me_ref, s32[16]{0:T(128)} %sizes_ref.3, s32[16]{0:T(128)} %pattern_ref, bf16[16,160,160]{2,1,0:T(8,128)(2,1)} %diag_ref.1, bf16[16,160,160]{2,1,0:T(8,128)(2,1)} %couple_ref.1), custom_call_target="tpu_custom_call" | custom-call | flops 11500000 | bytes 1 | tf_op jit(solution)/shard_map/ends/pallas_call | solution.py:404
  2.8 3.0 %collective-permute-start.3 = (bf16[40,1792]{1,0:T(8,128)(2,1)}, bf16[40,1792]{1,0:T(8,128)(2,1)S(1)}, u32[]{:S(2)}, u32[]{:S(2)}) collective-permute-start(bf16[40,1792]{1,0:T(8,128)(2,1)} %get-tuple-element.50), channel_id=1, source_target_pairs={{0,4},{4,8},{8,12},{12,16},{16,20},{20,24},{24,28},{28,0},{1,5},{5... | collective-permute-start | bytes 430088 | tf_op jit(solution)/shard_map/ppermute | solution.py:30
  5.8 3.1 %collective-permute-start.5 = (bf16[40,1664]{1,0:T(8,128)(2,1)}, bf16[40,1664]{1,0:T(8,128)(2,1)S(1)}, u32[]{:S(2)}, u32[]{:S(2)}) collective-permute-start(bf16[40,1664]{1,0:T(8,128)(2,1)} %get-tuple-element.37), channel_id=1, source_target_pairs={{0,28},{4,0},{8,4},{12,8},{16,12},{20,16},{24,20},{28,24},{1,29},{... | collective-permute-start | bytes 399368 | tf_op jit(solution)/shard_map/ppermute | solution.py:30
  10.0 4.7 %collective-permute-start.2 = (bf16[480,256]{1,0:T(8,128)(2,1)S(1)}, bf16[480,256]{1,0:T(8,128)(2,1)S(1)}, u32[]{:S(2)}, u32[]{:S(2)}) collective-permute-start(bf16[480,256]{1,0:T(8,128)(2,1)S(1)} %get-tuple-element.44), channel_id=1, source_target_pairs={{0,28},{4,0},{8,4},{12,8},{16,12},{20,16},{24,20},{28,24},{1,29},{... | collective-permute-start | bytes 737288 | tf_op jit(solution)/shard_map/ppermute | solution.py:30
  14.7 2.1 %rows.1.rows_ref = bf16[16,160,512]{2,1,0:T(8,128)(2,1)S(1)} custom-call(s32[16]{0:T(128)S(1)} %copy-done.13, s32[16]{0:T(128)S(1)} %copy-done.14, bf16[16,160,160]{2,1,0:T(8,128)(2,1)S(1)} %copy-done, bf16[16,160,160]{2,1,0:T(8,128)(2,1)S(1)} %copy-done.1), custom_call_target="tpu_custom_call" | custom-call | flops 11500000 | bytes 1 | tf_op jit(solution)/shard_map/rows/pallas_call | solution.py:417
  16.8 3.4 %interior_first.1 = (bf16[2,320,256]{2,1,0:T(8,128)(2,1)S(1)}, bf16[2,320,256]{2,1,0:T(8,128)(2,1)S(1)}, bf16[2560,256]{1,0:T(8,128)(2,1)S(1)}, bf16[2560,256]{1,0:T(8,128)(2,1)S(1)}) custom-call(bf16[16,160,512]{2,1,0:T(8,128)(2,1)S(1)} %rows.1.rows_ref, bf16[2560,256]{1,0:T(8,128)(2,1)S(1)} %get-tuple-element.39.refs_0_), custom_call_target="tpu_custom_call" | custom-call | flops 11500000 | bytes 1 | tf_op jit(solution)/shard_map/interior_first/pallas_call | solution.py:447
  20.3 1.7 %collective-permute-start.7 = (bf16[40,1792]{1,0:T(8,128)(2,1)S(1)}, bf16[40,1792]{1,0:T(8,128)(2,1)S(1)}, u32[]{:S(2)}, u32[]{:S(2)}) collective-permute-start(bf16[40,1792]{1,0:T(8,128)(2,1)S(1)} %collective-permute-done.3.refs_4_.refs_2_), channel_id=1, source_target_pairs={{0,2},{1,3},{2,0},{3,1},{4,6},{5,7},{6,4},{7,5},{8,10},{9,11},{10,... | collective-permute-start | bytes 430088 | tf_op jit(solution)/shard_map/ppermute | solution.py:35
  22.4 4.0 %interior_rest.1 = (bf16[4,320,256]{2,1,0:T(8,128)(2,1)S(1)}, bf16[4,320,256]{2,1,0:T(8,128)(2,1)S(1)}, bf16[640,256]{1,0:T(8,128)(2,1)S(1)}, f32[1,256]{1,0:T(1,128)S(1)}) custom-call(bf16[16,160,512]{2,1,0:T(8,128)(2,1)S(1)} %rows.1.rows_ref, bf16[2560,256]{1,0:T(8,128)(2,1)S(1)} %get-tuple-element.40.refs_0_, bf16[2560,256]{1,0:T(8,128)(2,1)S(1)} %get-tuple-element.41.refs_1_), custom_call_target="tpu_custom_call" | custom-call | flops 11500000 | bytes 1 | tf_op jit(solution)/shard_map/interior_rest/pallas_call | solution.py:461
  27.8 1.5 %collective-permute-start.14 = (bf16[640,256]{1,0:T(8,128)(2,1)S(1)}, bf16[640,256]{1,0:T(8,128)(2,1)S(1)}, u32[]{:S(2)}, u32[]{:S(2)}) collective-permute-start(bf16[640,256]{1,0:T(8,128)(2,1)S(1)} %get-tuple-element.42.refs_0_), channel_id=1, source_target_pairs={{0,2},{1,3},{2,0},{3,1},{4,6},{5,7},{6,4},{7,5},{8,10},{9,11},{10,... | collective-permute-start | bytes 983048 | tf_op jit(solution)/shard_map/ppermute | solution.py:35
  29.4 4.7 %collective-permute-start.13 = (bf16[480,256]{1,0:T(8,128)(2,1)S(1)}, bf16[480,256]{1,0:T(8,128)(2,1)S(1)}, u32[]{:S(2)}, u32[]{:S(2)}) collective-permute-start(bf16[480,256]{1,0:T(8,128)(2,1)S(1)} %get-tuple-element.59), channel_id=1, source_target_pairs={{0,28},{4,0},{8,4},{12,8},{16,12},{20,16},{24,20},{28,24},{1,29},{... | collective-permute-start | bytes 737288 | tf_op jit(solution)/shard_map/ppermute | solution.py:30
  34.1 2.9 %strip.2 = (bf16[960,256]{1,0:T(8,128)(2,1)S(1)}, bf16[6,320,256]{2,1,0:T(8,128)(2,1)S(1)}, bf16[6,320,256]{2,1,0:T(8,128)(2,1)S(1)}, f32[1,256]{1,0:T(1,128)S(1)}) custom-call(s32[1]{0:T(128)} %bitcast.1.me_ref, bf16[480,256]{1,0:T(8,128)(2,1)S(1)} %collective-permute-done.1.left_y_ref, bf16[480,256]{1,0:T(8,128)(2,1)S(1)} %collective-permute-done.2.right_y_ref, ...), custom_call_target="tpu_custom_call" | custom-call | flops 3449999872 | bytes 1 | tf_op jit(solution)/shard_map/strip/pallas_call | solution.py:490
  38.0 2.6 %collective-permute-done.12.left_y_ref = bf16[480,256]{1,0:T(8,128)(2,1)S(1)} collective-permute-done((bf16[480,256]{1,0:T(8,128)(2,1)S(1)}, bf16[480,256]{1,0:T(8,128)(2,1)S(1)}, u32[]{:S(2)}, u32[]{:S(2)}) %collective-permute-start.12) | collective-permute-done | bytes 245792 | tf_op jit(solution)/shard_map/ppermute | solution.py:30
  40.5 2.4 %collective-permute-done.13.right_y_ref = bf16[480,256]{1,0:T(8,128)(2,1)S(1)} collective-permute-done((bf16[480,256]{1,0:T(8,128)(2,1)S(1)}, bf16[480,256]{1,0:T(8,128)(2,1)S(1)}, u32[]{:S(2)}, u32[]{:S(2)}) %collective-permute-start.13) | collective-permute-done | bytes 245792 | tf_op jit(solution)/shard_map/ppermute | solution.py:30
  43.0 3.9 %strip.3 = (bf16[976,256]{1,0:T(8,128)(2,1)S(1)}, f32[8,128]{1,0:T(8,128)}, f32[8,128]{1,0:T(8,128)}, f32[1,256]{1,0:T(1,128)}) custom-call(s32[1]{0:T(128)} %bitcast.1.me_ref, bf16[480,256]{1,0:T(8,128)(2,1)S(1)} %collective-permute-done.12.left_y_ref, bf16[480,256]{1,0:T(8,128)(2,1)S(1)} %collective-permute-done.13.right_y_ref, ...), custom_call_target="tpu_custom_call" | custom-call | flops 3449999872 | bytes 1 | tf_op jit(solution)/shard_map/strip/pallas_call | solution.py:490
  47.6 2.2 %collective-permute-done.17.refs_5_.refs_6_ = bf16[960,256]{1,0:T(8,128)(2,1)S(1)} collective-permute-done((bf16[960,256]{1,0:T(8,128)(2,1)S(1)}, bf16[960,256]{1,0:T(8,128)(2,1)S(1)}, u32[]{:S(2)}, u32[]{:S(2)}) %collective-permute-start.17) | collective-permute-done | bytes 491552 | tf_op jit(solution)/shard_map/ppermute | solution.py:35
  50.3 1.8 %collective-permute-done.refs_1_ = bf16[640,256]{1,0:T(8,128)(2,1)S(1)} collective-permute-done((bf16[640,256]{1,0:T(8,128)(2,1)S(1)}, bf16[640,256]{1,0:T(8,128)(2,1)S(1)}, u32[]{:S(2)}, u32[]{:S(2)}) %collective-permute-start) | collective-permute-done | bytes 327712 | tf_op jit(solution)/shard_map/ppermute | solution.py:35
  52.2 1.3 %gram_early.1 = (bf16[4,64,512]{2,1,0:T(8,128)(2,1)S(1)}, bf16[2,16,256]{2,1,0:T(8,128)(2,1)S(1)}, bf16[256,2560]{1,0:T(8,128)(2,1)S(1)}) custom-call(bf16[640,256]{1,0:T(8,128)(2,1)S(1)} %get-tuple-element.42.refs_0_, bf16[640,256]{1,0:T(8,128)(2,1)S(1)} %collective-permute-done.refs_1_, bf16[960,256]{1,0:T(8,128)(2,1)S(1)} %get-tuple-element.55.refs_2_.refs_4_, ...), custom_call_target="tpu_custom_call" | custom-call | flops 11500000 | bytes 1 | tf_op jit(solution)/shard_map/gram_early/pallas_call | solution.py:519
  53.4 7.2 %collective-permute-done.19.refs_7_.refs_10_ = bf16[976,256]{1,0:T(8,128)(2,1)S(1)} collective-permute-done((bf16[976,256]{1,0:T(8,128)(2,1)S(1)}, bf16[976,256]{1,0:T(8,128)(2,1)S(1)}, u32[]{:S(2)}, u32[]{:S(2)}) %collective-permute-start.19) | collective-permute-done | bytes 499744 | tf_op jit(solution)/shard_map/ppermute | solution.py:35
  61.1 1.8 %collective-permute-done.16.refs_4_.refs_3_ = bf16[640,256]{1,0:T(8,128)(2,1)S(1)} collective-permute-done((bf16[640,256]{1,0:T(8,128)(2,1)S(1)}, bf16[640,256]{1,0:T(8,128)(2,1)S(1)}, u32[]{:S(2)}, u32[]{:S(2)}) %collective-permute-start.16) | collective-permute-done | bytes 327712 | tf_op jit(solution)/shard_map/ppermute | solution.py:35
  63.9 12.4 %all_to_all.10.got_ref = bf16[4,64,1152]{2,1,0:T(8,128)(2,1)S(1)} all-to-all(bf16[4,64,1152]{2,1,0:T(8,128)(2,1)S(1)} %gram_late.1), channel_id=1, replica_groups={{0,4,8,12},{16,20,24,28},{1,5,9,13},{17,21,25,29},{2,6,10,14},{18,22,26..., dimensions={0} | all-to-all | bytes 1179648 | tf_op jit(solution)/shard_map/all_to_all | solution.py:534
  77.0 1.4 %collective-permute-start.21 = (bf16[64,1152]{1,0:T(8,128)(2,1)}, bf16[64,1152]{1,0:T(8,128)(2,1)}, u32[]{:S(2)}, u32[]{:S(2)}) collective-permute-start(bf16[64,1152]{1,0:T(8,128)(2,1)} %sums.1.mine_ref), channel_id=1, source_target_pairs={{0,16},{4,20},{8,24},{12,28},{16,0},{20,4},{24,8},{28,12},{1,17},{... | collective-permute-start | bytes 442376 | tf_op jit(solution)/shard_map/ppermute | solution.py:30
  78.5 7.8 %collective-permute-done.21.other_ref = bf16[64,1152]{1,0:T(8,128)(2,1)} collective-permute-done((bf16[64,1152]{1,0:T(8,128)(2,1)}, bf16[64,1152]{1,0:T(8,128)(2,1)}, u32[]{:S(2)}, u32[]{:S(2)}) %collective-permute-start.21) | collective-permute-done | bytes 147488 | tf_op jit(solution)/shard_map/ppermute | solution.py:30
  87.4 10.7 %all_to_all.11 = bf16[4,64,1024]{2,1,0:T(8,128)(2,1)S(1)} all-to-all(bf16[4,64,1024]{2,1,0:T(8,128)(2,1)S(1)} %weights.1), channel_id=1, replica_groups={{0,4,8,12},{16,20,24,28},{1,5,9,13},{17,21,25,29},{2,6,10,14},{18,22,26..., dimensions={0} | all-to-all | bytes 1048576 | tf_op jit(solution)/shard_map/all_to_all | solution.py:555
  98.1 2.8 %rotate.1 = bf16[256,2560]{1,0:T(8,128)(2,1)} custom-call(bf16[256,1024]{1,0:T(8,128)(2,1)S(1)} %bitcast.3, bf16[640,256]{1,0:T(8,128)(2,1)S(1)} %copy-done.9, bf16[640,256]{1,0:T(8,128)(2,1)S(1)} %copy-done.11, bf16[640,256]{1,0:T(8,128)(2,1)S(1)} %copy-done.5, bf16[640,256]{1,0:T(8,128)(2,1)S(1)} %copy-done.7, ...), custom_call_target="tpu_custom_call" | custom-call | flops 11500000 | bytes 1 | tf_op jit(solution)/shard_map/rotate/pallas_call | solution.py:556
  (64 shorter events, 8.6 us)
Async XLA Ops:
  2.8 17.4 %collective-permute-start.3 = (bf16[40,1792]{1,0:T(8,128)(2,1)}, bf16[40,1792]{1,0:T(8,128)(2,1)S(1)}, u32[]{:S(2)}, u32[]{:S(2)}) collective-permute-start(bf16[40,1792]{1,0:T(8,128)(2,1)} %get-tuple-element.50), channel_id=1, source_target_pairs={{0,4},{4,8},{8,12},{12,16},{16,20},{20,24},{24,28},{28,0},{1,5},{5... | collective-permute-start | bytes 430088 | tf_op jit(solution)/shard_map/ppermute | solution.py:30
  5.8 16.1 %collective-permute-start.5 = (bf16[40,1664]{1,0:T(8,128)(2,1)}, bf16[40,1664]{1,0:T(8,128)(2,1)S(1)}, u32[]{:S(2)}, u32[]{:S(2)}) collective-permute-start(bf16[40,1664]{1,0:T(8,128)(2,1)} %get-tuple-element.37), channel_id=1, source_target_pairs={{0,28},{4,0},{8,4},{12,8},{16,12},{20,16},{24,20},{28,24},{1,29},{... | collective-permute-start | bytes 399368 | tf_op jit(solution)/shard_map/ppermute | solution.py:30
  10.0 16.5 %collective-permute-start.1 = (bf16[480,256]{1,0:T(8,128)(2,1)S(1)}, bf16[480,256]{1,0:T(8,128)(2,1)S(1)}, u32[]{:S(2)}, u32[]{:S(2)}) collective-permute-start(bf16[480,256]{1,0:T(8,128)(2,1)S(1)} %get-tuple-element.43), channel_id=1, source_target_pairs={{0,4},{4,8},{8,12},{12,16},{16,20},{20,24},{24,28},{28,0},{1,5},{5... | collective-permute-start | bytes 737288 | tf_op jit(solution)/shard_map/ppermute | solution.py:30
  10.0 16.4 %collective-permute-start.2 = (bf16[480,256]{1,0:T(8,128)(2,1)S(1)}, bf16[480,256]{1,0:T(8,128)(2,1)S(1)}, u32[]{:S(2)}, u32[]{:S(2)}) collective-permute-start(bf16[480,256]{1,0:T(8,128)(2,1)S(1)} %get-tuple-element.44), channel_id=1, source_target_pairs={{0,28},{4,0},{8,4},{12,8},{16,12},{20,16},{24,20},{28,24},{1,29},{... | collective-permute-start | bytes 737288 | tf_op jit(solution)/shard_map/ppermute | solution.py:30
  20.3 6.2 %collective-permute-start.7 = (bf16[40,1792]{1,0:T(8,128)(2,1)S(1)}, bf16[40,1792]{1,0:T(8,128)(2,1)S(1)}, u32[]{:S(2)}, u32[]{:S(2)}) collective-permute-start(bf16[40,1792]{1,0:T(8,128)(2,1)S(1)} %collective-permute-done.3.refs_4_.refs_2_), channel_id=1, source_target_pairs={{0,2},{1,3},{2,0},{3,1},{4,6},{5,7},{6,4},{7,5},{8,10},{9,11},{10,... | collective-permute-start | bytes 430088 | tf_op jit(solution)/shard_map/ppermute | solution.py:35
  22.0 5.9 %collective-permute-start.9 = (bf16[40,1664]{1,0:T(8,128)(2,1)S(1)}, bf16[40,1664]{1,0:T(8,128)(2,1)S(1)}, u32[]{:S(2)}, u32[]{:S(2)}) collective-permute-start(bf16[40,1664]{1,0:T(8,128)(2,1)S(1)} %collective-permute-done.5.refs_6_.refs_4_), channel_id=1, source_target_pairs={{0,2},{1,3},{2,0},{3,1},{4,6},{5,7},{6,4},{7,5},{8,10},{9,11},{10,... | collective-permute-start | bytes 399368 | tf_op jit(solution)/shard_map/ppermute | solution.py:35
  26.3 25.8 %copy-start.8 = (bf16[640,256]{1,0:T(8,128)(2,1)}, bf16[640,256]{1,0:T(8,128)(2,1)S(1)}, u32[]{:S(2)}) copy-start(bf16[640,256]{1,0:T(8,128)(2,1)S(1)} %get-tuple-element.42.refs_0_) | copy-start | bytes 983044
  26.3 3.0 %collective-permute-start.4 = (bf16[40,1792]{1,0:T(8,128)(2,1)S(1)}, bf16[40,1792]{1,0:T(8,128)(2,1)S(1)}, u32[]{:S(2)}, u32[]{:S(2)}) collective-permute-start(bf16[40,1792]{1,0:T(8,128)(2,1)S(1)} %collective-permute-done.3.refs_4_.refs_2_), channel_id=1, source_target_pairs={{0,1},{1,0},{2,3},{3,2},{4,5},{5,4},{6,7},{7,6},{8,9},{9,8},{10,11... | collective-permute-start | bytes 430088 | tf_op jit(solution)/shard_map/ppermute | solution.py:35
  26.5 7.6 %collective-permute-start.8 = (bf16[40,1792]{1,0:T(8,128)(2,1)S(1)}, bf16[40,1792]{1,0:T(8,128)(2,1)S(1)}, u32[]{:S(2)}, u32[]{:S(2)}) collective-permute-start(bf16[40,1792]{1,0:T(8,128)(2,1)S(1)} %collective-permute-done.7.refs_8_.refs_6_), channel_id=1, source_target_pairs={{0,1},{1,0},{2,3},{3,2},{4,5},{5,4},{6,7},{7,6},{8,9},{9,8},{10,11... | collective-permute-start | bytes 430088 | tf_op jit(solution)/shard_map/ppermute | solution.py:35
  27.0 2.4 %collective-permute-start.6 = (bf16[40,1664]{1,0:T(8,128)(2,1)S(1)}, bf16[40,1664]{1,0:T(8,128)(2,1)S(1)}, u32[]{:S(2)}, u32[]{:S(2)}) collective-permute-start(bf16[40,1664]{1,0:T(8,128)(2,1)S(1)} %collective-permute-done.5.refs_6_.refs_4_), channel_id=1, source_target_pairs={{0,1},{1,0},{2,3},{3,2},{4,5},{5,4},{6,7},{7,6},{8,9},{9,8},{10,11... | collective-permute-start | bytes 399368 | tf_op jit(solution)/shard_map/ppermute | solution.py:35
  27.8 6.3 %collective-permute-start.10 = (bf16[40,1664]{1,0:T(8,128)(2,1)S(1)}, bf16[40,1664]{1,0:T(8,128)(2,1)S(1)}, u32[]{:S(2)}, u32[]{:S(2)}) collective-permute-start(bf16[40,1664]{1,0:T(8,128)(2,1)S(1)} %collective-permute-done.9.refs_10_.refs_8_), channel_id=1, source_target_pairs={{0,1},{1,0},{2,3},{3,2},{4,5},{5,4},{6,7},{7,6},{8,9},{9,8},{10,11... | collective-permute-start | bytes 399368 | tf_op jit(solution)/shard_map/ppermute | solution.py:35
  27.8 10.1 %collective-permute-start.14 = (bf16[640,256]{1,0:T(8,128)(2,1)S(1)}, bf16[640,256]{1,0:T(8,128)(2,1)S(1)}, u32[]{:S(2)}, u32[]{:S(2)}) collective-permute-start(bf16[640,256]{1,0:T(8,128)(2,1)S(1)} %get-tuple-element.42.refs_0_), channel_id=1, source_target_pairs={{0,2},{1,3},{2,0},{3,1},{4,6},{5,7},{6,4},{7,5},{8,10},{9,11},{10,... | collective-permute-start | bytes 983048 | tf_op jit(solution)/shard_map/ppermute | solution.py:35
  29.4 11.2 %collective-permute-start.12 = (bf16[480,256]{1,0:T(8,128)(2,1)S(1)}, bf16[480,256]{1,0:T(8,128)(2,1)S(1)}, u32[]{:S(2)}, u32[]{:S(2)}) collective-permute-start(bf16[480,256]{1,0:T(8,128)(2,1)S(1)} %get-tuple-element.57), channel_id=1, source_target_pairs={{0,4},{4,8},{8,12},{12,16},{16,20},{20,24},{24,28},{28,0},{1,5},{5... | collective-permute-start | bytes 737288 | tf_op jit(solution)/shard_map/ppermute | solution.py:30
  29.4 13.6 %collective-permute-start.13 = (bf16[480,256]{1,0:T(8,128)(2,1)S(1)}, bf16[480,256]{1,0:T(8,128)(2,1)S(1)}, u32[]{:S(2)}, u32[]{:S(2)}) collective-permute-start(bf16[480,256]{1,0:T(8,128)(2,1)S(1)} %get-tuple-element.59), channel_id=1, source_target_pairs={{0,28},{4,0},{8,4},{12,8},{16,12},{20,16},{24,20},{28,24},{1,29},{... | collective-permute-start | bytes 737288 | tf_op jit(solution)/shard_map/ppermute | solution.py:30
  37.0 12.9 %collective-permute-start.17 = (bf16[960,256]{1,0:T(8,128)(2,1)S(1)}, bf16[960,256]{1,0:T(8,128)(2,1)S(1)}, u32[]{:S(2)}, u32[]{:S(2)}) collective-permute-start(bf16[960,256]{1,0:T(8,128)(2,1)S(1)} %get-tuple-element.55.refs_2_.refs_4_), channel_id=1, source_target_pairs={{0,2},{1,3},{2,0},{3,1},{4,6},{5,7},{6,4},{7,5},{8,10},{9,11},{10,... | collective-permute-start | bytes 1474568 | tf_op jit(solution)/shard_map/ppermute | solution.py:35
  38.0 25.0 %copy-start.4 = (bf16[640,256]{1,0:T(8,128)(2,1)}, bf16[640,256]{1,0:T(8,128)(2,1)S(1)}, u32[]{:S(2)}) copy-start(bf16[640,256]{1,0:T(8,128)(2,1)S(1)} %collective-permute-done.14.refs_3_.refs_2_) | copy-start | bytes 983044
  46.8 5.3 %collective-permute-start.15 = (bf16[976,256]{1,0:T(8,128)(2,1)S(1)}, bf16[976,256]{1,0:T(8,128)(2,1)S(1)}, u32[]{:S(2)}, u32[]{:S(2)}) collective-permute-start(bf16[976,256]{1,0:T(8,128)(2,1)S(1)} %get-tuple-element.64.refs_4_.refs_8_), channel_id=1, source_target_pairs={{0,1},{1,0},{2,3},{3,2},{4,5},{5,4},{6,7},{7,6},{8,9},{9,8},{10,11... | collective-permute-start | bytes 1499144 | tf_op jit(solution)/shard_map/ppermute | solution.py:35
  46.8 13.8 %collective-permute-start.19 = (bf16[976,256]{1,0:T(8,128)(2,1)S(1)}, bf16[976,256]{1,0:T(8,128)(2,1)S(1)}, u32[]{:S(2)}, u32[]{:S(2)}) collective-permute-start(bf16[976,256]{1,0:T(8,128)(2,1)S(1)} %get-tuple-element.64.refs_4_.refs_8_), channel_id=1, source_target_pairs={{0,2},{1,3},{2,0},{3,1},{4,6},{5,7},{6,4},{7,5},{8,10},{9,11},{10,... | collective-permute-start | bytes 1499144 | tf_op jit(solution)/shard_map/ppermute | solution.py:35
  47.4 4.8 %collective-permute-start.11 = (bf16[960,256]{1,0:T(8,128)(2,1)S(1)}, bf16[960,256]{1,0:T(8,128)(2,1)S(1)}, u32[]{:S(2)}, u32[]{:S(2)}) collective-permute-start(bf16[960,256]{1,0:T(8,128)(2,1)S(1)} %get-tuple-element.55.refs_2_.refs_4_), channel_id=1, source_target_pairs={{0,1},{1,0},{2,3},{3,2},{4,5},{5,4},{6,7},{7,6},{8,9},{9,8},{10,11... | collective-permute-start | bytes 1474568 | tf_op jit(solution)/shard_map/ppermute | solution.py:35
  49.8 10.8 %collective-permute-start.18 = (bf16[960,256]{1,0:T(8,128)(2,1)S(1)}, bf16[960,256]{1,0:T(8,128)(2,1)S(1)}, u32[]{:S(2)}, u32[]{:S(2)}) collective-permute-start(bf16[960,256]{1,0:T(8,128)(2,1)S(1)} %collective-permute-done.17.refs_5_.refs_6_), channel_id=1, source_target_pairs={{0,1},{1,0},{2,3},{3,2},{4,5},{5,4},{6,7},{7,6},{8,9},{9,8},{10,11... | collective-permute-start | bytes 1474568 | tf_op jit(solution)/shard_map/ppermute | solution.py:35
  49.8 2.3 %collective-permute-start = (bf16[640,256]{1,0:T(8,128)(2,1)S(1)}, bf16[640,256]{1,0:T(8,128)(2,1)S(1)}, u32[]{:S(2)}, u32[]{:S(2)}) collective-permute-start(bf16[640,256]{1,0:T(8,128)(2,1)S(1)} %get-tuple-element.42.refs_0_), channel_id=1, source_target_pairs={{0,1},{1,0},{2,3},{3,2},{4,5},{5,4},{6,7},{7,6},{8,9},{9,8},{10,11... | collective-permute-start | bytes 983048 | tf_op jit(solution)/shard_map/ppermute | solution.py:35
  60.6 2.4 %collective-permute-start.20 = (bf16[976,256]{1,0:T(8,128)(2,1)S(1)}, bf16[976,256]{1,0:T(8,128)(2,1)S(1)}, u32[]{:S(2)}, u32[]{:S(2)}) collective-permute-start(bf16[976,256]{1,0:T(8,128)(2,1)S(1)} %collective-permute-done.19.refs_7_.refs_10_), channel_id=1, source_target_pairs={{0,1},{1,0},{2,3},{3,2},{4,5},{5,4},{6,7},{7,6},{8,9},{9,8},{10,11... | collective-permute-start | bytes 1499144 | tf_op jit(solution)/shard_map/ppermute | solution.py:35
  60.6 2.3 %collective-permute-start.16 = (bf16[640,256]{1,0:T(8,128)(2,1)S(1)}, bf16[640,256]{1,0:T(8,128)(2,1)S(1)}, u32[]{:S(2)}, u32[]{:S(2)}) collective-permute-start(bf16[640,256]{1,0:T(8,128)(2,1)S(1)} %collective-permute-done.14.refs_3_.refs_2_), channel_id=1, source_target_pairs={{0,1},{1,0},{2,3},{3,2},{4,5},{5,4},{6,7},{7,6},{8,9},{9,8},{10,11... | collective-permute-start | bytes 983048 | tf_op jit(solution)/shard_map/ppermute | solution.py:35
  77.0 9.3 %collective-permute-start.21 = (bf16[64,1152]{1,0:T(8,128)(2,1)}, bf16[64,1152]{1,0:T(8,128)(2,1)}, u32[]{:S(2)}, u32[]{:S(2)}) collective-permute-start(bf16[64,1152]{1,0:T(8,128)(2,1)} %sums.1.mine_ref), channel_id=1, source_target_pairs={{0,16},{4,20},{8,24},{12,28},{16,0},{20,4},{24,8},{28,12},{1,17},{... | collective-permute-start | bytes 442376 | tf_op jit(solution)/shard_map/ppermute | solution.py:30
  (13 other events, 160.3 us)

commit v8 on v7

--- a/solution.py
+++ b/solution.py
@@ -362,21 +362,32 @@
 
 
 def rotate_kernel(chunks, blocks, spans, weights_ref, *refs):
-    out_ref = refs[-1]
+    out_ref, made_ref, sems = refs[-3:]
     grid = [refs[c * blocks : (c + 1) * blocks] for c in range(chunks)]
     local = grid[0][0].shape[1]
-    for c in range(chunks):
-        for begin, size, column in spans[c]:
-            total = None
-            for r in range(blocks):
-                term = lax.dot_general(
-                    weights_ref[:, r * local : (r + 1) * local],
-                    grid[c][r][begin : begin + size, :],
-                    (((1,), (1,)), ((), ())),
-                    preferred_element_type=F32,
-                )
-                total = term if total is None else total + term
-            out_ref[:, column : column + size] = total.astype(BF16)
+    order = sorted((column, begin, size, c) for c in range(chunks) for begin, size, column in spans[c])
+    copies = []
+    sent = 0
+    for index, (column, begin, size, c) in enumerate(order):
+        total = None
+        for r in range(blocks):
+            term = lax.dot_general(
+                weights_ref[:, r * local : (r + 1) * local],
+                grid[c][r][begin : begin + size, :],
+                (((1,), (1,)), ((), ())),
+                preferred_element_type=F32,
+            )
+            total = term if total is None else total + term
+        made_ref[:, column : column + size] = total.astype(BF16)
+        done = column + size
+        ready = done if index == len(order) - 1 else done // LANES * LANES
+        if ready > sent:
+            at = pl.ds(sent, ready - sent)
+            copies.append(pltpu.make_async_copy(made_ref.at[:, at], out_ref.at[:, at], sems.at[len(copies)]))
+            copies[-1].start()
+            sent = ready
+    for copy in copies:
+        copy.wait()
 
 
 def lower_blocks(own):
@@ -557,7 +568,11 @@
         functools.partial(rotate_kernel, len(chunks), band_size, spans),
         out_shape=jax.ShapeDtypeStruct((local, count * n), BF16),
         in_specs=[VMEM] * (1 + len(flat)),
-        out_specs=VMEM,
+        out_specs=HBM,
+        scratch_shapes=[
+            pltpu.VMEM((local, count * n), BF16),
+            pltpu.SemaphoreType.DMA((1 + 2 * len(STRIPS),)),
+        ],
         compiler_params=params(24),
         cost_estimate=about(0.01),
         name="rotate",

time: 101 us -> 101 us (level)
  no operation moved by 1% of the time
where the time goes in v8:
time: 101 us
  waiting for transfers between devices  26.9 us (27%)
  Pallas kernels  26.6 us (26%)
  starting transfers between devices  23.8 us (24%)
  blocking collectives  23 us (23%)
    ppermute x7, starting transfers between devices, from_behind(): return lax.ppermute(value, axis, pairs)  17 us
    ppermute x15, waiting for transfers between devices, swap(): lax.ppermute(value, axis, [(source, source ^ bit) for source in range(cou...  14.1 us
    ppermute x7, waiting for transfers between devices, from_behind(): return lax.ppermute(value, axis, pairs)  12.8 us
    all_to_all x1, blocking collectives, fast_shards(): lax.all_to_all(late, 'elem', 0, 0, tiled=True, axis_index_groups=groups)  12.4 us
    all_to_all x1, blocking collectives, fast_shards(): lax.all_to_all(weights, 'elem', 0, 0, tiled=True, axis_index_groups=groups)  10.7 us
    ppermute x15, starting transfers between devices, swap(): lax.ppermute(value, axis, [(source, source ^ bit) for source in range(cou...  6.81 us
    pallas_call x2, Pallas kernels, fast_shards(): pl.pallas_call(functools.partial(strip_kernel, n, count, strip, offset, l...  6.7 us
    pallas_call x1, Pallas kernels, fast_shards(): pl.pallas_call(functools.partial(interior_kernel, n, count, SPLIT, DEGREE...  3.97 us
  transfers between devices with their start and end apart: 22, of which 9 were waited for; matrix products, arithmetic and copies ran while one was open for 0% of the time, Pallas kernels for 18%

profile of v8, /device:TPU:0, one launch (start us, length us, event | category | flops | bytes accessed | tf_op | source)
XLA Modules:
  0.0 100.8 jit_solution(14233971962644096489)
XLA Ops:
  0.0 2.8 %ends.1 = (bf16[40,1664]{1,0:T(8,128)(2,1)}, bf16[40,1792]{1,0:T(8,128)(2,1)}) custom-call(s32[1]{0:T(128)} %bitcast.1.me_ref, s32[16]{0:T(128)} %sizes_ref.3, s32[16]{0:T(128)} %pattern_ref, bf16[16,160,160]{2,1,0:T(8,128)(2,1)} %diag_ref.1, bf16[16,160,160]{2,1,0:T(8,128)(2,1)} %couple_ref.1), custom_call_target="tpu_custom_call" | custom-call | flops 11500000 | bytes 1 | tf_op jit(solution)/shard_map/ends/pallas_call | solution.py:415
  2.8 3.0 %collective-permute-start.3 = (bf16[40,1792]{1,0:T(8,128)(2,1)}, bf16[40,1792]{1,0:T(8,128)(2,1)S(1)}, u32[]{:S(2)}, u32[]{:S(2)}) collective-permute-start(bf16[40,1792]{1,0:T(8,128)(2,1)} %get-tuple-element.50), channel_id=1, source_target_pairs={{0,4},{4,8},{8,12},{12,16},{16,20},{20,24},{24,28},{28,0},{1,5},{5... | collective-permute-start | bytes 430088 | tf_op jit(solution)/shard_map/ppermute | solution.py:30
  5.8 3.1 %collective-permute-start.5 = (bf16[40,1664]{1,0:T(8,128)(2,1)}, bf16[40,1664]{1,0:T(8,128)(2,1)S(1)}, u32[]{:S(2)}, u32[]{:S(2)}) collective-permute-start(bf16[40,1664]{1,0:T(8,128)(2,1)} %get-tuple-element.37), channel_id=1, source_target_pairs={{0,28},{4,0},{8,4},{12,8},{16,12},{20,16},{24,20},{28,24},{1,29},{... | collective-permute-start | bytes 399368 | tf_op jit(solution)/shard_map/ppermute | solution.py:30
  10.0 4.7 %collective-permute-start.2 = (bf16[480,256]{1,0:T(8,128)(2,1)S(1)}, bf16[480,256]{1,0:T(8,128)(2,1)S(1)}, u32[]{:S(2)}, u32[]{:S(2)}) collective-permute-start(bf16[480,256]{1,0:T(8,128)(2,1)S(1)} %get-tuple-element.44), channel_id=1, source_target_pairs={{0,28},{4,0},{8,4},{12,8},{16,12},{20,16},{24,20},{28,24},{1,29},{... | collective-permute-start | bytes 737288 | tf_op jit(solution)/shard_map/ppermute | solution.py:30
  14.7 2.1 %rows.1.rows_ref = bf16[16,160,512]{2,1,0:T(8,128)(2,1)S(1)} custom-call(s32[16]{0:T(128)S(1)} %copy-done.13, s32[16]{0:T(128)S(1)} %copy-done.14, bf16[16,160,160]{2,1,0:T(8,128)(2,1)S(1)} %copy-done, bf16[16,160,160]{2,1,0:T(8,128)(2,1)S(1)} %copy-done.1), custom_call_target="tpu_custom_call" | custom-call | flops 11500000 | bytes 1 | tf_op jit(solution)/shard_map/rows/pallas_call | solution.py:428
  16.8 3.4 %interior_first.1 = (bf16[2,320,256]{2,1,0:T(8,128)(2,1)S(1)}, bf16[2,320,256]{2,1,0:T(8,128)(2,1)S(1)}, bf16[2560,256]{1,0:T(8,128)(2,1)S(1)}, bf16[2560,256]{1,0:T(8,128)(2,1)S(1)}) custom-call(bf16[16,160,512]{2,1,0:T(8,128)(2,1)S(1)} %rows.1.rows_ref, bf16[2560,256]{1,0:T(8,128)(2,1)S(1)} %get-tuple-element.39.refs_0_), custom_call_target="tpu_custom_call" | custom-call | flops 11500000 | bytes 1 | tf_op jit(solution)/shard_map/interior_first/pallas_call | solution.py:458
  20.3 1.7 %collective-permute-start.7 = (bf16[40,1792]{1,0:T(8,128)(2,1)S(1)}, bf16[40,1792]{1,0:T(8,128)(2,1)S(1)}, u32[]{:S(2)}, u32[]{:S(2)}) collective-permute-start(bf16[40,1792]{1,0:T(8,128)(2,1)S(1)} %collective-permute-done.3.refs_4_.refs_2_), channel_id=1, source_target_pairs={{0,2},{1,3},{2,0},{3,1},{4,6},{5,7},{6,4},{7,5},{8,10},{9,11},{10,... | collective-permute-start | bytes 430088 | tf_op jit(solution)/shard_map/ppermute | solution.py:35
  22.4 4.0 %interior_rest.1 = (bf16[4,320,256]{2,1,0:T(8,128)(2,1)S(1)}, bf16[4,320,256]{2,1,0:T(8,128)(2,1)S(1)}, bf16[640,256]{1,0:T(8,128)(2,1)S(1)}, f32[1,256]{1,0:T(1,128)S(1)}) custom-call(bf16[16,160,512]{2,1,0:T(8,128)(2,1)S(1)} %rows.1.rows_ref, bf16[2560,256]{1,0:T(8,128)(2,1)S(1)} %get-tuple-element.40.refs_0_, bf16[2560,256]{1,0:T(8,128)(2,1)S(1)} %get-tuple-element.41.refs_1_), custom_call_target="tpu_custom_call" | custom-call | flops 11500000 | bytes 1 | tf_op jit(solution)/shard_map/interior_rest/pallas_call | solution.py:472
  27.8 1.5 %collective-permute-start.14 = (bf16[640,256]{1,0:T(8,128)(2,1)S(1)}, bf16[640,256]{1,0:T(8,128)(2,1)S(1)}, u32[]{:S(2)}, u32[]{:S(2)}) collective-permute-start(bf16[640,256]{1,0:T(8,128)(2,1)S(1)} %get-tuple-element.42.refs_0_), channel_id=1, source_target_pairs={{0,2},{1,3},{2,0},{3,1},{4,6},{5,7},{6,4},{7,5},{8,10},{9,11},{10,... | collective-permute-start | bytes 983048 | tf_op jit(solution)/shard_map/ppermute | solution.py:35
  29.4 4.7 %collective-permute-start.13 = (bf16[480,256]{1,0:T(8,128)(2,1)S(1)}, bf16[480,256]{1,0:T(8,128)(2,1)S(1)}, u32[]{:S(2)}, u32[]{:S(2)}) collective-permute-start(bf16[480,256]{1,0:T(8,128)(2,1)S(1)} %get-tuple-element.59), channel_id=1, source_target_pairs={{0,28},{4,0},{8,4},{12,8},{16,12},{20,16},{24,20},{28,24},{1,29},{... | collective-permute-start | bytes 737288 | tf_op jit(solution)/shard_map/ppermute | solution.py:30
  34.1 2.9 %strip.2 = (bf16[960,256]{1,0:T(8,128)(2,1)S(1)}, bf16[6,320,256]{2,1,0:T(8,128)(2,1)S(1)}, bf16[6,320,256]{2,1,0:T(8,128)(2,1)S(1)}, f32[1,256]{1,0:T(1,128)S(1)}) custom-call(s32[1]{0:T(128)} %bitcast.1.me_ref, bf16[480,256]{1,0:T(8,128)(2,1)S(1)} %collective-permute-done.1.left_y_ref, bf16[480,256]{1,0:T(8,128)(2,1)S(1)} %collective-permute-done.2.right_y_ref, ...), custom_call_target="tpu_custom_call" | custom-call | flops 3449999872 | bytes 1 | tf_op jit(solution)/shard_map/strip/pallas_call | solution.py:501
  38.0 2.6 %collective-permute-done.12.left_y_ref = bf16[480,256]{1,0:T(8,128)(2,1)S(1)} collective-permute-done((bf16[480,256]{1,0:T(8,128)(2,1)S(1)}, bf16[480,256]{1,0:T(8,128)(2,1)S(1)}, u32[]{:S(2)}, u32[]{:S(2)}) %collective-permute-start.12) | collective-permute-done | bytes 245792 | tf_op jit(solution)/shard_map/ppermute | solution.py:30
  40.5 2.4 %collective-permute-done.13.right_y_ref = bf16[480,256]{1,0:T(8,128)(2,1)S(1)} collective-permute-done((bf16[480,256]{1,0:T(8,128)(2,1)S(1)}, bf16[480,256]{1,0:T(8,128)(2,1)S(1)}, u32[]{:S(2)}, u32[]{:S(2)}) %collective-permute-start.13) | collective-permute-done | bytes 245792 | tf_op jit(solution)/shard_map/ppermute | solution.py:30
  43.0 3.9 %strip.3 = (bf16[976,256]{1,0:T(8,128)(2,1)S(1)}, f32[8,128]{1,0:T(8,128)}, f32[8,128]{1,0:T(8,128)}, f32[1,256]{1,0:T(1,128)}) custom-call(s32[1]{0:T(128)} %bitcast.1.me_ref, bf16[480,256]{1,0:T(8,128)(2,1)S(1)} %collective-permute-done.12.left_y_ref, bf16[480,256]{1,0:T(8,128)(2,1)S(1)} %collective-permute-done.13.right_y_ref, ...), custom_call_target="tpu_custom_call" | custom-call | flops 3449999872 | bytes 1 | tf_op jit(solution)/shard_map/strip/pallas_call | solution.py:501
  47.6 2.2 %collective-permute-done.17.refs_5_.refs_6_ = bf16[960,256]{1,0:T(8,128)(2,1)S(1)} collective-permute-done((bf16[960,256]{1,0:T(8,128)(2,1)S(1)}, bf16[960,256]{1,0:T(8,128)(2,1)S(1)}, u32[]{:S(2)}, u32[]{:S(2)}) %collective-permute-start.17) | collective-permute-done | bytes 491552 | tf_op jit(solution)/shard_map/ppermute | solution.py:35
  50.3 1.8 %collective-permute-done.refs_1_ = bf16[640,256]{1,0:T(8,128)(2,1)S(1)} collective-permute-done((bf16[640,256]{1,0:T(8,128)(2,1)S(1)}, bf16[640,256]{1,0:T(8,128)(2,1)S(1)}, u32[]{:S(2)}, u32[]{:S(2)}) %collective-permute-start) | collective-permute-done | bytes 327712 | tf_op jit(solution)/shard_map/ppermute | solution.py:35
  52.2 1.3 %gram_early.1 = (bf16[4,64,512]{2,1,0:T(8,128)(2,1)S(1)}, bf16[2,16,256]{2,1,0:T(8,128)(2,1)S(1)}, bf16[256,2560]{1,0:T(8,128)(2,1)S(1)}) custom-call(bf16[640,256]{1,0:T(8,128)(2,1)S(1)} %get-tuple-element.42.refs_0_, bf16[640,256]{1,0:T(8,128)(2,1)S(1)} %collective-permute-done.refs_1_, bf16[960,256]{1,0:T(8,128)(2,1)S(1)} %get-tuple-element.55.refs_2_.refs_4_, ...), custom_call_target="tpu_custom_call" | custom-call | flops 11500000 | bytes 1 | tf_op jit(solution)/shard_map/gram_early/pallas_call | solution.py:530
  53.4 7.2 %collective-permute-done.19.refs_7_.refs_10_ = bf16[976,256]{1,0:T(8,128)(2,1)S(1)} collective-permute-done((bf16[976,256]{1,0:T(8,128)(2,1)S(1)}, bf16[976,256]{1,0:T(8,128)(2,1)S(1)}, u32[]{:S(2)}, u32[]{:S(2)}) %collective-permute-start.19) | collective-permute-done | bytes 499744 | tf_op jit(solution)/shard_map/ppermute | solution.py:35
  61.1 1.8 %collective-permute-done.16.refs_4_.refs_3_ = bf16[640,256]{1,0:T(8,128)(2,1)S(1)} collective-permute-done((bf16[640,256]{1,0:T(8,128)(2,1)S(1)}, bf16[640,256]{1,0:T(8,128)(2,1)S(1)}, u32[]{:S(2)}, u32[]{:S(2)}) %collective-permute-start.16) | collective-permute-done | bytes 327712 | tf_op jit(solution)/shard_map/ppermute | solution.py:35
  63.9 12.4 %all_to_all.10.got_ref = bf16[4,64,1152]{2,1,0:T(8,128)(2,1)S(1)} all-to-all(bf16[4,64,1152]{2,1,0:T(8,128)(2,1)S(1)} %gram_late.1), channel_id=1, replica_groups={{0,4,8,12},{16,20,24,28},{1,5,9,13},{17,21,25,29},{2,6,10,14},{18,22,26..., dimensions={0} | all-to-all | bytes 1179648 | tf_op jit(solution)/shard_map/all_to_all | solution.py:545
  77.0 1.4 %collective-permute-start.21 = (bf16[64,1152]{1,0:T(8,128)(2,1)}, bf16[64,1152]{1,0:T(8,128)(2,1)}, u32[]{:S(2)}, u32[]{:S(2)}) collective-permute-start(bf16[64,1152]{1,0:T(8,128)(2,1)} %sums.1.mine_ref), channel_id=1, source_target_pairs={{0,16},{4,20},{8,24},{12,28},{16,0},{20,4},{24,8},{28,12},{1,17},{... | collective-permute-start | bytes 442376 | tf_op jit(solution)/shard_map/ppermute | solution.py:30
  78.5 7.8 %collective-permute-done.21.other_ref = bf16[64,1152]{1,0:T(8,128)(2,1)} collective-permute-done((bf16[64,1152]{1,0:T(8,128)(2,1)}, bf16[64,1152]{1,0:T(8,128)(2,1)}, u32[]{:S(2)}, u32[]{:S(2)}) %collective-permute-start.21) | collective-permute-done | bytes 147488 | tf_op jit(solution)/shard_map/ppermute | solution.py:30
  87.4 10.7 %all_to_all.11 = bf16[4,64,1024]{2,1,0:T(8,128)(2,1)S(1)} all-to-all(bf16[4,64,1024]{2,1,0:T(8,128)(2,1)S(1)} %weights.1), channel_id=1, replica_groups={{0,4,8,12},{16,20,24,28},{1,5,9,13},{17,21,25,29},{2,6,10,14},{18,22,26..., dimensions={0} | all-to-all | bytes 1048576 | tf_op jit(solution)/shard_map/all_to_all | solution.py:566
  98.1 2.5 %rotate.1 = bf16[256,2560]{1,0:T(8,128)(2,1)} custom-call(bf16[256,1024]{1,0:T(8,128)(2,1)S(1)} %bitcast.3, bf16[640,256]{1,0:T(8,128)(2,1)S(1)} %copy-done.9, bf16[640,256]{1,0:T(8,128)(2,1)S(1)} %copy-done.11, bf16[640,256]{1,0:T(8,128)(2,1)S(1)} %copy-done.5, bf16[640,256]{1,0:T(8,128)(2,1)S(1)} %copy-done.7, ...), custom_call_target="tpu_custom_call" | custom-call | flops 11500000 | bytes 1 | tf_op jit(solution)/shard_map/rotate/pallas_call | solution.py:567
  (64 shorter events, 8.6 us)
Async XLA Ops:
  2.8 17.4 %collective-permute-start.3 = (bf16[40,1792]{1,0:T(8,128)(2,1)}, bf16[40,1792]{1,0:T(8,128)(2,1)S(1)}, u32[]{:S(2)}, u32[]{:S(2)}) collective-permute-start(bf16[40,1792]{1,0:T(8,128)(2,1)} %get-tuple-element.50), channel_id=1, source_target_pairs={{0,4},{4,8},{8,12},{12,16},{16,20},{20,24},{24,28},{28,0},{1,5},{5... | collective-permute-start | bytes 430088 | tf_op jit(solution)/shard_map/ppermute | solution.py:30
  5.8 16.1 %collective-permute-start.5 = (bf16[40,1664]{1,0:T(8,128)(2,1)}, bf16[40,1664]{1,0:T(8,128)(2,1)S(1)}, u32[]{:S(2)}, u32[]{:S(2)}) collective-permute-start(bf16[40,1664]{1,0:T(8,128)(2,1)} %get-tuple-element.37), channel_id=1, source_target_pairs={{0,28},{4,0},{8,4},{12,8},{16,12},{20,16},{24,20},{28,24},{1,29},{... | collective-permute-start | bytes 399368 | tf_op jit(solution)/shard_map/ppermute | solution.py:30
  10.0 16.5 %collective-permute-start.1 = (bf16[480,256]{1,0:T(8,128)(2,1)S(1)}, bf16[480,256]{1,0:T(8,128)(2,1)S(1)}, u32[]{:S(2)}, u32[]{:S(2)}) collective-permute-start(bf16[480,256]{1,0:T(8,128)(2,1)S(1)} %get-tuple-element.43), channel_id=1, source_target_pairs={{0,4},{4,8},{8,12},{12,16},{16,20},{20,24},{24,28},{28,0},{1,5},{5... | collective-permute-start | bytes 737288 | tf_op jit(solution)/shard_map/ppermute | solution.py:30
  10.0 16.4 %collective-permute-start.2 = (bf16[480,256]{1,0:T(8,128)(2,1)S(1)}, bf16[480,256]{1,0:T(8,128)(2,1)S(1)}, u32[]{:S(2)}, u32[]{:S(2)}) collective-permute-start(bf16[480,256]{1,0:T(8,128)(2,1)S(1)} %get-tuple-element.44), channel_id=1, source_target_pairs={{0,28},{4,0},{8,4},{12,8},{16,12},{20,16},{24,20},{28,24},{1,29},{... | collective-permute-start | bytes 737288 | tf_op jit(solution)/shard_map/ppermute | solution.py:30
  20.3 6.2 %collective-permute-start.7 = (bf16[40,1792]{1,0:T(8,128)(2,1)S(1)}, bf16[40,1792]{1,0:T(8,128)(2,1)S(1)}, u32[]{:S(2)}, u32[]{:S(2)}) collective-permute-start(bf16[40,1792]{1,0:T(8,128)(2,1)S(1)} %collective-permute-done.3.refs_4_.refs_2_), channel_id=1, source_target_pairs={{0,2},{1,3},{2,0},{3,1},{4,6},{5,7},{6,4},{7,5},{8,10},{9,11},{10,... | collective-permute-start | bytes 430088 | tf_op jit(solution)/shard_map/ppermute | solution.py:35
  22.0 5.9 %collective-permute-start.9 = (bf16[40,1664]{1,0:T(8,128)(2,1)S(1)}, bf16[40,1664]{1,0:T(8,128)(2,1)S(1)}, u32[]{:S(2)}, u32[]{:S(2)}) collective-permute-start(bf16[40,1664]{1,0:T(8,128)(2,1)S(1)} %collective-permute-done.5.refs_6_.refs_4_), channel_id=1, source_target_pairs={{0,2},{1,3},{2,0},{3,1},{4,6},{5,7},{6,4},{7,5},{8,10},{9,11},{10,... | collective-permute-start | bytes 399368 | tf_op jit(solution)/shard_map/ppermute | solution.py:35
  26.3 25.8 %copy-start.8 = (bf16[640,256]{1,0:T(8,128)(2,1)}, bf16[640,256]{1,0:T(8,128)(2,1)S(1)}, u32[]{:S(2)}) copy-start(bf16[640,256]{1,0:T(8,128)(2,1)S(1)} %get-tuple-element.42.refs_0_) | copy-start | bytes 983044
  26.3 3.0 %collective-permute-start.4 = (bf16[40,1792]{1,0:T(8,128)(2,1)S(1)}, bf16[40,1792]{1,0:T(8,128)(2,1)S(1)}, u32[]{:S(2)}, u32[]{:S(2)}) collective-permute-start(bf16[40,1792]{1,0:T(8,128)(2,1)S(1)} %collective-permute-done.3.refs_4_.refs_2_), channel_id=1, source_target_pairs={{0,1},{1,0},{2,3},{3,2},{4,5},{5,4},{6,7},{7,6},{8,9},{9,8},{10,11... | collective-permute-start | bytes 430088 | tf_op jit(solution)/shard_map/ppermute | solution.py:35
  26.5 7.6 %collective-permute-start.8 = (bf16[40,1792]{1,0:T(8,128)(2,1)S(1)}, bf16[40,1792]{1,0:T(8,128)(2,1)S(1)}, u32[]{:S(2)}, u32[]{:S(2)}) collective-permute-start(bf16[40,1792]{1,0:T(8,128)(2,1)S(1)} %collective-permute-done.7.refs_8_.refs_6_), channel_id=1, source_target_pairs={{0,1},{1,0},{2,3},{3,2},{4,5},{5,4},{6,7},{7,6},{8,9},{9,8},{10,11... | collective-permute-start | bytes 430088 | tf_op jit(solution)/shard_map/ppermute | solution.py:35
  27.0 2.4 %collective-permute-start.6 = (bf16[40,1664]{1,0:T(8,128)(2,1)S(1)}, bf16[40,1664]{1,0:T(8,128)(2,1)S(1)}, u32[]{:S(2)}, u32[]{:S(2)}) collective-permute-start(bf16[40,1664]{1,0:T(8,128)(2,1)S(1)} %collective-permute-done.5.refs_6_.refs_4_), channel_id=1, source_target_pairs={{0,1},{1,0},{2,3},{3,2},{4,5},{5,4},{6,7},{7,6},{8,9},{9,8},{10,11... | collective-permute-start | bytes 399368 | tf_op jit(solution)/shard_map/ppermute | solution.py:35
  27.8 6.3 %collective-permute-start.10 = (bf16[40,1664]{1,0:T(8,128)(2,1)S(1)}, bf16[40,1664]{1,0:T(8,128)(2,1)S(1)}, u32[]{:S(2)}, u32[]{:S(2)}) collective-permute-start(bf16[40,1664]{1,0:T(8,128)(2,1)S(1)} %collective-permute-done.9.refs_10_.refs_8_), channel_id=1, source_target_pairs={{0,1},{1,0},{2,3},{3,2},{4,5},{5,4},{6,7},{7,6},{8,9},{9,8},{10,11... | collective-permute-start | bytes 399368 | tf_op jit(solution)/shard_map/ppermute | solution.py:35
  27.8 10.1 %collective-permute-start.14 = (bf16[640,256]{1,0:T(8,128)(2,1)S(1)}, bf16[640,256]{1,0:T(8,128)(2,1)S(1)}, u32[]{:S(2)}, u32[]{:S(2)}) collective-permute-start(bf16[640,256]{1,0:T(8,128)(2,1)S(1)} %get-tuple-element.42.refs_0_), channel_id=1, source_target_pairs={{0,2},{1,3},{2,0},{3,1},{4,6},{5,7},{6,4},{7,5},{8,10},{9,11},{10,... | collective-permute-start | bytes 983048 | tf_op jit(solution)/shard_map/ppermute | solution.py:35
  29.4 11.2 %collective-permute-start.12 = (bf16[480,256]{1,0:T(8,128)(2,1)S(1)}, bf16[480,256]{1,0:T(8,128)(2,1)S(1)}, u32[]{:S(2)}, u32[]{:S(2)}) collective-permute-start(bf16[480,256]{1,0:T(8,128)(2,1)S(1)} %get-tuple-element.57), channel_id=1, source_target_pairs={{0,4},{4,8},{8,12},{12,16},{16,20},{20,24},{24,28},{28,0},{1,5},{5... | collective-permute-start | bytes 737288 | tf_op jit(solution)/shard_map/ppermute | solution.py:30
  29.4 13.6 %collective-permute-start.13 = (bf16[480,256]{1,0:T(8,128)(2,1)S(1)}, bf16[480,256]{1,0:T(8,128)(2,1)S(1)}, u32[]{:S(2)}, u32[]{:S(2)}) collective-permute-start(bf16[480,256]{1,0:T(8,128)(2,1)S(1)} %get-tuple-element.59), channel_id=1, source_target_pairs={{0,28},{4,0},{8,4},{12,8},{16,12},{20,16},{24,20},{28,24},{1,29},{... | collective-permute-start | bytes 737288 | tf_op jit(solution)/shard_map/ppermute | solution.py:30
  37.0 12.9 %collective-permute-start.17 = (bf16[960,256]{1,0:T(8,128)(2,1)S(1)}, bf16[960,256]{1,0:T(8,128)(2,1)S(1)}, u32[]{:S(2)}, u32[]{:S(2)}) collective-permute-start(bf16[960,256]{1,0:T(8,128)(2,1)S(1)} %get-tuple-element.55.refs_2_.refs_4_), channel_id=1, source_target_pairs={{0,2},{1,3},{2,0},{3,1},{4,6},{5,7},{6,4},{7,5},{8,10},{9,11},{10,... | collective-permute-start | bytes 1474568 | tf_op jit(solution)/shard_map/ppermute | solution.py:35
  38.0 25.0 %copy-start.4 = (bf16[640,256]{1,0:T(8,128)(2,1)}, bf16[640,256]{1,0:T(8,128)(2,1)S(1)}, u32[]{:S(2)}) copy-start(bf16[640,256]{1,0:T(8,128)(2,1)S(1)} %collective-permute-done.14.refs_3_.refs_2_) | copy-start | bytes 983044
  46.8 5.3 %collective-permute-start.15 = (bf16[976,256]{1,0:T(8,128)(2,1)S(1)}, bf16[976,256]{1,0:T(8,128)(2,1)S(1)}, u32[]{:S(2)}, u32[]{:S(2)}) collective-permute-start(bf16[976,256]{1,0:T(8,128)(2,1)S(1)} %get-tuple-element.64.refs_4_.refs_8_), channel_id=1, source_target_pairs={{0,1},{1,0},{2,3},{3,2},{4,5},{5,4},{6,7},{7,6},{8,9},{9,8},{10,11... | collective-permute-start | bytes 1499144 | tf_op jit(solution)/shard_map/ppermute | solution.py:35
  46.8 13.8 %collective-permute-start.19 = (bf16[976,256]{1,0:T(8,128)(2,1)S(1)}, bf16[976,256]{1,0:T(8,128)(2,1)S(1)}, u32[]{:S(2)}, u32[]{:S(2)}) collective-permute-start(bf16[976,256]{1,0:T(8,128)(2,1)S(1)} %get-tuple-element.64.refs_4_.refs_8_), channel_id=1, source_target_pairs={{0,2},{1,3},{2,0},{3,1},{4,6},{5,7},{6,4},{7,5},{8,10},{9,11},{10,... | collective-permute-start | bytes 1499144 | tf_op jit(solution)/shard_map/ppermute | solution.py:35
  47.4 4.8 %collective-permute-start.11 = (bf16[960,256]{1,0:T(8,128)(2,1)S(1)}, bf16[960,256]{1,0:T(8,128)(2,1)S(1)}, u32[]{:S(2)}, u32[]{:S(2)}) collective-permute-start(bf16[960,256]{1,0:T(8,128)(2,1)S(1)} %get-tuple-element.55.refs_2_.refs_4_), channel_id=1, source_target_pairs={{0,1},{1,0},{2,3},{3,2},{4,5},{5,4},{6,7},{7,6},{8,9},{9,8},{10,11... | collective-permute-start | bytes 1474568 | tf_op jit(solution)/shard_map/ppermute | solution.py:35
  49.8 10.8 %collective-permute-start.18 = (bf16[960,256]{1,0:T(8,128)(2,1)S(1)}, bf16[960,256]{1,0:T(8,128)(2,1)S(1)}, u32[]{:S(2)}, u32[]{:S(2)}) collective-permute-start(bf16[960,256]{1,0:T(8,128)(2,1)S(1)} %collective-permute-done.17.refs_5_.refs_6_), channel_id=1, source_target_pairs={{0,1},{1,0},{2,3},{3,2},{4,5},{5,4},{6,7},{7,6},{8,9},{9,8},{10,11... | collective-permute-start | bytes 1474568 | tf_op jit(solution)/shard_map/ppermute | solution.py:35
  49.8 2.3 %collective-permute-start = (bf16[640,256]{1,0:T(8,128)(2,1)S(1)}, bf16[640,256]{1,0:T(8,128)(2,1)S(1)}, u32[]{:S(2)}, u32[]{:S(2)}) collective-permute-start(bf16[640,256]{1,0:T(8,128)(2,1)S(1)} %get-tuple-element.42.refs_0_), channel_id=1, source_target_pairs={{0,1},{1,0},{2,3},{3,2},{4,5},{5,4},{6,7},{7,6},{8,9},{9,8},{10,11... | collective-permute-start | bytes 983048 | tf_op jit(solution)/shard_map/ppermute | solution.py:35
  60.6 2.4 %collective-permute-start.20 = (bf16[976,256]{1,0:T(8,128)(2,1)S(1)}, bf16[976,256]{1,0:T(8,128)(2,1)S(1)}, u32[]{:S(2)}, u32[]{:S(2)}) collective-permute-start(bf16[976,256]{1,0:T(8,128)(2,1)S(1)} %collective-permute-done.19.refs_7_.refs_10_), channel_id=1, source_target_pairs={{0,1},{1,0},{2,3},{3,2},{4,5},{5,4},{6,7},{7,6},{8,9},{9,8},{10,11... | collective-permute-start | bytes 1499144 | tf_op jit(solution)/shard_map/ppermute | solution.py:35
  60.6 2.3 %collective-permute-start.16 = (bf16[640,256]{1,0:T(8,128)(2,1)S(1)}, bf16[640,256]{1,0:T(8,128)(2,1)S(1)}, u32[]{:S(2)}, u32[]{:S(2)}) collective-permute-start(bf16[640,256]{1,0:T(8,128)(2,1)S(1)} %collective-permute-done.14.refs_3_.refs_2_), channel_id=1, source_target_pairs={{0,1},{1,0},{2,3},{3,2},{4,5},{5,4},{6,7},{7,6},{8,9},{9,8},{10,11... | collective-permute-start | bytes 983048 | tf_op jit(solution)/shard_map/ppermute | solution.py:35
  77.0 9.3 %collective-permute-start.21 = (bf16[64,1152]{1,0:T(8,128)(2,1)}, bf16[64,1152]{1,0:T(8,128)(2,1)}, u32[]{:S(2)}, u32[]{:S(2)}) collective-permute-start(bf16[64,1152]{1,0:T(8,128)(2,1)} %sums.1.mine_ref), channel_id=1, source_target_pairs={{0,16},{4,20},{8,24},{12,28},{16,0},{20,4},{24,8},{28,12},{1,17},{... | collective-permute-start | bytes 442376 | tf_op jit(solution)/shard_map/ppermute | solution.py:30
  (13 other events, 160.3 us)
